TPU v7x, 256 devices: a whole 4x4x8 slice. The times are simulated.
256 devices in a mesh: row: 8 (over z), col: 32 (over x, y, core).
Axes of the slice: x: 4, y: 4, z: 8, core: 2. Of those that a mesh axis runs over, the one named last changes fastest.
Arguments:
- hamiltonian: bfloat16 [32768, 32768], P('row', 'col'), may hold values from -0.5 to 0.5, as said below
- start_block: float32 [32768, 128], P('row'), may hold values from -120 to 120
- spectral_bound: float32 [1], replicated, may hold values from 1.25 to 1.45
Outputs:
- basis: float32 [32768, 128], P(('row', 'col'))
- r_factor: float32 [128, 128], replicated
Inputs may be any that keep to these rules, and one draw needn't show every extreme that they name: hamiltonian is exactly symmetric.
All inputs are finite; a program needn't handle non-finite values.
Results may differ from a plain program's by a relative error of at most 0.005.
Values may be sent and summed in bfloat16 or wider, within the bound.
No kernel may reach another device: no remote copies, remote signals or barrier semaphores. Data moves between devices by JAX's collectives and lax.ppermute only.
A program may use at most 64 MiB of HBM per device.

v0:
```python
import math

import jax
import jax.numpy as jnp
from jax import lax
from jax.sharding import PartitionSpec as P

N = 32768
DEG = 4


def gram_matrix(vectors):
    return lax.dot_general(
        vectors,
        vectors,
        (((0,), (0,)), ((), ())),
        precision=lax.Precision.HIGHEST,
        preferred_element_type=jnp.float32,
    )


def right_solve(lower, vectors):
    return lax.linalg.triangular_solve(
        lower, vectors, left_side=False, lower=True, transpose_a=True
    )


def orthonormalize(vectors, combine):
    lower_one = jnp.linalg.cholesky(combine(gram_matrix(vectors)))
    first_basis = right_solve(lower_one, vectors)
    lower_two = jnp.linalg.cholesky(combine(gram_matrix(first_basis)))
    second_basis = right_solve(lower_two, first_basis)
    triangle = jnp.dot(lower_two.T, lower_one.T, precision=lax.Precision.HIGHEST)
    return (second_basis, triangle)


def run_filter(first, step_even, step_odd, inverse_bound):
    odd_block = inverse_bound * step_even(first)

    def two_steps(counter, state):
        even_block, odd_block = state
        even_block = 2.0 * inverse_bound * step_odd(odd_block) - even_block
        odd_block = 2.0 * inverse_bound * step_even(even_block) - odd_block
        return (even_block, odd_block)

    even_block, odd_block = lax.fori_loop(0, DEG // 2 - 1, two_steps, (first, odd_block))
    return 2.0 * inverse_bound * step_odd(odd_block) - even_block


def body(hamiltonian, start_block, spectral_bound):
    inverse_bound = 1.0 / spectral_bound[0]
    block_rows, block_cols = hamiltonian.shape
    share_rows = block_rows // lax.axis_size("col")
    col_place = lax.axis_index("col")

    def step_even(vectors):
        operand = vectors.astype(jnp.bfloat16)
        partial_sum = lax.dot_general(
            hamiltonian, operand, (((0,), (0,)), ((), ())), preferred_element_type=jnp.float32
        )
        return lax.psum(partial_sum, "row")

    def step_odd(vectors):
        operand = vectors.astype(jnp.bfloat16)
        partial_sum = jnp.dot(hamiltonian, operand, preferred_element_type=jnp.float32)
        return lax.psum(partial_sum, "col")

    filtered = run_filter(start_block, step_even, step_odd, inverse_bound)
    root = math.sqrt(N)

    def combine_rows(matrix):
        return lax.psum(matrix, "row")

    second_basis, triangle = orthonormalize(filtered, combine_rows)
    basis = lax.dynamic_slice_in_dim(second_basis, col_place * share_rows, share_rows, 0) * root
    return (basis, triangle / root)


def solution(mesh):
    in_specs = (P("row", "col"), P("row", None), P())
    out_specs = (P(("row", "col"), None), P())
    return jax.shard_map(body, mesh=mesh, in_specs=in_specs, out_specs=out_specs, check_vma=False)
```

profile of v0, /device:TPU:1, one launch (start us, length us, event | category | flops | bytes accessed | tf_op | source)
XLA Modules:
  0.0 631.2 jit_solution(15324289683120576881)
XLA Ops:
  7.2 0.0 all-reduce.7.cloned.1.call-start
  7.2 7.1 %fusion.1 = f32[1024,128]{1,0:T(8,128)} fusion(bf16[4096,1024]{1,0:T(8,128)(2,1)} %param.6, f32[4096,128]{1,0:T(8,128)} %param.7), kind=kOutput, calls=%fused_computation.9 | convolution fusion | flops 1074266112 | bytes 11010048 | tf_op jit(solution)/shard_map/dot_general | solution.py:58
  14.3 0.0 all-reduce.7.cloned.1.call-update
  14.4 0.0 all-reduce.9.cloned.1.call-start
  15.1 72.0 %all-reduce.7.cloned.1.call-done = f32[1024,128]{1,0:T(8,128)} async-done(((f32[1024,128]{1,0:T(8,128)}), f32[1024,128]{1,0:T(8,128)}) %all-reduce.7.cloned.1.call-update) | async-done | bytes 524304 | tf_op jit(solution)/shard_map/psum | solution.py:61
  87.1 7.8 %convolution_bitcast_fusion.3 = f32[4096,128]{0,1:T(8,128)} fusion(bf16[4096,1024]{1,0:T(8,128)(2,1)} %param.6, f32[1024,128]{1,0:T(8,128)} %all-reduce.7.cloned.1.call-done, f32[]{:T(128)} %bitcast), kind=kOutput, calls=%fused_computation.3 | convolution fusion | flops 1074003968 | bytes 11010052 | tf_op jit(solution)/shard_map/while/body/eval_jaxpr/dot_general | solution.py:65
  94.9 0.0 all-reduce.9.cloned.1.call-update
  94.9 0.0 all-reduce.11.cloned.1.call-start
  95.0 1.9 copy.5
  96.9 0.0 copy-start.1
  96.9 118.5 %all-reduce.9.cloned.1.call-done = f32[4096,128]{0,1:T(8,128)} async-done(((f32[4096,128]{0,1:T(8,128)}), f32[4096,128]{0,1:T(8,128)}) %all-reduce.9.cloned.1.call-update) | async-done | bytes 2097168 | tf_op jit(solution)/shard_map/while/body/eval_jaxpr/psum | solution.py:66
  215.4 8.2 %convolution_bitcast_fusion.4 = f32[1024,128]{1,0:T(8,128)} fusion(bf16[4096,1024]{1,0:T(8,128)(2,1)} %param.6, f32[4096,128]{0,1:T(8,128)S(1)} %copy.5, f32[4096,128]{0,1:T(8,128)} %all-reduce.9.cloned.1.call-done, f32[]{:T(128)S(6)} %mul.38), kind=kOutput, calls=%fused_computation.6 | convolution fusion | flops 1075314688 | bytes 13107204 | tf_op jit(solution)/shard_map/while/body/eval_jaxpr/dot_general | solution.py:58
  223.6 0.0 all-reduce.11.cloned.1.call-update
  223.7 0.0 all-reduce.13.cloned.1.call-start
  223.7 68.8 %all-reduce.11.cloned.1.call-done = f32[1024,128]{1,0:T(8,128)} async-done(((f32[1024,128]{1,0:T(8,128)}), f32[1024,128]{1,0:T(8,128)}) %all-reduce.11.cloned.1.call-update) | async-done | bytes 524304 | tf_op jit(solution)/shard_map/while/body/eval_jaxpr/psum | solution.py:61
  292.5 0.0 copy-done.1
  292.5 7.8 %convolution_bitcast_fusion.2 = f32[4096,128]{0,1:T(8,128)} fusion(bf16[4096,1024]{1,0:T(8,128)(2,1)} %param.6, f32[1024,128]{1,0:T(8,128)} %all-reduce.11.cloned.1.call-done, f32[1024,128]{1,0:T(8,128)S(1)} %copy-done.1, f32[]{:T(128)} %bitcast, f32[]{:T(128)S(6)} %mul.38), kind=kOutput, calls=%fused_computation.2 | convolution fusion | flops 1074266112 | bytes 11534344 | tf_op jit(solution)/shard_map/dot_general | solution.py:65
  300.3 0.0 all-reduce.13.cloned.1.call-update
  300.4 0.0 all-reduce.15.cloned.1.call-start
  300.4 120.5 %all-reduce.13.cloned.1.call-done = f32[4096,128]{0,1:T(8,128)} async-done(((f32[4096,128]{0,1:T(8,128)}), f32[4096,128]{0,1:T(8,128)}) %all-reduce.13.cloned.1.call-update) | async-done | bytes 2097168 | tf_op jit(solution)/shard_map/psum | solution.py:66
  420.9 2.6 multiply_subtract_fusion
  423.5 0.0 copy-start
  423.6 1.3 copy-done
  424.9 2.4 fusion.24
  427.3 0.0 all-reduce.15.cloned.1.call-update
  427.3 0.2 all-reduce.17.cloned.1.call-start
  427.6 66.3 %all-reduce.15.cloned.1.call-done = f32[128,128]{0,1:T(8,128)} async-done(((f32[128,128]{0,1:T(8,128)}), f32[128,128]{0,1:T(8,128)}) %all-reduce.15.cloned.1.call-update) | async-done | bytes 65552 | tf_op jit(solution)/shard_map/psum | solution.py:72
  493.8 0.9 copy.7
  494.8 0.9 fusion.9
  495.6 11.7 %cholesky.44 = f32[128,128]{1,0:T(8,128)S(1)} custom-call(f32[128,128]{1,0:T(8,128)S(1)} %fusion.9), custom_call_target="Cholesky" | custom-call | tf_op jit(solution)/shard_map/jit(cholesky)/cholesky | solution.py:29
  507.4 0.6 compare_reduce_fusion.1
  508.0 0.7 fusion.13
  508.7 9.8 %custom-call.6 = f32[1,128,128]{1,2,0:T(8,128)S(1)} custom-call(f32[1,128,128]{2,1,0:T(8,128)S(1)} %fusion.13), custom_call_target="InvertDiagBlocksLowerTriangular" | custom-call | tf_op jit(solution)/shard_map/triangular_solve/custom-call.0 | solution.py:23
  518.5 3.5 convolution_bitcast_fusion.1
  522.0 2.4 fusion.25
  524.4 0.0 all-reduce.17.cloned.1.call-update
  524.4 69.9 %all-reduce.17.cloned.1.call-done = f32[128,128]{0,1:T(8,128)} async-done(((f32[128,128]{0,1:T(8,128)}), f32[128,128]{0,1:T(8,128)}) %all-reduce.17.cloned.1.call-update) | async-done | bytes 65552 | tf_op jit(solution)/shard_map/psum | solution.py:72
  594.4 0.9 copy.9
  595.3 0.9 fusion.7
  596.2 11.9 %cholesky.55 = f32[128,128]{1,0:T(8,128)S(1)} custom-call(f32[128,128]{1,0:T(8,128)S(1)} %fusion.7), custom_call_target="Cholesky" | custom-call | tf_op jit(solution)/shard_map/jit(cholesky)/cholesky | solution.py:31
  608.1 0.7 compare_reduce_fusion
  608.8 2.3 convolution_multiply_fusion
  611.1 0.7 select_bitcast_fusion
  611.8 9.8 %custom-call.7 = f32[1,128,128]{1,2,0:T(8,128)S(1)} custom-call(f32[1,128,128]{2,1,0:T(8,128)S(1)} %select_bitcast_fusion), custom_call_target="InvertDiagBlocksLowerTriangular" | custom-call | tf_op jit(solution)/shard_map/triangular_solve/custom-call.0 | solution.py:23
  621.6 1.9 convolution_bitcast_fusion
  623.6 0.7 copy.10
  (3 shorter events, 0.1 us)
Async XLA Ops:
  7.2 80.0 %all-reduce.7.cloned.1.call-start = ((), (), s32[]{:S(2)}) async-start(), calls=%async_computation | async-start | bytes 1048576 | tf_op jit(solution)/shard_map/psum | solution.py:61
  14.4 201.1 %all-reduce.9.cloned.1.call-start = ((), (), s32[]{:S(2)}) async-start(), calls=%async_computation.1 | async-start | bytes 4194304 | tf_op jit(solution)/shard_map/while/body/eval_jaxpr/psum | solution.py:66
  94.9 197.6 %all-reduce.11.cloned.1.call-start = ((), (), s32[]{:S(2)}) async-start(), calls=%async_computation.2 | async-start | bytes 1048576 | tf_op jit(solution)/shard_map/while/body/eval_jaxpr/psum | solution.py:61
  96.9 195.6 %copy-start.1 = (f32[1024,128]{1,0:T(8,128)S(1)}, f32[1024,128]{1,0:T(8,128)}, u32[]{:S(2)}) copy-start(f32[1024,128]{1,0:T(8,128)} %all-reduce.7.cloned.1.call-done) | copy-start | bytes 1572868
  223.7 197.2 %all-reduce.13.cloned.1.call-start = ((), (), s32[]{:S(2)}) async-start(), calls=%async_computation.3 | async-start | bytes 4194304 | tf_op jit(solution)/shard_map/psum | solution.py:66
  300.4 193.5 %all-reduce.15.cloned.1.call-start = ((), (), s32[]{:S(2)}) async-start(), calls=%async_computation.4 | async-start | bytes 131072 | tf_op jit(solution)/shard_map/psum | solution.py:72
  423.5 1.4 copy-start
  427.3 167.0 %all-reduce.17.cloned.1.call-start = ((), (), s32[]{:S(2)}) async-start(), calls=%async_computation.5 | async-start | bytes 131072 | tf_op jit(solution)/shard_map/psum | solution.py:72
Sparse Core Ops, SparseCore 0:
  14.5 72.5 all-reduce.6
  95.0 120.3 all-reduce.8
  223.8 68.6 all-reduce.10
  300.5 120.3 all-reduce.12
  427.5 66.3 all-reduce.14
  524.6 69.7 all-reduce.16
where the time goes:
time: 636 us; the launch traced here: 631 us
  waiting for transfers between devices  516 us (81%)
  other arithmetic  50.4 us (8%)
  matrix products  43.4 us (7%)
  between operations  14.9 us (2%)
    psum x2, waiting for transfers between devices, step_odd(): return lax.psum(partial_sum, 'col')  239 us
    psum x2, waiting for transfers between devices, step_even(): return lax.psum(partial_sum, 'row')  141 us
    psum x2, waiting for transfers between devices, combine_rows(): return lax.psum(matrix, 'row')  136 us
    another operation x4, other arithmetic, right_solve(): lax.linalg.triangular_solve(lower, vectors, left_side=False, lower=True,...  21 us
    dot_general x2, matrix products, step_odd(): jnp.dot(hamiltonian, operand, preferred_element_type=jnp.float32)  15.6 us
    dot_general x2, matrix products, step_even(): lax.dot_general(hamiltonian, operand, (((0,), (0,)), ((), ())), preferred...  15.3 us
  transfers between devices with their start and end apart: 6, of which 6 were waited for; matrix products, arithmetic and copies ran while one was open for 0% of the time, Pallas kernels for 0%

commit v1 on v0

v1 whole, which is shorter than its diff:
```python
import math

import jax
import jax.numpy as jnp
from jax import lax
from jax.sharding import PartitionSpec as P

N = 32768
K = 128
HIGHEST = lax.Precision.HIGHEST
PLANE = ("x", "y")


def contract_rows(left, right, **kwargs):
    return lax.dot_general(
        left, right, (((0,), (0,)), ((), ())), preferred_element_type=jnp.float32, **kwargs
    )


def scatter_sum(parts, axes):
    return jnp.sum(lax.all_to_all(parts, axes, 0, 0, tiled=True).astype(jnp.float32), axis=0)


def gather(block, axes, count):
    copies = jnp.broadcast_to(block[None], (count, *block.shape))
    return lax.all_to_all(copies, axes, 0, 0, tiled=True)


def swap_core(block):
    return lax.ppermute(block, "core", ((0, 1), (1, 0)))


def body(hamiltonian, start_block, spectral_bound):
    inverse_bound = 1.0 / spectral_bound[0]
    block_rows, block_cols = hamiltonian.shape
    row_count = lax.axis_size("row")
    plane_count = lax.axis_size("x") * lax.axis_size("y")
    core = lax.axis_index("core")
    plane = lax.axis_index("x") * lax.axis_size("y") + lax.axis_index("y")
    half = block_rows // 2
    share = half // plane_count
    col_share = block_cols // row_count
    first_row = core * half + plane * share

    def step_even(vectors):
        parts = contract_rows(hamiltonian, vectors).astype(jnp.bfloat16)
        return scatter_sum(parts.reshape(row_count, col_share, K), "row")

    def gather_even(slice_):
        return gather(slice_.astype(jnp.bfloat16), "row", row_count).reshape(block_cols, K)

    def step_odd(vectors):
        part = jnp.dot(hamiltonian, vectors, preferred_element_type=jnp.float32)
        other = lax.dynamic_slice_in_dim(part, (1 - core) * half, half, 0)
        mine = lax.dynamic_slice_in_dim(part, core * half, half, 0)
        pair = mine + swap_core(other.astype(jnp.bfloat16)).astype(jnp.float32)
        return scatter_sum(pair.astype(jnp.bfloat16).reshape(plane_count, share, K), PLANE)

    def gather_odd(slice_):
        mine = gather(slice_, PLANE, plane_count).reshape(half, K)
        other = swap_core(mine)
        whole = jnp.zeros((block_rows, K), slice_.dtype)
        whole = lax.dynamic_update_slice_in_dim(whole, mine, core * half, 0)
        return lax.dynamic_update_slice_in_dim(whole, other, (1 - core) * half, 0)

    def sum_rows(matrix):
        return jnp.sum(gather(matrix, "row", row_count), axis=0)

    def right_solve(lower, vectors):
        return lax.linalg.triangular_solve(
            lower, vectors, left_side=False, lower=True, transpose_a=True
        )

    zeroth = lax.dynamic_slice_in_dim(start_block, first_row, share, 0)
    first = inverse_bound * step_even(start_block.astype(jnp.bfloat16))
    second = 2.0 * inverse_bound * step_odd(gather_even(first)) - zeroth
    third = 2.0 * inverse_bound * step_even(gather_odd(second.astype(jnp.bfloat16))) - first
    fourth = 2.0 * inverse_bound * step_odd(gather_even(third)) - second
    filtered = gather_odd(fourth)

    root = math.sqrt(N)
    lower_one = jnp.linalg.cholesky(sum_rows(contract_rows(filtered, filtered, precision=HIGHEST)))
    first_basis = right_solve(lower_one, filtered)
    lower_two = jnp.linalg.cholesky(
        sum_rows(contract_rows(first_basis, first_basis, precision=HIGHEST))
    )
    out_rows = block_rows // (2 * plane_count)
    out_first = (plane * 2 + core) * out_rows
    own = lax.dynamic_slice_in_dim(first_basis, out_first, out_rows, 0)
    basis = right_solve(lower_two, own) * root
    triangle = jnp.dot(lower_two.T, lower_one.T, precision=HIGHEST)
    return (basis, triangle / root)


def solution(mesh):
    rows = mesh.shape["row"]
    torus = jax.sharding.Mesh(mesh.devices.reshape(rows, 4, 4, 2), ("row", "x", "y", "core"))
    col = ("x", "y", "core")
    in_specs = (P("row", col), P("row", None), P())
    out_specs = (P(("row", *col), None), P())
    return jax.shard_map(
        body, mesh=torus, in_specs=in_specs, out_specs=out_specs, check_vma=False
    )
```

time: 636 us -> 272 us (0.43)
  waiting for transfers between devices: 516 us -> 52.2 us
  blocking collectives: 0 us -> 94.2 us
  starting transfers between devices: 0.43 us -> 33.7 us
  between operations: 14.9 us -> 1.66 us
    psum x6 -> x0, waiting for transfers between devices: 516 us -> none  [the longest x2 239 us: step_odd(): return lax.psum(partial_sum, 'col')]
    all_to_all x0 -> x6, blocking collectives: none -> 94.2 us  [the longest x4 66.1 us: gather(): return lax.all_to_all(copies, axes, 0, 0, tiled=True)]
    all_to_all x0 -> x4, waiting for transfers between devices: none -> 45.7 us  [the longest x2 25.7 us: gather(): return lax.all_to_all(copies, axes, 0, 0, tiled=True)]
    all_to_all x0 -> x4, starting transfers between devices: none -> 22.9 us  [the longest x2 15.8 us: scatter_sum(): lax.all_to_all(parts, axes, 0, 0, tiled=True).astype(jnp.float32)]
    ppermute x0 -> x4, starting transfers between devices: none -> 10.8 us  [swap_core(): return lax.ppermute(block, 'core', ((0, 1), (1, 0)))]
    ppermute x0 -> x4, waiting for transfers between devices: none -> 6.45 us  [swap_core(): return lax.ppermute(block, 'core', ((0, 1), (1, 0)))]
  transfers between devices with their start and end apart: 6 -> 8, of which waited for: 6 -> 8; matrix products, arithmetic and copies ran while one was open for 0% -> 0% of each run, Pallas kernels for 0% -> 0%
where the time goes in v1:
time: 272 us; the launch traced here: 271 us
  blocking collectives  94.2 us (35%)
  waiting for transfers between devices  52.2 us (19%)
  other arithmetic  48.8 us (18%)
  matrix products  37.2 us (14%)
  starting transfers between devices  33.7 us (12%)
  local copies, waits for them, and re-layouts  3.01 us (1%)
    all_to_all x4, blocking collectives, gather(): return lax.all_to_all(copies, axes, 0, 0, tiled=True)  66.1 us
    all_to_all x2, blocking collectives, scatter_sum(): lax.all_to_all(parts, axes, 0, 0, tiled=True).astype(jnp.float32)  28.1 us
    all_to_all x2, waiting for transfers between devices, gather(): return lax.all_to_all(copies, axes, 0, 0, tiled=True)  25.7 us
    another operation x4, other arithmetic, right_solve(): lax.linalg.triangular_solve(lower, vectors, left_side=False, lower=True,...  20.9 us
    all_to_all x2, waiting for transfers between devices, scatter_sum(): lax.all_to_all(parts, axes, 0, 0, tiled=True).astype(jnp.float32)  20 us
    dot_general x4, matrix products, contract_rows(): lax.dot_general(left, right, (((0,), (0,)), ((), ())), preferred_element_...  18.8 us
    all_to_all x2, starting transfers between devices, scatter_sum(): lax.all_to_all(parts, axes, 0, 0, tiled=True).astype(jnp.float32)  15.8 us
    dot_general x2, matrix products, step_odd(): part = jnp.dot(hamiltonian, vectors, preferred_element_type=jnp.float32)  12.6 us
  transfers between devices with their start and end apart: 8, of which 8 were waited for; matrix products, arithmetic and copies ran while one was open for 0% of the time, Pallas kernels for 0%

profile of v1, /device:TPU:1, one launch (start us, length us, event | category | flops | bytes accessed | tf_op | source)
XLA Modules:
  0.0 270.7 jit_solution(12875942159672449544)
XLA Ops:
  0.6 7.1 %convolution_convert_fusion.1 = bf16[1024,128]{1,0:T(8,128)(2,1)} fusion(bf16[4096,1024]{1,0:T(8,128)(2,1)} %param.4, f32[4096,128]{1,0:T(8,128)} %param.5), kind=kOutput, calls=%fused_computation.1 | convolution fusion | flops 1074397184 | bytes 10747904 | tf_op jit(solution)/shard_map/dot_general | solution.py:15
  7.7 9.0 %all-to-all-start = ((bf16[8,128,128]{2,1,0:T(8,128)(2,1)}), bf16[8,128,128]{2,1,0:T(8,128)(2,1)S(1)}, u32[]{:S(2)}, u32[]{:S(2)}) async-start(bf16[8,128,128]{2,1,0:T(8,128)(2,1)} %bitcast.1), calls=%async_computation | async-start | bytes 524288 | tf_op jit(solution)/shard_map/all_to_all | solution.py:21
  17.4 9.7 %all-to-all-done = bf16[8,128,128]{2,1,0:T(8,128)(2,1)S(1)} async-done(((bf16[8,128,128]{2,1,0:T(8,128)(2,1)}), bf16[8,128,128]{2,1,0:T(8,128)(2,1)S(1)}, u32[]{:S(2)}, u32[]{:S(2)}) %all-to-all-start) | async-done | bytes 262176 | tf_op jit(solution)/shard_map/all_to_all | solution.py:21
  27.1 0.7 broadcast_in_dim.18
  27.9 3.4 %all-to-all-start.1 = ((bf16[8,128,128]{2,1,0:T(8,128)(2,1)}), bf16[8,128,128]{2,1,0:T(8,128)(2,1)S(1)}, u32[]{:S(2)}, u32[]{:S(2)}) async-start(bf16[8,128,128]{2,1,0:T(8,128)(2,1)} %broadcast_in_dim.18), calls=%async_computation.1 | async-start | bytes 524288 | tf_op jit(solution)/shard_map/all_to_all | solution.py:26
  31.3 9.3 %all-to-all-done.1 = bf16[8,128,128]{2,1,0:T(8,128)(2,1)S(1)} async-done(((bf16[8,128,128]{2,1,0:T(8,128)(2,1)}), bf16[8,128,128]{2,1,0:T(8,128)(2,1)S(1)}, u32[]{:S(2)}, u32[]{:S(2)}) %all-to-all-start.1) | async-done | bytes 262176 | tf_op jit(solution)/shard_map/all_to_all | solution.py:26
  40.6 6.3 %fusion.22 = f32[128,4096]{1,0:T(8,128)S(1)} fusion(bf16[1024,128]{1,0:T(8,128)(2,1)S(1)} %bitcast.75, bf16[4096,1024]{1,0:T(8,128)(2,1)} %param.4), kind=kOutput, calls=%fused_computation.57 | convolution fusion | flops 1073741824 | bytes 10747904 | tf_op jit(solution)/shard_map/dot_general | solution.py:53
  47.0 3.6 %collective-permute-start = (bf16[2048,128]{0,1:T(8,128)(2,1)S(1)}, bf16[2048,128]{0,1:T(8,128)(2,1)S(1)}, u32[]{:S(2)}, u32[]{:S(2)}) collective-permute-start(bf16[2048,128]{0,1:T(8,128)(2,1)S(1)} %fusion.4), channel_id=1, source_target_pairs={{0,1},{1,0},{2,3},{3,2},{4,5},{5,4},{6,7},{7,6},{8,9},{9,8},{10,11... | collective-permute-start | bytes 1572872 | tf_op jit(solution)/shard_map/ppermute | solution.py:30
  50.6 1.5 collective-permute-done
  52.1 0.9 copy_bitcast_fusion.1
  53.1 6.8 %all-to-all-start.2 = ((bf16[16,128,128]{1,2,0:T(8,128)(2,1)}), bf16[16,128,128]{1,2,0:T(8,128)(2,1)S(1)}, u32[]{:S(2)}, u32[]{:S(2)}) async-start(bf16[16,128,128]{1,2,0:T(8,128)(2,1)} %copy_bitcast_fusion.1), calls=%async_computation.2 | async-start | bytes 1048576 | tf_op jit(solution)/shard_map/all_to_all | solution.py:21
  59.9 10.3 %all-to-all-done.2 = bf16[16,128,128]{1,2,0:T(8,128)(2,1)S(1)} async-done(((bf16[16,128,128]{1,2,0:T(8,128)(2,1)}), bf16[16,128,128]{1,2,0:T(8,128)(2,1)S(1)}, u32[]{:S(2)}, u32[]{:S(2)}) %all-to-all-start.2) | async-done | bytes 524320 | tf_op jit(solution)/shard_map/all_to_all | solution.py:21
  70.4 0.9 fusion.18
  71.3 12.7 %all_to_all.50 = bf16[16,128,128]{2,1,0:T(8,128)(2,1)S(1)} all-to-all(bf16[16,128,128]{2,1,0:T(8,128)(2,1)S(1)} %broadcast_in_dim.19), channel_id=1, replica_groups=mesh['row'=8,'x'=4,'y'=4,'core'=2] {'x','y'}, dimensions={0} | all-to-all | bytes 1048576 | tf_op jit(solution)/shard_map/all_to_all | solution.py:26
  84.0 3.3 %collective-permute-start.1 = (bf16[2048,128]{1,0:T(8,128)(2,1)S(1)}, bf16[2048,128]{1,0:T(8,128)(2,1)S(1)}, u32[]{:S(2)}, u32[]{:S(2)}) collective-permute-start(bf16[2048,128]{1,0:T(8,128)(2,1)S(1)} %bitcast.72), channel_id=1, source_target_pairs={{0,1},{1,0},{2,3},{3,2},{4,5},{5,4},{6,7},{7,6},{8,9},{9,8},{10,11... | collective-permute-start | bytes 1572872 | tf_op jit(solution)/shard_map/ppermute | solution.py:30
  87.3 0.1 broadcast_in_dim.17
  87.5 1.3 collective-permute-done.1
  88.9 4.7 %fusion = bf16[16,8,8,128]{3,2,1,0:T(8,128)(2,1)S(1)} fusion(bf16[4096,128]{1,0:T(8,128)(2,1)S(1)} %constant_dynamic-update-slice_fusion.2, bf16[4096,1024]{1,0:T(8,128)(2,1)} %param.4), kind=kOutput, calls=%fused_computation.2 | convolution fusion | flops 1073872896 | bytes 9699328 | tf_op jit(solution)/shard_map/dot_general | solution.py:15
  93.7 14.8 %all_to_all.51 = bf16[8,128,128]{1,2,0:T(8,128)(2,1)S(1)} all-to-all(bf16[8,128,128]{1,2,0:T(8,128)(2,1)S(1)} %bitcast.74), channel_id=1, replica_groups=mesh['row'=8,'x'=4,'y'=4,'core'=2] {'row'}, dimensions={0} | all-to-all | bytes 524288 | tf_op jit(solution)/shard_map/all_to_all | solution.py:21
  108.7 14.6 %all_to_all.52 = bf16[8,128,128]{2,1,0:T(8,128)(2,1)S(1)} all-to-all(bf16[8,128,128]{2,1,0:T(8,128)(2,1)S(1)} %broadcast_in_dim.20), channel_id=1, replica_groups=mesh['row'=8,'x'=4,'y'=4,'core'=2] {'row'}, dimensions={0} | all-to-all | bytes 524288 | tf_op jit(solution)/shard_map/all_to_all | solution.py:26
  123.3 6.3 %fusion.23 = f32[128,4096]{1,0:T(8,128)S(1)} fusion(bf16[1024,128]{1,0:T(8,128)(2,1)S(1)} %bitcast.76, bf16[4096,1024]{1,0:T(8,128)(2,1)} %param.4), kind=kOutput, calls=%fused_computation.58 | convolution fusion | flops 1073741824 | bytes 10747904 | tf_op jit(solution)/shard_map/dot_general | solution.py:53
  129.7 0.7 collective-permute-start.2
  130.4 1.5 collective-permute-done.2
  131.9 0.1 copy_bitcast_fusion
  132.1 13.3 %all_to_all.53 = bf16[16,128,128]{1,2,0:T(8,128)(2,1)S(1)} all-to-all(bf16[16,128,128]{1,2,0:T(8,128)(2,1)S(1)} %copy_bitcast_fusion), channel_id=1, replica_groups=mesh['row'=8,'x'=4,'y'=4,'core'=2] {'x','y'}, dimensions={0} | all-to-all | bytes 1048576 | tf_op jit(solution)/shard_map/all_to_all | solution.py:21
  145.6 0.9 multiply_subtract_fusion
  146.4 0.1 broadcast_in_dim.21
  146.5 18.4 %all_to_all.54 = f32[16,128,128]{2,1,0:T(8,128)S(1)} all-to-all(f32[16,128,128]{2,1,0:T(8,128)S(1)} %broadcast_in_dim.21), channel_id=1, replica_groups=mesh['row'=8,'x'=4,'y'=4,'core'=2] {'x','y'}, dimensions={0} | all-to-all | bytes 2097152 | tf_op jit(solution)/shard_map/all_to_all | solution.py:26
  164.9 3.2 %collective-permute-start.3 = (f32[2048,128]{1,0:T(8,128)S(1)}, f32[2048,128]{1,0:T(8,128)S(1)}, u32[]{:S(2)}, u32[]{:S(2)}) collective-permute-start(f32[2048,128]{1,0:T(8,128)S(1)} %bitcast.70), channel_id=1, source_target_pairs={{0,1},{1,0},{2,3},{3,2},{4,5},{5,4},{6,7},{7,6},{8,9},{9,8},{10,11... | collective-permute-start | bytes 3145736 | tf_op jit(solution)/shard_map/ppermute | solution.py:30
  168.1 0.1 broadcast_in_dim.16
  168.4 2.1 collective-permute-done.3
  170.5 3.5 %fusion.24 = f32[128,128]{1,0:T(8,128)S(1)} fusion(f32[4096,128]{1,0:T(8,128)S(1)} %constant_dynamic-update-slice_fusion), kind=kOutput, calls=%fused_computation.59 | convolution fusion | flops 805306368 | bytes 2162688 | tf_op jit(solution)/shard_map/dot_general | solution.py:15
  174.0 20.4 %all_to_all.55 = f32[8,128,128]{2,1,0:T(8,128)S(1)} all-to-all(f32[8,128,128]{2,1,0:T(8,128)S(1)} %broadcast_in_dim.22), channel_id=1, replica_groups=mesh['row'=8,'x'=4,'y'=4,'core'=2] {'row'}, dimensions={0} | all-to-all | bytes 1048576 | tf_op jit(solution)/shard_map/all_to_all | solution.py:26
  194.5 11.7 %cholesky.44 = f32[128,128]{1,0:T(8,128)S(1)} custom-call(f32[128,128]{1,0:T(8,128)S(1)} %fusion.12), custom_call_target="Cholesky" | custom-call | tf_op jit(solution)/shard_map/jit(cholesky)/cholesky | solution.py:82
  206.3 0.6 compare_reduce_fusion.1
  206.9 0.7 select_bitcast_fusion.1
  207.6 9.8 %custom-call.8 = f32[1,128,128]{1,2,0:T(8,128)S(1)} custom-call(f32[1,128,128]{2,1,0:T(8,128)S(1)} %select_bitcast_fusion.1), custom_call_target="InvertDiagBlocksLowerTriangular" | custom-call | tf_op jit(solution)/shard_map/triangular_solve | solution.py:70
  217.4 1.9 fusion.10
  219.3 3.6 %fusion.25 = f32[128,128]{1,0:T(8,128)S(1)} fusion(f32[4096,128]{1,0:T(8,128)S(1)} %fusion.10), kind=kOutput, calls=%fused_computation.60 | convolution fusion | flops 805306368 | bytes 2162688 | tf_op jit(solution)/shard_map/dot_general | solution.py:15
  222.9 0.8 broadcast_in_dim.24
  223.7 3.7 %all-to-all-start.9 = ((f32[8,128,128]{2,1,0:T(8,128)}), f32[8,128,128]{2,1,0:T(8,128)S(1)}, u32[]{:S(2)}, u32[]{:S(2)}) async-start(f32[8,128,128]{2,1,0:T(8,128)} %broadcast_in_dim.24), calls=%async_computation.9 | async-start | bytes 1048576 | tf_op jit(solution)/shard_map/all_to_all | solution.py:26
  227.5 16.4 %all-to-all-done.9 = f32[8,128,128]{2,1,0:T(8,128)S(1)} async-done(((f32[8,128,128]{2,1,0:T(8,128)}), f32[8,128,128]{2,1,0:T(8,128)S(1)}, u32[]{:S(2)}, u32[]{:S(2)}) %all-to-all-start.9) | async-done | bytes 524320 | tf_op jit(solution)/shard_map/all_to_all | solution.py:26
  244.0 11.7 %cholesky.55 = f32[128,128]{1,0:T(8,128)S(1)} custom-call(f32[128,128]{1,0:T(8,128)S(1)} %fusion.9), custom_call_target="Cholesky" | custom-call | tf_op jit(solution)/shard_map/jit(cholesky)/cholesky | solution.py:84
  255.7 0.6 compare_reduce_fusion
  256.4 2.2 convolution_multiply_fusion
  258.6 0.6 select_bitcast_fusion
  259.2 9.8 %custom-call.9 = f32[1,128,128]{1,2,0:T(8,128)S(1)} custom-call(f32[1,128,128]{2,1,0:T(8,128)S(1)} %select_bitcast_fusion), custom_call_target="InvertDiagBlocksLowerTriangular" | custom-call | tf_op jit(solution)/shard_map/triangular_solve | solution.py:70
  269.0 1.7 convolution_multiply_fusion.1
  (29 shorter events, 1.5 us)
Async XLA Ops:
  7.7 19.4 %all-to-all-start = ((bf16[8,128,128]{2,1,0:T(8,128)(2,1)}), bf16[8,128,128]{2,1,0:T(8,128)(2,1)S(1)}, u32[]{:S(2)}, u32[]{:S(2)}) async-start(bf16[8,128,128]{2,1,0:T(8,128)(2,1)} %bitcast.1), calls=%async_computation | async-start | bytes 524288 | tf_op jit(solution)/shard_map/all_to_all | solution.py:21
  27.9 12.8 %all-to-all-start.1 = ((bf16[8,128,128]{2,1,0:T(8,128)(2,1)}), bf16[8,128,128]{2,1,0:T(8,128)(2,1)S(1)}, u32[]{:S(2)}, u32[]{:S(2)}) async-start(bf16[8,128,128]{2,1,0:T(8,128)(2,1)} %broadcast_in_dim.18), calls=%async_computation.1 | async-start | bytes 524288 | tf_op jit(solution)/shard_map/all_to_all | solution.py:26
  47.0 5.1 %collective-permute-start = (bf16[2048,128]{0,1:T(8,128)(2,1)S(1)}, bf16[2048,128]{0,1:T(8,128)(2,1)S(1)}, u32[]{:S(2)}, u32[]{:S(2)}) collective-permute-start(bf16[2048,128]{0,1:T(8,128)(2,1)S(1)} %fusion.4), channel_id=1, source_target_pairs={{0,1},{1,0},{2,3},{3,2},{4,5},{5,4},{6,7},{7,6},{8,9},{9,8},{10,11... | collective-permute-start | bytes 1572872 | tf_op jit(solution)/shard_map/ppermute | solution.py:30
  53.1 17.1 %all-to-all-start.2 = ((bf16[16,128,128]{1,2,0:T(8,128)(2,1)}), bf16[16,128,128]{1,2,0:T(8,128)(2,1)S(1)}, u32[]{:S(2)}, u32[]{:S(2)}) async-start(bf16[16,128,128]{1,2,0:T(8,128)(2,1)} %copy_bitcast_fusion.1), calls=%async_computation.2 | async-start | bytes 1048576 | tf_op jit(solution)/shard_map/all_to_all | solution.py:21
  84.0 4.8 %collective-permute-start.1 = (bf16[2048,128]{1,0:T(8,128)(2,1)S(1)}, bf16[2048,128]{1,0:T(8,128)(2,1)S(1)}, u32[]{:S(2)}, u32[]{:S(2)}) collective-permute-start(bf16[2048,128]{1,0:T(8,128)(2,1)S(1)} %bitcast.72), channel_id=1, source_target_pairs={{0,1},{1,0},{2,3},{3,2},{4,5},{5,4},{6,7},{7,6},{8,9},{9,8},{10,11... | collective-permute-start | bytes 1572872 | tf_op jit(solution)/shard_map/ppermute | solution.py:30
  129.7 2.2 collective-permute-start.2
  164.9 5.5 %collective-permute-start.3 = (f32[2048,128]{1,0:T(8,128)S(1)}, f32[2048,128]{1,0:T(8,128)S(1)}, u32[]{:S(2)}, u32[]{:S(2)}) collective-permute-start(f32[2048,128]{1,0:T(8,128)S(1)} %bitcast.70), channel_id=1, source_target_pairs={{0,1},{1,0},{2,3},{3,2},{4,5},{5,4},{6,7},{7,6},{8,9},{9,8},{10,11... | collective-permute-start | bytes 3145736 | tf_op jit(solution)/shard_map/ppermute | solution.py:30
  219.3 3.6 %copy-start = (f32[4096,128]{1,0:T(8,128)}, f32[4096,128]{1,0:T(8,128)S(1)}, u32[]{:S(2)}) copy-start(f32[4096,128]{1,0:T(8,128)S(1)} %fusion.10) | copy-start | bytes 6291460
  223.7 20.1 %all-to-all-start.9 = ((f32[8,128,128]{2,1,0:T(8,128)}), f32[8,128,128]{2,1,0:T(8,128)S(1)}, u32[]{:S(2)}, u32[]{:S(2)}) async-start(f32[8,128,128]{2,1,0:T(8,128)} %broadcast_in_dim.24), calls=%async_computation.9 | async-start | bytes 1048576 | tf_op jit(solution)/shard_map/all_to_all | solution.py:26

commit v2 on v1

v2 whole, which is shorter than its diff:
```python
import math

import jax
import jax.numpy as jnp
from jax import lax
from jax.experimental import pallas as pl
from jax.experimental.pallas import tpu as pltpu
from jax.sharding import PartitionSpec as P

N = 32768
K = 128
HALF = K // 2
PACK = HALF + 8
PANEL = 8
HIGHEST = lax.Precision.HIGHEST
PLANE = ("x", "y")


def f32_shape(*shape):
    return jax.ShapeDtypeStruct(shape, jnp.float32)


def gram_of(block):
    return lax.dot_general(
        block, block, (((0,), (0,)), ((), ())), precision=HIGHEST, preferred_element_type=jnp.float32
    )


def times_transposed(block, matrix):
    return lax.dot_general(
        block, matrix, (((1,), (1,)), ((), ())), precision=HIGHEST, preferred_element_type=jnp.float32
    )


def factor(gram, upper_ref, inverse_ref):
    count = K // PANEL
    lane = lax.broadcasted_iota(jnp.int32, (PANEL, K), 1)
    sub = lax.broadcasted_iota(jnp.int32, (PANEL, K), 0)
    left = [gram[i * PANEL : (i + 1) * PANEL, :] for i in range(count)]
    right = [jnp.where(lane == sub + i * PANEL, 1.0, 0.0).astype(jnp.float32) for i in range(count)]
    for b in range(count):
        base = b * PANEL
        cols = [
            [
                jnp.broadcast_to(left[i][:, base + k : base + k + 1], (PANEL, K))
                for i in range(b, count)
            ]
            for k in range(PANEL)
        ]
        for k in range(PANEL):
            j = base + k
            root = lax.rsqrt(cols[k][0][k : k + 1, :])
            left_row = left[b][k : k + 1, :] * root
            right_row = right[b][k : k + 1, :] * root
            upper_ref[j : j + 1, :] = jnp.where(lane[:1] >= j, left_row, 0.0)
            inverse_ref[j : j + 1, :] = right_row
            left_row = left_row * root
            right_row = right_row * root
            heads = [cols[m][0][k : k + 1, :] * (root * root) for m in range(k + 1, PANEL)]
            for i in range(b, count):
                col = cols[k][i - b]
                if i == b:
                    if k == PANEL - 1:
                        continue
                    col = jnp.where(sub > k, col, 0.0)
                for m, head in zip(range(k + 1, PANEL), heads):
                    cols[m][i - b] = cols[m][i - b] - col * head
                left[i] = left[i] - col * left_row
                right[i] = right[i] - col * right_row


def grids():
    shape = (HALF, K)
    return lax.broadcasted_iota(jnp.int32, shape, 0), lax.broadcasted_iota(jnp.int32, shape, 1)


def pack(gram, out_ref):
    top, bottom = gram[:HALF], gram[HALF:]
    row, lane = grids()
    triangles = jnp.where(lane >= row, top, pltpu.roll(bottom, HALF, 1))
    diagonal = jnp.sum(jnp.where(lane == row + HALF, bottom, 0.0), axis=0, keepdims=True)
    for i in range(out_ref.shape[0]):
        out_ref[i, :HALF] = triangles
        out_ref[i, HALF:] = jnp.broadcast_to(diagonal, (PACK - HALF, K))


def unpack_sum(parts_ref):
    packed = parts_ref[0]
    for i in range(1, parts_ref.shape[0]):
        packed = packed + parts_ref[i]
    row, lane = grids()
    triangles, diagonal = packed[:HALF], packed[HALF : HALF + 1]
    last = pltpu.roll(jnp.where(lane < row, triangles, 0.0), HALF, 1)
    strict = jnp.concatenate([jnp.where(lane > row, triangles, 0.0), last], axis=0)
    middle = jnp.concatenate(
        [jnp.where(lane == row, triangles, 0.0), jnp.where(lane == row + HALF, diagonal, 0.0)], axis=0
    )
    return strict + strict.T + middle


def first_gram_kernel(even_ref, odd_ref, out_ref):
    pack(gram_of(even_ref[...]) + gram_of(odd_ref[...]), out_ref)


def second_gram_kernel(parts_ref, even_ref, odd_ref, out_ref, upper_ref, inverse_ref):
    factor(unpack_sum(parts_ref), upper_ref, inverse_ref)
    inverse = inverse_ref[...]
    even = times_transposed(even_ref[...], inverse)
    odd = times_transposed(odd_ref[...], inverse)
    pack(gram_of(even) + gram_of(odd), out_ref)


def last_kernel(
    parts_ref, upper_one_ref, inverse_one_ref, block_ref, basis_ref, triangle_ref, upper_ref, inverse_ref
):
    factor(unpack_sum(parts_ref), upper_ref, inverse_ref)
    root = math.sqrt(N)
    first_basis = times_transposed(block_ref[...], inverse_one_ref[...])
    basis_ref[...] = times_transposed(first_basis, inverse_ref[...]) * root
    product = jnp.dot(
        upper_ref[...], upper_one_ref[...], precision=HIGHEST, preferred_element_type=jnp.float32
    )
    triangle_ref[...] = product / root


def first_gram(count, even, odd):
    return pl.pallas_call(first_gram_kernel, out_shape=f32_shape(count, PACK, K))(even, odd)


def second_gram(parts, even, odd):
    shapes = (f32_shape(*parts.shape), f32_shape(K, K), f32_shape(K, K))
    return pl.pallas_call(second_gram_kernel, out_shape=shapes)(parts, even, odd)


def last_step(parts, upper, inverse, block):
    return pl.pallas_call(
        last_kernel,
        out_shape=(f32_shape(*block.shape), f32_shape(K, K)),
        scratch_shapes=[pltpu.VMEM((K, K), jnp.float32)] * 2,
    )(parts, upper, inverse, block)


def scatter_sum(parts, axes):
    return jnp.sum(lax.all_to_all(parts, axes, 0, 0, tiled=True).astype(jnp.float32), axis=0)


def gather(block, axes, count):
    copies = jnp.broadcast_to(block[None], (count, *block.shape))
    return lax.all_to_all(copies, axes, 0, 0, tiled=True)


def swap_core(block):
    return lax.ppermute(block, "core", ((0, 1), (1, 0)))


def body(hamiltonian, start_block, spectral_bound):
    inverse_bound = 1.0 / spectral_bound[0]
    block_rows, block_cols = hamiltonian.shape
    row_count = lax.axis_size("row")
    plane_count = lax.axis_size("x") * lax.axis_size("y")
    core = lax.axis_index("core")
    plane = lax.axis_index("x") * lax.axis_size("y") + lax.axis_index("y")
    share = block_rows // (2 * plane_count)
    col_share = block_cols // row_count

    def step_even(vectors):
        part = lax.dot_general(
            hamiltonian, vectors, (((0,), (0,)), ((), ())), preferred_element_type=jnp.float32
        )
        return scatter_sum(part.astype(jnp.bfloat16).reshape(row_count, col_share, K), "row")

    def gather_even(slice_):
        return gather(slice_.astype(jnp.bfloat16), "row", row_count).reshape(block_cols, K)

    def step_odd(vectors):
        part = jnp.dot(hamiltonian, vectors, preferred_element_type=jnp.float32)
        part = part.reshape(plane_count, 2, share, K)
        other = lax.dynamic_index_in_dim(part, 1 - core, 1, False)
        mine = lax.dynamic_index_in_dim(part, core, 1, False)
        pair = mine + swap_core(other.astype(jnp.bfloat16)).astype(jnp.float32)
        return scatter_sum(pair.astype(jnp.bfloat16), PLANE)

    def gather_odd(slice_):
        mine = gather(slice_, PLANE, plane_count)
        other = swap_core(mine)
        return (jnp.where(core == 0, mine, other), jnp.where(core == 0, other, mine))

    def interleave(even, odd):
        return jnp.stack([even, odd], axis=1).reshape(block_rows, K)

    zeroth = lax.dynamic_slice_in_dim(start_block, (plane * 2 + core) * share, share, 0)
    first = inverse_bound * step_even(start_block.astype(jnp.bfloat16))
    second = 2.0 * inverse_bound * step_odd(gather_even(first)) - zeroth
    third = 2.0 * inverse_bound * step_even(interleave(*gather_odd(second.astype(jnp.bfloat16)))) - first
    fourth = 2.0 * inverse_bound * step_odd(gather_even(third)) - second

    even, odd = (block.reshape(plane_count * share, K) for block in gather_odd(fourth))

    def exchange(parts):
        return lax.all_to_all(parts, "row", 0, 0, tiled=True)

    parts = exchange(first_gram(row_count, even, odd))
    parts, upper, inverse = second_gram(parts, even, odd)
    return last_step(exchange(parts), upper, inverse, fourth)


def solution(mesh):
    rows = mesh.shape["row"]
    torus = jax.sharding.Mesh(mesh.devices.reshape(rows, 4, 4, 2), ("row", "x", "y", "core"))
    col = ("x", "y", "core")
    in_specs = (P("row", col), P("row", None), P())
    out_specs = (P(("row", *col), None), P())
    return jax.shard_map(
        body, mesh=torus, in_specs=in_specs, out_specs=out_specs, check_vma=False
    )
```

time: 272 us -> 242 us (0.89)
  other arithmetic: 48.8 us -> 6.78 us
  Pallas kernels: 0 us -> 19.8 us
  waiting for transfers between devices: 52.2 us -> 33.3 us
  local copies, waits for them, and re-layouts: 3.01 us -> 16.7 us
  blocking collectives: 94.2 us -> 106 us
  matrix products: 37.2 us -> 27.1 us
  starting transfers between devices: 33.7 us -> 29.8 us
    another operation x10 -> x2, other arithmetic: 45.7 us -> 0.18 us  [interleave(): return jnp.stack([even, odd], axis=1).reshape(block_rows, K)]
    all_to_all x0 -> x2, blocking collectives: none -> 31.9 us  [exchange(): return lax.all_to_all(parts, 'row', 0, 0, tiled=True)]
    all_to_all x4 -> x3, blocking collectives: 66.1 us -> 45.7 us  [gather(): return lax.all_to_all(copies, axes, 0, 0, tiled=True)]
    pallas_call x0 -> x3, Pallas kernels: none -> 19.8 us  [the longest x1 9.8 us: second_gram(): pl.pallas_call(second_gram_kernel, out_shape=shapes)(parts, even, odd)]
    all_to_all x2 -> x1, waiting for transfers between devices: 25.7 us -> 9.34 us  [gather(): return lax.all_to_all(copies, axes, 0, 0, tiled=True)]
    dot_general x5 -> x2, matrix products: 21 us -> 11.8 us  [step_even(): lax.dot_general(hamiltonian, vectors, (((0,), (0,)), ((), ())), preferred...]
    reshape x1 -> x3, local copies, waits for them, and re-layouts: 0.05 us -> 6.1 us  [the longest x2 6.06 us: step_odd(): part = part.reshape(plane_count, 2, share, K)]
    dynamic_slice x0 -> x6, local copies, waits for them, and re-layouts: none -> 5.8 us  [the longest x4 3.66 us: step_odd(): mine = lax.dynamic_index_in_dim(part, core, 1, False)]
  transfers between devices with their start and end apart: 8 -> 7, of which waited for: 8 -> 5; matrix products, arithmetic and copies ran while one was open for 0% -> 2% of each run, Pallas kernels for 0% -> 0%
where the time goes in v2:
time: 242 us; the launch traced here: 241 us
  blocking collectives  106 us (44%)
  waiting for transfers between devices  33.3 us (14%)
  starting transfers between devices  29.8 us (12%)
  matrix products  27.1 us (11%)
  Pallas kernels  19.8 us (8%)
  local copies, waits for them, and re-layouts  16.7 us (7%)
  other arithmetic  6.78 us (3%)
    all_to_all x3, blocking collectives, gather(): return lax.all_to_all(copies, axes, 0, 0, tiled=True)  45.7 us
    all_to_all x2, blocking collectives, exchange(): return lax.all_to_all(parts, 'row', 0, 0, tiled=True)  31.9 us
    all_to_all x2, blocking collectives, scatter_sum(): lax.all_to_all(parts, axes, 0, 0, tiled=True).astype(jnp.float32)  28.3 us
    all_to_all x2, waiting for transfers between devices, scatter_sum(): lax.all_to_all(parts, axes, 0, 0, tiled=True).astype(jnp.float32)  20 us
    all_to_all x2, starting transfers between devices, scatter_sum(): lax.all_to_all(parts, axes, 0, 0, tiled=True).astype(jnp.float32)  15.8 us
    dot_general x2, matrix products, step_odd(): part = jnp.dot(hamiltonian, vectors, preferred_element_type=jnp.float32)  15.3 us
    dot_general x2, matrix products, step_even(): lax.dot_general(hamiltonian, vectors, (((0,), (0,)), ((), ())), preferred...  11.8 us
    ppermute x4, starting transfers between devices, swap_core(): return lax.ppermute(block, 'core', ((0, 1), (1, 0)))  10.6 us
  transfers between devices with their start and end apart: 7, of which 5 were waited for; matrix products, arithmetic and copies ran while one was open for 2% of the time, Pallas kernels for 0%

profile of v2, /device:TPU:1, one launch (start us, length us, event | category | flops | bytes accessed | tf_op | source)
XLA Modules:
  0.0 240.8 jit_solution(15555489776849802862)
XLA Ops:
  0.6 7.1 %convolution_convert_fusion.1 = bf16[1024,128]{1,0:T(8,128)(2,1)} fusion(bf16[4096,1024]{1,0:T(8,128)(2,1)} %param.3, f32[4096,128]{1,0:T(8,128)} %param.4), kind=kOutput, calls=%fused_computation.3 | convolution fusion | flops 1074397184 | bytes 10747904 | tf_op jit(solution)/shard_map/dot_general | solution.py:167
  7.7 9.0 %all-to-all-start = ((bf16[8,128,128]{2,1,0:T(8,128)(2,1)}), bf16[8,128,128]{2,1,0:T(8,128)(2,1)S(1)}, u32[]{:S(2)}, u32[]{:S(2)}) async-start(bf16[8,128,128]{2,1,0:T(8,128)(2,1)} %bitcast.1), calls=%async_computation | async-start | bytes 524288 | tf_op jit(solution)/shard_map/all_to_all | solution.py:144
  17.4 9.7 %all-to-all-done = bf16[8,128,128]{2,1,0:T(8,128)(2,1)S(1)} async-done(((bf16[8,128,128]{2,1,0:T(8,128)(2,1)}), bf16[8,128,128]{2,1,0:T(8,128)(2,1)S(1)}, u32[]{:S(2)}, u32[]{:S(2)}) %all-to-all-start) | async-done | bytes 262176 | tf_op jit(solution)/shard_map/all_to_all | solution.py:144
  27.1 0.7 broadcast_in_dim.8
  27.9 3.4 %all-to-all-start.1 = ((bf16[8,128,128]{2,1,0:T(8,128)(2,1)}), bf16[8,128,128]{2,1,0:T(8,128)(2,1)S(1)}, u32[]{:S(2)}, u32[]{:S(2)}) async-start(bf16[8,128,128]{2,1,0:T(8,128)(2,1)} %broadcast_in_dim.8), calls=%async_computation.1 | async-start | bytes 524288 | tf_op jit(solution)/shard_map/all_to_all | solution.py:149
  31.3 9.3 %all-to-all-done.1 = bf16[8,128,128]{2,1,0:T(8,128)(2,1)S(1)} async-done(((bf16[8,128,128]{2,1,0:T(8,128)(2,1)}), bf16[8,128,128]{2,1,0:T(8,128)(2,1)S(1)}, u32[]{:S(2)}, u32[]{:S(2)}) %all-to-all-start.1) | async-done | bytes 262176 | tf_op jit(solution)/shard_map/all_to_all | solution.py:149
  40.6 7.6 %convolution_bitcast_fusion.1 = f32[4096,128]{0,1:T(8,128)} fusion(bf16[1024,128]{1,0:T(8,128)(2,1)S(1)} %bitcast.54, bf16[4096,1024]{1,0:T(8,128)(2,1)} %param.3), kind=kOutput, calls=%fused_computation.1 | convolution fusion | flops 1073741824 | bytes 10747904 | tf_op jit(solution)/shard_map/dot_general | solution.py:176
  48.3 3.0 %reshape.50 = f32[16,2,128,128]{2,1,0,3:T(2,128)S(1)} reshape(f32[4096,128]{0,1:T(8,128)} %convolution_bitcast_fusion.1) | data formatting | bytes 4194304 | tf_op jit(solution)/shard_map/reshape | solution.py:177
  51.3 1.1 constant_dynamic-slice_fusion.2
  52.4 1.9 copy.19
  54.3 3.5 %collective-permute-start = (bf16[16,128,128]{2,1,0:T(8,128)(2,1)}, bf16[16,128,128]{2,1,0:T(8,128)(2,1)}, u32[]{:S(2)}, u32[]{:S(2)}) collective-permute-start(bf16[16,128,128]{2,1,0:T(8,128)(2,1)} %bitcast.56), channel_id=1, source_target_pairs={{0,1},{1,0},{2,3},{3,2},{4,5},{5,4},{6,7},{7,6},{8,9},{9,8},{10,11... | collective-permute-start | bytes 1572872 | tf_op jit(solution)/shard_map/ppermute | solution.py:153
  57.8 1.1 constant_dynamic-slice_fusion.3
  58.9 0.7 copy.10
  59.7 2.0 fusion.2
  61.6 6.8 %all-to-all-start.2 = ((bf16[16,128,128]{2,1,0:T(8,128)(2,1)}), bf16[16,128,128]{2,1,0:T(8,128)(2,1)S(1)}, u32[]{:S(2)}, u32[]{:S(2)}) async-start(bf16[16,128,128]{2,1,0:T(8,128)(2,1)} %fusion.2), calls=%async_computation.2 | async-start | bytes 1048576 | tf_op jit(solution)/shard_map/all_to_all | solution.py:144
  68.4 10.3 %all-to-all-done.2 = bf16[16,128,128]{2,1,0:T(8,128)(2,1)S(1)} async-done(((bf16[16,128,128]{2,1,0:T(8,128)(2,1)}), bf16[16,128,128]{2,1,0:T(8,128)(2,1)S(1)}, u32[]{:S(2)}, u32[]{:S(2)}) %all-to-all-start.2) | async-done | bytes 524320 | tf_op jit(solution)/shard_map/all_to_all | solution.py:144
  78.7 0.1 convert_reduce_fusion.1
  78.8 0.9 fusion.4
  79.7 0.1 broadcast_in_dim.9
  79.8 12.7 %all_to_all.50 = bf16[16,128,128]{2,1,0:T(8,128)(2,1)S(1)} all-to-all(bf16[16,128,128]{2,1,0:T(8,128)(2,1)S(1)} %broadcast_in_dim.9), channel_id=1, replica_groups=mesh['row'=8,'x'=4,'y'=4,'core'=2] {'x','y'}, dimensions={0} | all-to-all | bytes 1048576 | tf_op jit(solution)/shard_map/all_to_all | solution.py:149
  92.5 3.3 %collective-permute-start.1 = (bf16[16,128,128]{2,1,0:T(8,128)(2,1)S(1)}, bf16[16,128,128]{2,1,0:T(8,128)(2,1)S(1)}, u32[]{:S(2)}, u32[]{:S(2)}) collective-permute-start(bf16[16,128,128]{2,1,0:T(8,128)(2,1)S(1)} %all_to_all.50), channel_id=1, source_target_pairs={{0,1},{1,0},{2,3},{3,2},{4,5},{5,4},{6,7},{7,6},{8,9},{9,8},{10,11... | collective-permute-start | bytes 1572872 | tf_op jit(solution)/shard_map/ppermute | solution.py:153
  95.8 1.5 collective-permute-done.1
  97.4 0.1 pad_maximum_fusion
  97.5 4.7 %fusion = bf16[16,8,8,128]{3,2,1,0:T(8,128)(2,1)S(1)} fusion(bf16[4096,128]{1,0:T(8,128)(2,1)S(1)} %bitcast.52, bf16[4096,1024]{1,0:T(8,128)(2,1)} %param.3), kind=kOutput, calls=%fused_computation.4 | convolution fusion | flops 1073872896 | bytes 9699328 | tf_op jit(solution)/shard_map/dot_general | solution.py:167
  102.3 14.9 %all_to_all.51 = bf16[8,128,128]{1,2,0:T(8,128)(2,1)S(1)} all-to-all(bf16[8,128,128]{1,2,0:T(8,128)(2,1)S(1)} %bitcast.53), channel_id=1, replica_groups=mesh['row'=8,'x'=4,'y'=4,'core'=2] {'row'}, dimensions={0} | all-to-all | bytes 524288 | tf_op jit(solution)/shard_map/all_to_all | solution.py:144
  117.2 0.1 copy.15
  117.4 14.6 %all_to_all.52 = bf16[8,128,128]{2,1,0:T(8,128)(2,1)S(1)} all-to-all(bf16[8,128,128]{2,1,0:T(8,128)(2,1)S(1)} %broadcast_in_dim.10), channel_id=1, replica_groups=mesh['row'=8,'x'=4,'y'=4,'core'=2] {'row'}, dimensions={0} | all-to-all | bytes 524288 | tf_op jit(solution)/shard_map/all_to_all | solution.py:149
  132.1 7.7 %convolution_bitcast_fusion = f32[4096,128]{0,1:T(8,128)} fusion(bf16[1024,128]{1,0:T(8,128)(2,1)S(1)} %bitcast.55, bf16[4096,1024]{1,0:T(8,128)(2,1)} %param.3), kind=kOutput, calls=%fused_computation | convolution fusion | flops 1073741824 | bytes 10747904 | tf_op jit(solution)/shard_map/dot_general | solution.py:176
  139.7 3.0 %reshape.54 = f32[16,2,128,128]{2,1,0,3:T(2,128)S(1)} reshape(f32[4096,128]{0,1:T(8,128)} %convolution_bitcast_fusion) | data formatting | bytes 4194304 | tf_op jit(solution)/shard_map/reshape | solution.py:177
  142.8 1.1 constant_dynamic-slice_fusion
  143.8 1.9 copy.20
  145.7 0.6 collective-permute-start.2
  146.3 1.1 constant_dynamic-slice_fusion.1
  147.4 0.7 copy.16
  148.2 1.2 fusion.1
  149.4 13.3 %all_to_all.53 = bf16[16,128,128]{2,1,0:T(8,128)(2,1)S(1)} all-to-all(bf16[16,128,128]{2,1,0:T(8,128)(2,1)S(1)} %fusion.1), channel_id=1, replica_groups=mesh['row'=8,'x'=4,'y'=4,'core'=2] {'x','y'}, dimensions={0} | all-to-all | bytes 1048576 | tf_op jit(solution)/shard_map/all_to_all | solution.py:144
  162.7 0.1 convert_reduce_fusion
  162.8 0.9 multiply_subtract_fusion.block_ref
  163.6 0.1 broadcast_in_dim.11
  163.7 18.4 %all_to_all.54 = f32[16,128,128]{2,1,0:T(8,128)S(1)} all-to-all(f32[16,128,128]{2,1,0:T(8,128)S(1)} %broadcast_in_dim.11), channel_id=1, replica_groups=mesh['row'=8,'x'=4,'y'=4,'core'=2] {'x','y'}, dimensions={0} | all-to-all | bytes 2097152 | tf_op jit(solution)/shard_map/all_to_all | solution.py:149
  182.1 3.2 %collective-permute-start.3 = (f32[16,128,128]{2,1,0:T(8,128)S(1)}, f32[16,128,128]{2,1,0:T(8,128)S(1)}, u32[]{:S(2)}, u32[]{:S(2)}) collective-permute-start(f32[16,128,128]{2,1,0:T(8,128)S(1)} %all_to_all.54), channel_id=1, source_target_pairs={{0,1},{1,0},{2,3},{3,2},{4,5},{5,4},{6,7},{7,6},{8,9},{9,8},{10,11... | collective-permute-start | bytes 3145736 | tf_op jit(solution)/shard_map/ppermute | solution.py:153
  185.3 2.3 collective-permute-done.3
  187.6 1.5 broadcast_select_fusion
  189.1 4.3 %shard_map.50 = f32[8,72,128]{2,1,0:T(8,128)} custom-call(f32[2048,128]{1,0:T(8,128)} %bitcast.50, f32[2048,128]{1,0:T(8,128)} %bitcast.48), custom_call_target="tpu_custom_call" | custom-call | tf_op jit(solution)/shard_map/pallas_call | solution.py:127
  193.4 16.7 %all_to_all.55.parts_ref = f32[8,72,128]{2,1,0:T(8,128)} all-to-all(f32[8,72,128]{2,1,0:T(8,128)} %shard_map.50), channel_id=1, replica_groups=mesh['row'=8,'x'=4,'y'=4,'core'=2] {'row'}, dimensions={0} | all-to-all | bytes 589824 | tf_op jit(solution)/shard_map/all_to_all | solution.py:200
  210.2 9.8 %shard_map.51 = (f32[8,72,128]{2,1,0:T(8,128)}, f32[128,128]{1,0:T(8,128)}, f32[128,128]{1,0:T(8,128)}) custom-call(f32[8,72,128]{2,1,0:T(8,128)} %all_to_all.55.parts_ref, f32[2048,128]{1,0:T(8,128)} %bitcast.51, f32[2048,128]{1,0:T(8,128)} %bitcast.49), custom_call_target="tpu_custom_call" | custom-call | tf_op jit(solution)/shard_map/pallas_call | solution.py:132
  220.0 15.2 %all_to_all.56.parts_ref = f32[8,72,128]{2,1,0:T(8,128)} all-to-all(f32[8,72,128]{2,1,0:T(8,128)} %get-tuple-element.5), channel_id=1, replica_groups=mesh['row'=8,'x'=4,'y'=4,'core'=2] {'row'}, dimensions={0} | all-to-all | bytes 589824 | tf_op jit(solution)/shard_map/all_to_all | solution.py:200
  235.1 5.7 %shard_map.52 = (f32[128,128]{1,0:T(8,128)}, f32[128,128]{1,0:T(8,128)}) custom-call(f32[8,72,128]{2,1,0:T(8,128)} %all_to_all.56.parts_ref, f32[128,128]{1,0:T(8,128)} %get-tuple-element.6.upper_one_ref, f32[128,128]{1,0:T(8,128)} %get-tuple-element.7.inverse_one_ref, f32[128,128]{1,0:T(8,128)} %copy-done), custom_call_target="tpu_custom_call" | custom-call | tf_op jit(solution)/shard_map/pallas_call | solution.py:136
  (11 shorter events, 0.3 us)
Async XLA Ops:
  7.7 19.4 %all-to-all-start = ((bf16[8,128,128]{2,1,0:T(8,128)(2,1)}), bf16[8,128,128]{2,1,0:T(8,128)(2,1)S(1)}, u32[]{:S(2)}, u32[]{:S(2)}) async-start(bf16[8,128,128]{2,1,0:T(8,128)(2,1)} %bitcast.1), calls=%async_computation | async-start | bytes 524288 | tf_op jit(solution)/shard_map/all_to_all | solution.py:144
  27.9 12.8 %all-to-all-start.1 = ((bf16[8,128,128]{2,1,0:T(8,128)(2,1)}), bf16[8,128,128]{2,1,0:T(8,128)(2,1)S(1)}, u32[]{:S(2)}, u32[]{:S(2)}) async-start(bf16[8,128,128]{2,1,0:T(8,128)(2,1)} %broadcast_in_dim.8), calls=%async_computation.1 | async-start | bytes 524288 | tf_op jit(solution)/shard_map/all_to_all | solution.py:149
  54.3 5.4 %collective-permute-start = (bf16[16,128,128]{2,1,0:T(8,128)(2,1)}, bf16[16,128,128]{2,1,0:T(8,128)(2,1)}, u32[]{:S(2)}, u32[]{:S(2)}) collective-permute-start(bf16[16,128,128]{2,1,0:T(8,128)(2,1)} %bitcast.56), channel_id=1, source_target_pairs={{0,1},{1,0},{2,3},{3,2},{4,5},{5,4},{6,7},{7,6},{8,9},{9,8},{10,11... | collective-permute-start | bytes 1572872 | tf_op jit(solution)/shard_map/ppermute | solution.py:153
  61.6 17.1 %all-to-all-start.2 = ((bf16[16,128,128]{2,1,0:T(8,128)(2,1)}), bf16[16,128,128]{2,1,0:T(8,128)(2,1)S(1)}, u32[]{:S(2)}, u32[]{:S(2)}) async-start(bf16[16,128,128]{2,1,0:T(8,128)(2,1)} %fusion.2), calls=%async_computation.2 | async-start | bytes 1048576 | tf_op jit(solution)/shard_map/all_to_all | solution.py:144
  92.5 4.8 %collective-permute-start.1 = (bf16[16,128,128]{2,1,0:T(8,128)(2,1)S(1)}, bf16[16,128,128]{2,1,0:T(8,128)(2,1)S(1)}, u32[]{:S(2)}, u32[]{:S(2)}) collective-permute-start(bf16[16,128,128]{2,1,0:T(8,128)(2,1)S(1)} %all_to_all.50), channel_id=1, source_target_pairs={{0,1},{1,0},{2,3},{3,2},{4,5},{5,4},{6,7},{7,6},{8,9},{9,8},{10,11... | collective-permute-start | bytes 1572872 | tf_op jit(solution)/shard_map/ppermute | solution.py:153
  145.7 2.5 %collective-permute-start.2 = (bf16[16,128,128]{2,1,0:T(8,128)(2,1)}, bf16[16,128,128]{2,1,0:T(8,128)(2,1)}, u32[]{:S(2)}, u32[]{:S(2)}) collective-permute-start(bf16[16,128,128]{2,1,0:T(8,128)(2,1)} %bitcast.57), channel_id=1, source_target_pairs={{0,1},{1,0},{2,3},{3,2},{4,5},{5,4},{6,7},{7,6},{8,9},{9,8},{10,11... | collective-permute-start | bytes 1572872 | tf_op jit(solution)/shard_map/ppermute | solution.py:153
  163.6 25.5 %copy-start = (f32[128,128]{1,0:T(8,128)}, f32[128,128]{1,0:T(8,128)S(1)}, u32[]{:S(2)}) copy-start(f32[128,128]{1,0:T(8,128)S(1)} %multiply_subtract_fusion.block_ref) | copy-start | bytes 196612
  182.1 5.5 %collective-permute-start.3 = (f32[16,128,128]{2,1,0:T(8,128)S(1)}, f32[16,128,128]{2,1,0:T(8,128)S(1)}, u32[]{:S(2)}, u32[]{:S(2)}) collective-permute-start(f32[16,128,128]{2,1,0:T(8,128)S(1)} %all_to_all.54), channel_id=1, source_target_pairs={{0,1},{1,0},{2,3},{3,2},{4,5},{5,4},{6,7},{7,6},{8,9},{9,8},{10,11... | collective-permute-start | bytes 3145736 | tf_op jit(solution)/shard_map/ppermute | solution.py:153

commit v3 on v2

v3 whole, which is shorter than its diff:
```python
import functools
import math

import jax
import jax.numpy as jnp
from jax import lax
from jax.experimental import pallas as pl
from jax.experimental.pallas import tpu as pltpu
from jax.sharding import PartitionSpec as P

N = 32768
K = 128
HALF = K // 2
PACK = HALF + 8
PANEL = 8
HIGHEST = lax.Precision.HIGHEST
VMEM_LIMIT = 24 * 2**20
COLUMNS = 256
CHUNKS = 4
PLANE = ("x", "y")


def local_call(kernel, out_types, *args, name, out_space=pltpu.VMEM, scratch_shapes=()):
    vmem = pl.BlockSpec(memory_space=pltpu.VMEM)
    return pl.pallas_call(
        kernel,
        in_specs=[vmem] * len(args),
        out_specs=[vmem] * len(out_types),
        out_shape=[out_space(*out_type) for out_type in out_types],
        scratch_shapes=list(scratch_shapes),
        compiler_params=pltpu.CompilerParams(vmem_limit_bytes=VMEM_LIMIT),
        name=name,
    )(*(pltpu.with_memory_space_constraint(arg, pltpu.VMEM) for arg in args))


def gram_of(block):
    return lax.dot_general(
        block, block, (((0,), (0,)), ((), ())), precision=HIGHEST, preferred_element_type=jnp.float32
    )


def times_transposed(block, matrix):
    return lax.dot_general(
        block, matrix, (((1,), (1,)), ((), ())), precision=HIGHEST, preferred_element_type=jnp.float32
    )


def factor(gram, upper_ref, inverse_ref):
    count = K // PANEL
    lane = lax.broadcasted_iota(jnp.int32, (PANEL, K), 1)
    sub = lax.broadcasted_iota(jnp.int32, (PANEL, K), 0)
    left = [gram[i * PANEL : (i + 1) * PANEL, :] for i in range(count)]
    right = [jnp.where(lane == sub + i * PANEL, 1.0, 0.0).astype(jnp.float32) for i in range(count)]
    for b in range(count):
        base = b * PANEL
        cols = [
            [
                jnp.broadcast_to(left[i][:, base + k : base + k + 1], (PANEL, K))
                for i in range(b, count)
            ]
            for k in range(PANEL)
        ]
        for k in range(PANEL):
            j = base + k
            root = lax.rsqrt(cols[k][0][k : k + 1, :])
            left_row = left[b][k : k + 1, :] * root
            right_row = right[b][k : k + 1, :] * root
            upper_ref[j : j + 1, :] = jnp.where(lane[:1] >= j, left_row, 0.0)
            inverse_ref[j : j + 1, :] = right_row
            left_row = left_row * root
            right_row = right_row * root
            heads = [cols[m][0][k : k + 1, :] * (root * root) for m in range(k + 1, PANEL)]
            for i in range(b, count):
                col = cols[k][i - b]
                if i == b:
                    if k == PANEL - 1:
                        continue
                    col = jnp.where(sub > k, col, 0.0)
                for m, head in zip(range(k + 1, PANEL), heads):
                    cols[m][i - b] = cols[m][i - b] - col * head
                left[i] = left[i] - col * left_row
                right[i] = right[i] - col * right_row


def grids():
    shape = (HALF, K)
    return lax.broadcasted_iota(jnp.int32, shape, 0), lax.broadcasted_iota(jnp.int32, shape, 1)


def pack(gram, out_ref):
    top, bottom = gram[:HALF], gram[HALF:]
    row, lane = grids()
    triangles = jnp.where(lane >= row, top, pltpu.roll(bottom, HALF, 1))
    diagonal = jnp.sum(jnp.where(lane == row + HALF, bottom, 0.0), axis=0, keepdims=True)
    for i in range(out_ref.shape[0]):
        out_ref[i, :HALF] = triangles
        out_ref[i, HALF:] = jnp.broadcast_to(diagonal, (PACK - HALF, K))


def sum_copies(parts_ref):
    total = parts_ref[0].astype(jnp.float32)
    for i in range(1, parts_ref.shape[0]):
        total = total + parts_ref[i].astype(jnp.float32)
    return total


def unpack_sum(parts_ref):
    packed = sum_copies(parts_ref)
    row, lane = grids()
    triangles, diagonal = packed[:HALF], packed[HALF : HALF + 1]
    last = pltpu.roll(jnp.where(lane < row, triangles, 0.0), HALF, 1)
    strict = jnp.concatenate([jnp.where(lane > row, triangles, 0.0), last], axis=0)
    middle = jnp.concatenate(
        [jnp.where(lane == row, triangles, 0.0), jnp.where(lane == row + HALF, diagonal, 0.0)], axis=0
    )
    return strict + strict.T + middle


def flat(value):
    return value.reshape(-1, value.shape[-1])


def contract_rows(left, right):
    return lax.dot_general(
        left, right, (((0,), (0,)), ((), ())), preferred_element_type=jnp.float32
    )


def store_row_blocks(product, first, out_ref):
    rows = out_ref.shape[1]
    for i in range(product.shape[1] // rows):
        block = product[:, i * rows : (i + 1) * rows]
        out_ref[first + i] = block.T.astype(out_ref.dtype)


def start_kernel(matrix_ref, start_ref, out_ref, own_ref):
    plane = lax.axis_index("x") * lax.axis_size("y") + lax.axis_index("y")
    own_ref[...] = start_ref[plane, lax.axis_index("core")]
    vectors = start_ref[...].astype(jnp.bfloat16).reshape(-1, K)
    for i in range(matrix_ref.shape[-1] // COLUMNS):
        piece = matrix_ref[:, :, :, i * COLUMNS : (i + 1) * COLUMNS].reshape(-1, COLUMNS)
        store_row_blocks(contract_rows(vectors, piece), i * COLUMNS // out_ref.shape[1], out_ref)


def even_kernel(matrix_ref, mine_ref, other_ref, out_ref):
    core = lax.axis_index("core")
    mine, other = flat(mine_ref[...]), flat(other_ref[...])
    for i in range(matrix_ref.shape[-1] // COLUMNS):
        lanes = slice(i * COLUMNS, (i + 1) * COLUMNS)
        product = contract_rows(mine, flat(matrix_ref[:, core, :, lanes]))
        product = product + contract_rows(other, flat(matrix_ref[:, 1 - core, :, lanes]))
        store_row_blocks(product, i * COLUMNS // out_ref.shape[1], out_ref)


def odd_kernel(offset, matrix_ref, vectors_ref, out_ref):
    core = lax.axis_index("core")
    which = core if offset == 0 else 1 - core
    vectors = flat(vectors_ref[...])
    for i in range(0, out_ref.shape[0], CHUNKS):
        rows = flat(matrix_ref[i : i + CHUNKS, which])
        product = jnp.dot(rows, vectors, preferred_element_type=jnp.float32)
        out_ref[i : i + CHUNKS] = product.reshape(CHUNKS, -1, K).astype(out_ref.dtype)


def pair_kernel(mine_ref, received_ref, out_ref):
    out_ref[...] = (mine_ref[...] + received_ref[...].astype(jnp.float32)).astype(out_ref.dtype)


def first_share_kernel(scale_ref, parts_ref, share_ref, copies_ref):
    total = sum_copies(parts_ref) * scale_ref[:1]
    share_ref[...] = total
    copies_ref[...] = jnp.broadcast_to(total.astype(copies_ref.dtype)[None], copies_ref.shape)


def next_share_kernel(scale_ref, parts_ref, previous_ref, share_ref, copies_ref):
    total = 2.0 * scale_ref[:1] * sum_copies(parts_ref) - previous_ref[...]
    share_ref[...] = total
    copies_ref[...] = jnp.broadcast_to(total.astype(copies_ref.dtype)[None], copies_ref.shape)


def first_gram_kernel(mine_ref, other_ref, out_ref):
    pack(gram_of(flat(mine_ref[...])) + gram_of(flat(other_ref[...])), out_ref)


def second_gram_kernel(parts_ref, mine_ref, other_ref, out_ref, upper_ref, inverse_ref):
    factor(unpack_sum(parts_ref), upper_ref, inverse_ref)
    inverse = inverse_ref[...]
    mine = times_transposed(flat(mine_ref[...]), inverse)
    other = times_transposed(flat(other_ref[...]), inverse)
    pack(gram_of(mine) + gram_of(other), out_ref)


def last_kernel(
    parts_ref, upper_one_ref, inverse_one_ref, block_ref, basis_ref, triangle_ref, upper_ref, inverse_ref
):
    factor(unpack_sum(parts_ref), upper_ref, inverse_ref)
    root = math.sqrt(N)
    first_basis = times_transposed(block_ref[...], inverse_one_ref[...])
    basis_ref[...] = times_transposed(first_basis, inverse_ref[...]) * root
    product = jnp.dot(
        upper_ref[...], upper_one_ref[...], precision=HIGHEST, preferred_element_type=jnp.float32
    )
    triangle_ref[...] = product / root


def swap_core(block):
    return lax.ppermute(block, "core", ((0, 1), (1, 0)))


def exchange(blocks, axes):
    return lax.all_to_all(blocks, axes, 0, 0, tiled=True)


def body(hamiltonian, start_block, spectral_bound):
    f32, bf16 = jnp.float32, jnp.bfloat16
    block_rows, block_cols = hamiltonian.shape
    row_count = lax.axis_size("row")
    plane_count = lax.axis_size("x") * lax.axis_size("y")
    share = block_rows // (2 * plane_count)
    col_share = block_cols // row_count
    scale = jnp.broadcast_to(1.0 / spectral_bound[0], (8, K))
    matrix = hamiltonian.reshape(plane_count, 2, share, block_cols)
    start = start_block.reshape(plane_count, 2, share, K)
    half = (plane_count, share, K)
    columns = (row_count, col_share, K)

    def odd_parts(vectors):
        kernels = [functools.partial(odd_kernel, offset) for offset in (0, 1)]
        (other,) = local_call(kernels[1], [(half, bf16)], matrix, vectors, name="odd_other")
        received = swap_core(other)
        (mine,) = local_call(kernels[0], [(half, f32)], matrix, vectors, name="odd_mine")
        (pair,) = local_call(pair_kernel, [(half, bf16)], mine, received, name="pair")
        return exchange(pair, PLANE)

    def next_share(parts, previous, dtype):
        types = [(previous.shape, f32), (parts.shape, dtype)]
        return local_call(next_share_kernel, types, scale, parts, previous, name="next_share")

    parts, zeroth = local_call(
        start_kernel, [(columns, bf16), ((share, K), f32)], matrix, start, name="start"
    )
    first, copies = local_call(
        first_share_kernel, [((col_share, K), f32), (columns, bf16)], scale, exchange(parts, "row"),
        name="first_share",
    )
    second, copies = next_share(odd_parts(exchange(copies, "row")), zeroth, bf16)
    mine = exchange(copies, PLANE)
    (parts,) = local_call(
        even_kernel, [(columns, bf16)], matrix, mine, swap_core(mine), name="even"
    )
    third, copies = next_share(exchange(parts, "row"), first, bf16)
    fourth, copies = next_share(odd_parts(exchange(copies, "row")), second, f32)

    mine = exchange(copies, PLANE)
    other = swap_core(mine)
    packed = ((row_count, PACK, K), f32)
    square = ((K, K), f32)
    (parts,) = local_call(first_gram_kernel, [packed], mine, other, name="first_gram")
    parts, upper, inverse = local_call(
        second_gram_kernel, [packed, square, square], exchange(parts, "row"), mine, other,
        name="second_gram",
    )
    return local_call(
        last_kernel, [((share, K), f32), square], exchange(parts, "row"), upper, inverse, fourth,
        name="last", out_space=jax.ShapeDtypeStruct, scratch_shapes=[pltpu.VMEM((K, K), f32)] * 2,
    )


def solution(mesh):
    rows = mesh.shape["row"]
    torus = jax.sharding.Mesh(mesh.devices.reshape(rows, 4, 4, 2), ("row", "x", "y", "core"))
    col = ("x", "y", "core")
    in_specs = (P("row", col), P("row", None), P())
    out_specs = (P(("row", *col), None), P())
    return jax.shard_map(
        body, mesh=torus, in_specs=in_specs, out_specs=out_specs, check_vma=False
    )
```

time: 242 us -> 199 us (0.82)
  matrix products: 27.1 us -> 0 us
  blocking collectives: 106 us -> 132 us
  waiting for transfers between devices: 33.3 us -> 14.1 us
  starting transfers between devices: 29.8 us -> 19.6 us
  local copies, waits for them, and re-layouts: 16.7 us -> 8.36 us
  other arithmetic: 6.78 us -> 0.01 us
  Pallas kernels: 19.8 us -> 23.7 us
    dot_general x4 -> x0, matrix products: 27.1 us -> none  [the longest x2 15.3 us: step_odd(): part = jnp.dot(hamiltonian, vectors, preferred_element_type=jnp.float32)]
    all_to_all x7 -> x9, blocking collectives: 106 us -> 132 us  [exchange(): return lax.all_to_all(blocks, axes, 0, 0, tiled=True)]
    all_to_all x3 -> x1, waiting for transfers between devices: 29.4 us -> 9.69 us  [exchange(): return lax.all_to_all(blocks, axes, 0, 0, tiled=True)]
    all_to_all x3 -> x1, starting transfers between devices: 19.2 us -> 9.01 us  [exchange(): return lax.all_to_all(blocks, axes, 0, 0, tiled=True)]
    reshape x3 -> x0, local copies, waits for them, and re-layouts: 6.1 us -> none  [the longest x2 6.06 us: step_odd(): part = part.reshape(plane_count, 2, share, K)]
    dynamic_slice x6 -> x0, local copies, waits for them, and re-layouts: 5.8 us -> none  [the longest x4 3.66 us: step_odd(): mine = lax.dynamic_index_in_dim(part, core, 1, False)]
    unnamed x4 -> x10, local copies, waits for them, and re-layouts: 3.78 us -> 8.36 us
    convert_element_type x5 -> x0, other arithmetic: 4.02 us -> none  [the longest x2 3.14 us: step_odd(): return scatter_sum(pair.astype(jnp.bfloat16), PLANE)]
  transfers between devices with their start and end apart: 7 -> 5, of which waited for: 5 -> 5; matrix products, arithmetic and copies ran while one was open for 2% -> 0% of each run, Pallas kernels for 0% -> 1%
where the time goes in v3:
time: 199 us
  blocking collectives  132 us (66%)
  Pallas kernels  23.7 us (12%)
  starting transfers between devices  19.6 us (10%)
  waiting for transfers between devices  14.1 us (7%)
  local copies, waits for them, and re-layouts  8.36 us (4%)
    all_to_all x9, blocking collectives, exchange(): return lax.all_to_all(blocks, axes, 0, 0, tiled=True)  132 us
    pallas_call x15, Pallas kernels, local_call(): pl.pallas_call(kernel, in_specs=[vmem] * len(args), out_specs=[vmem] * le...  23.7 us
    ppermute x4, starting transfers between devices, swap_core(): return lax.ppermute(block, 'core', ((0, 1), (1, 0)))  10.6 us
    all_to_all x1, waiting for transfers between devices, exchange(): return lax.all_to_all(blocks, axes, 0, 0, tiled=True)  9.69 us
    all_to_all x1, starting transfers between devices, exchange(): return lax.all_to_all(blocks, axes, 0, 0, tiled=True)  9.01 us
    unnamed x10, local copies, waits for them, and re-layouts  8.36 us
    ppermute x4, waiting for transfers between devices, swap_core(): return lax.ppermute(block, 'core', ((0, 1), (1, 0)))  4.41 us
  transfers between devices with their start and end apart: 5, of which 5 were waited for; matrix products, arithmetic and copies ran while one was open for 0% of the time, Pallas kernels for 1%

profile of v3, /device:TPU:1, one launch (start us, length us, event | category | flops | bytes accessed | tf_op | source)
XLA Modules:
  0.0 198.8 jit_solution(6306730327049112805)
XLA Ops:
  0.6 0.0 copy-start
  0.6 3.4 %copy-done = bf16[4096,1024]{1,0:T(8,128)(2,1)S(1)} copy-done((bf16[4096,1024]{1,0:T(8,128)(2,1)S(1)}, bf16[4096,1024]{1,0:T(8,128)(2,1)}, u32[]{:S(2)}) %copy-start) | copy-done | bytes 8388632
  4.0 0.0 copy-start.2
  4.0 1.6 copy-done.2
  5.6 2.1 %start.1 = (bf16[8,128,128]{2,1,0:T(8,128)(2,1)}, f32[128,128]{1,0:T(8,128)S(1)}) custom-call(bf16[16,2,128,1024]{3,2,1,0:T(8,128)(2,1)S(1)} %bitcast.3, f32[16,2,128,128]{3,2,1,0:T(8,128)S(1)} %bitcast.11), custom_call_target="tpu_custom_call" | custom-call | tf_op jit(solution)/shard_map/start/pallas_call | solution.py:25
  7.7 9.0 %all-to-all-start = ((bf16[8,128,128]{2,1,0:T(8,128)(2,1)}), bf16[8,128,128]{2,1,0:T(8,128)(2,1)S(1)}, u32[]{:S(2)}, u32[]{:S(2)}) async-start(bf16[8,128,128]{2,1,0:T(8,128)(2,1)} %get-tuple-element.14), calls=%async_computation | async-start | bytes 524288 | tf_op jit(solution)/shard_map/all_to_all | solution.py:211
  17.4 9.7 %all-to-all-done.parts_ref = bf16[8,128,128]{2,1,0:T(8,128)(2,1)S(1)} async-done(((bf16[8,128,128]{2,1,0:T(8,128)(2,1)}), bf16[8,128,128]{2,1,0:T(8,128)(2,1)S(1)}, u32[]{:S(2)}, u32[]{:S(2)}) %all-to-all-start) | async-done | bytes 262176 | tf_op jit(solution)/shard_map/all_to_all | solution.py:211
  27.1 12.0 %all_to_all.50.vectors_ref = bf16[8,128,128]{2,1,0:T(8,128)(2,1)S(1)} all-to-all(bf16[8,128,128]{2,1,0:T(8,128)(2,1)S(1)} %get-tuple-element.15), channel_id=1, replica_groups=mesh['row'=8,'x'=4,'y'=4,'core'=2] {'row'}, dimensions={0} | all-to-all | bytes 524288 | tf_op jit(solution)/shard_map/all_to_all | solution.py:211
  39.2 0.0 copy-start.1
  39.2 3.4 %copy-done.1 = bf16[4096,1024]{1,0:T(8,128)(2,1)S(1)} copy-done((bf16[4096,1024]{1,0:T(8,128)(2,1)S(1)}, bf16[4096,1024]{1,0:T(8,128)(2,1)}, u32[]{:S(2)}) %copy-start.1) | copy-done | bytes 8388632
  42.5 0.0 slice-start
  42.5 1.2 odd_other.2
  43.8 0.0 slice-start.1
  43.8 3.4 %collective-permute-start = (bf16[16,128,128]{2,1,0:T(8,128)(2,1)S(1)}, bf16[16,128,128]{2,1,0:T(8,128)(2,1)S(1)}, u32[]{:S(2)}, u32[]{:S(2)}) collective-permute-start(bf16[16,128,128]{2,1,0:T(8,128)(2,1)S(1)} %odd_other.2), channel_id=1, source_target_pairs={{0,1},{1,0},{2,3},{3,2},{4,5},{5,4},{6,7},{7,6},{8,9},{9,8},{10,11... | collective-permute-start | bytes 1572872 | tf_op jit(solution)/shard_map/ppermute | solution.py:207
  47.2 1.2 odd_mine.2.mine_ref
  48.5 0.3 collective-permute-done.received_ref
  48.8 0.1 pair.2
  48.9 16.9 %all_to_all.51.parts_ref = bf16[16,128,128]{2,1,0:T(8,128)(2,1)S(1)} all-to-all(bf16[16,128,128]{2,1,0:T(8,128)(2,1)S(1)} %pair.2), channel_id=1, replica_groups=mesh['row'=8,'x'=4,'y'=4,'core'=2] {'x','y'}, dimensions={0} | all-to-all | bytes 1048576 | tf_op jit(solution)/shard_map/all_to_all | solution.py:211
  65.8 0.1 next_share.3
  65.9 12.7 %all_to_all.52.mine_ref = bf16[16,128,128]{2,1,0:T(8,128)(2,1)S(1)} all-to-all(bf16[16,128,128]{2,1,0:T(8,128)(2,1)S(1)} %get-tuple-element.17), channel_id=1, replica_groups=mesh['row'=8,'x'=4,'y'=4,'core'=2] {'x','y'}, dimensions={0} | all-to-all | bytes 1048576 | tf_op jit(solution)/shard_map/all_to_all | solution.py:211
  78.6 3.3 %collective-permute-start.1 = (bf16[16,128,128]{2,1,0:T(8,128)(2,1)S(1)}, bf16[16,128,128]{2,1,0:T(8,128)(2,1)S(1)}, u32[]{:S(2)}, u32[]{:S(2)}) collective-permute-start(bf16[16,128,128]{2,1,0:T(8,128)(2,1)S(1)} %all_to_all.52.mine_ref), channel_id=1, source_target_pairs={{0,1},{1,0},{2,3},{3,2},{4,5},{5,4},{6,7},{7,6},{8,9},{9,8},{10,11... | collective-permute-start | bytes 1572872 | tf_op jit(solution)/shard_map/ppermute | solution.py:207
  81.9 1.5 collective-permute-done.1.other_ref
  83.4 0.0 slice-done
  83.4 0.0 slice-done.1
  83.4 1.4 even.1
  84.8 14.8 %all_to_all.53.parts_ref = bf16[8,128,128]{2,1,0:T(8,128)(2,1)S(1)} all-to-all(bf16[8,128,128]{2,1,0:T(8,128)(2,1)S(1)} %even.1), channel_id=1, replica_groups=mesh['row'=8,'x'=4,'y'=4,'core'=2] {'row'}, dimensions={0} | all-to-all | bytes 524288 | tf_op jit(solution)/shard_map/all_to_all | solution.py:211
  99.5 0.7 next_share.4
  100.2 14.6 %all_to_all.54.vectors_ref = bf16[8,128,128]{2,1,0:T(8,128)(2,1)S(1)} all-to-all(bf16[8,128,128]{2,1,0:T(8,128)(2,1)S(1)} %get-tuple-element.19), channel_id=1, replica_groups=mesh['row'=8,'x'=4,'y'=4,'core'=2] {'row'}, dimensions={0} | all-to-all | bytes 524288 | tf_op jit(solution)/shard_map/all_to_all | solution.py:211
  114.8 1.2 odd_other.3
  116.1 0.7 collective-permute-start.2
  116.8 1.2 odd_mine.3.mine_ref
  118.0 0.3 collective-permute-done.2.received_ref
  118.3 0.1 pair.3
  118.4 13.3 %all_to_all.55.parts_ref = bf16[16,128,128]{2,1,0:T(8,128)(2,1)S(1)} all-to-all(bf16[16,128,128]{2,1,0:T(8,128)(2,1)S(1)} %pair.3), channel_id=1, replica_groups=mesh['row'=8,'x'=4,'y'=4,'core'=2] {'x','y'}, dimensions={0} | all-to-all | bytes 1048576 | tf_op jit(solution)/shard_map/all_to_all | solution.py:211
  131.7 0.1 next_share.5
  131.9 18.4 %all_to_all.56.mine_ref = f32[16,128,128]{2,1,0:T(8,128)S(1)} all-to-all(f32[16,128,128]{2,1,0:T(8,128)S(1)} %get-tuple-element.21), channel_id=1, replica_groups=mesh['row'=8,'x'=4,'y'=4,'core'=2] {'x','y'}, dimensions={0} | all-to-all | bytes 2097152 | tf_op jit(solution)/shard_map/all_to_all | solution.py:211
  150.2 3.2 %collective-permute-start.3 = (f32[16,128,128]{2,1,0:T(8,128)S(1)}, f32[16,128,128]{2,1,0:T(8,128)S(1)}, u32[]{:S(2)}, u32[]{:S(2)}) collective-permute-start(f32[16,128,128]{2,1,0:T(8,128)S(1)} %all_to_all.56.mine_ref), channel_id=1, source_target_pairs={{0,1},{1,0},{2,3},{3,2},{4,5},{5,4},{6,7},{7,6},{8,9},{9,8},{10,11... | collective-permute-start | bytes 3145736 | tf_op jit(solution)/shard_map/ppermute | solution.py:207
  153.5 2.3 %collective-permute-done.3.other_ref = f32[16,128,128]{2,1,0:T(8,128)S(1)} collective-permute-done((f32[16,128,128]{2,1,0:T(8,128)S(1)}, f32[16,128,128]{2,1,0:T(8,128)S(1)}, u32[]{:S(2)}, u32[]{:S(2)}) %collective-permute-start.3) | collective-permute-done | bytes 1048608 | tf_op jit(solution)/shard_map/ppermute | solution.py:207
  155.7 2.1 %first_gram.1 = f32[8,72,128]{2,1,0:T(8,128)S(1)} custom-call(f32[16,128,128]{2,1,0:T(8,128)S(1)} %all_to_all.56.mine_ref, f32[16,128,128]{2,1,0:T(8,128)S(1)} %collective-permute-done.3.other_ref), custom_call_target="tpu_custom_call" | custom-call | tf_op jit(solution)/shard_map/first_gram/pallas_call | solution.py:25
  157.8 15.0 %all_to_all.57.parts_ref = f32[8,72,128]{2,1,0:T(8,128)S(1)} all-to-all(f32[8,72,128]{2,1,0:T(8,128)S(1)} %first_gram.1), channel_id=1, replica_groups=mesh['row'=8,'x'=4,'y'=4,'core'=2] {'row'}, dimensions={0} | all-to-all | bytes 589824 | tf_op jit(solution)/shard_map/all_to_all | solution.py:211
  172.9 7.5 %second_gram.1 = (f32[8,72,128]{2,1,0:T(8,128)S(1)}, f32[128,128]{1,0:T(8,128)S(1)}, f32[128,128]{1,0:T(8,128)S(1)}) custom-call(f32[8,72,128]{2,1,0:T(8,128)S(1)} %all_to_all.57.parts_ref, f32[16,128,128]{2,1,0:T(8,128)S(1)} %all_to_all.56.mine_ref, f32[16,128,128]{2,1,0:T(8,128)S(1)} %collective-permute-done.3.other_ref), custom_call_target="tpu_custom_call" | custom-call | tf_op jit(solution)/shard_map/second_gram/pallas_call | solution.py:25
  180.3 13.8 %all_to_all.58.parts_ref = f32[8,72,128]{2,1,0:T(8,128)S(1)} all-to-all(f32[8,72,128]{2,1,0:T(8,128)S(1)} %get-tuple-element.22), channel_id=1, replica_groups=mesh['row'=8,'x'=4,'y'=4,'core'=2] {'row'}, dimensions={0} | all-to-all | bytes 589824 | tf_op jit(solution)/shard_map/all_to_all | solution.py:211
  194.1 4.6 %last.1 = (f32[128,128]{1,0:T(8,128)}, f32[128,128]{1,0:T(8,128)}) custom-call(f32[8,72,128]{2,1,0:T(8,128)S(1)} %all_to_all.58.parts_ref, f32[128,128]{1,0:T(8,128)S(1)} %get-tuple-element.23.upper_one_ref, f32[128,128]{1,0:T(8,128)S(1)} %get-tuple-element.24.inverse_one_ref, f32[128,128]{1,0:T(8,128)S(1)} %get-tuple-element.25.block_ref), custom_call_target="tpu_custom_call" | custom-call | tf_op jit(solution)/shard_map/last/pallas_call | solution.py:25
  (3 shorter events, 0.0 us)
Async XLA Ops:
  0.6 3.4 %copy-start = (bf16[4096,1024]{1,0:T(8,128)(2,1)S(1)}, bf16[4096,1024]{1,0:T(8,128)(2,1)}, u32[]{:S(2)}) copy-start(bf16[4096,1024]{1,0:T(8,128)(2,1)} %param.3) | copy-start | bytes 25165828
  4.0 1.6 copy-start.2
  7.7 19.4 %all-to-all-start = ((bf16[8,128,128]{2,1,0:T(8,128)(2,1)}), bf16[8,128,128]{2,1,0:T(8,128)(2,1)S(1)}, u32[]{:S(2)}, u32[]{:S(2)}) async-start(bf16[8,128,128]{2,1,0:T(8,128)(2,1)} %get-tuple-element.14), calls=%async_computation | async-start | bytes 524288 | tf_op jit(solution)/shard_map/all_to_all | solution.py:211
  39.2 3.4 %copy-start.1 = (bf16[4096,1024]{1,0:T(8,128)(2,1)S(1)}, bf16[4096,1024]{1,0:T(8,128)(2,1)}, u32[]{:S(2)}) copy-start(bf16[4096,1024]{1,0:T(8,128)(2,1)} %param.3) | copy-start | bytes 25165828
  42.5 40.9 %slice-start = ((s8[8388608]{0:T(1024)(128)(4,1)}), s8[4194304]{0:T(1024)(128)(4,1)S(1)}, s32[]{:S(2)}) async-start(s8[8388608]{0:T(1024)(128)(4,1)} %bitcast.6), calls=%async_computation.10 | async-start | bytes 8388608
  43.8 39.6 %slice-start.1 = ((s8[8388608]{0:T(1024)(128)(4,1)}), s8[4194304]{0:T(1024)(128)(4,1)S(1)}, s32[]{:S(2)}) async-start(s8[8388608]{0:T(1024)(128)(4,1)} %bitcast.6), calls=%async_computation.11 | async-start | bytes 8388608
  43.8 5.0 %collective-permute-start = (bf16[16,128,128]{2,1,0:T(8,128)(2,1)S(1)}, bf16[16,128,128]{2,1,0:T(8,128)(2,1)S(1)}, u32[]{:S(2)}, u32[]{:S(2)}) collective-permute-start(bf16[16,128,128]{2,1,0:T(8,128)(2,1)S(1)} %odd_other.2), channel_id=1, source_target_pairs={{0,1},{1,0},{2,3},{3,2},{4,5},{5,4},{6,7},{7,6},{8,9},{9,8},{10,11... | collective-permute-start | bytes 1572872 | tf_op jit(solution)/shard_map/ppermute | solution.py:207
  78.6 4.8 %collective-permute-start.1 = (bf16[16,128,128]{2,1,0:T(8,128)(2,1)S(1)}, bf16[16,128,128]{2,1,0:T(8,128)(2,1)S(1)}, u32[]{:S(2)}, u32[]{:S(2)}) collective-permute-start(bf16[16,128,128]{2,1,0:T(8,128)(2,1)S(1)} %all_to_all.52.mine_ref), channel_id=1, source_target_pairs={{0,1},{1,0},{2,3},{3,2},{4,5},{5,4},{6,7},{7,6},{8,9},{9,8},{10,11... | collective-permute-start | bytes 1572872 | tf_op jit(solution)/shard_map/ppermute | solution.py:207
  116.1 2.2 %collective-permute-start.2 = (bf16[16,128,128]{2,1,0:T(8,128)(2,1)S(1)}, bf16[16,128,128]{2,1,0:T(8,128)(2,1)S(1)}, u32[]{:S(2)}, u32[]{:S(2)}) collective-permute-start(bf16[16,128,128]{2,1,0:T(8,128)(2,1)S(1)} %odd_other.3), channel_id=1, source_target_pairs={{0,1},{1,0},{2,3},{3,2},{4,5},{5,4},{6,7},{7,6},{8,9},{9,8},{10,11... | collective-permute-start | bytes 1572872 | tf_op jit(solution)/shard_map/ppermute | solution.py:207
  150.2 5.5 %collective-permute-start.3 = (f32[16,128,128]{2,1,0:T(8,128)S(1)}, f32[16,128,128]{2,1,0:T(8,128)S(1)}, u32[]{:S(2)}, u32[]{:S(2)}) collective-permute-start(f32[16,128,128]{2,1,0:T(8,128)S(1)} %all_to_all.56.mine_ref), channel_id=1, source_target_pairs={{0,1},{1,0},{2,3},{3,2},{4,5},{5,4},{6,7},{7,6},{8,9},{9,8},{10,11... | collective-permute-start | bytes 3145736 | tf_op jit(solution)/shard_map/ppermute | solution.py:207

commit v4 on v3

--- a/solution.py
+++ b/solution.py
@@ -17,20 +17,23 @@
 VMEM_LIMIT = 24 * 2**20
 COLUMNS = 256
 CHUNKS = 4
+PLANES = 2
 PLANE = ("x", "y")
 
 
-def local_call(kernel, out_types, *args, name, out_space=pltpu.VMEM, scratch_shapes=()):
+def local_call(
+    kernel, out_types, *args, name, in_space=pltpu.VMEM, out_space=pltpu.VMEM, scratch_shapes=()
+):
     vmem = pl.BlockSpec(memory_space=pltpu.VMEM)
     return pl.pallas_call(
         kernel,
-        in_specs=[vmem] * len(args),
+        in_specs=[pl.BlockSpec(memory_space=in_space)] * len(args),
         out_specs=[vmem] * len(out_types),
         out_shape=[out_space(*out_type) for out_type in out_types],
         scratch_shapes=list(scratch_shapes),
         compiler_params=pltpu.CompilerParams(vmem_limit_bytes=VMEM_LIMIT),
         name=name,
-    )(*(pltpu.with_memory_space_constraint(arg, pltpu.VMEM) for arg in args))
+    )(*(pltpu.with_memory_space_constraint(arg, in_space) for arg in args))
 
 
 def gram_of(block):
@@ -133,13 +136,29 @@
         out_ref[first + i] = block.T.astype(out_ref.dtype)
 
 
-def start_kernel(matrix_ref, start_ref, out_ref, own_ref):
+def start_kernel(
+    matrix_ref, start_ref, out_ref, own_ref, kept_ref, vectors_ref, total_ref, matrix_sems, start_sems
+):
+    pieces = []
+    for i in range(0, matrix_ref.shape[0], PLANES):
+        part, n = pl.ds(i, PLANES), i // PLANES
+        copies = (
+            pltpu.make_async_copy(start_ref.at[part], vectors_ref.at[part], start_sems.at[n]),
+            pltpu.make_async_copy(matrix_ref.at[part], kept_ref.at[part], matrix_sems.at[n]),
+        )
+        for copy in copies:
+            copy.start()
+        pieces.append(copies)
+    for n, copies in enumerate(pieces):
+        for copy in copies:
+            copy.wait()
+        part = slice(n * PLANES, (n + 1) * PLANES)
+        vectors = vectors_ref[part].astype(jnp.bfloat16).reshape(-1, K)
+        product = contract_rows(vectors, kept_ref[part].reshape(-1, kept_ref.shape[-1]))
+        total_ref[...] = product if n == 0 else total_ref[...] + product
+    store_row_blocks(total_ref[...], 0, out_ref)
     plane = lax.axis_index("x") * lax.axis_size("y") + lax.axis_index("y")
-    own_ref[...] = start_ref[plane, lax.axis_index("core")]
-    vectors = start_ref[...].astype(jnp.bfloat16).reshape(-1, K)
-    for i in range(matrix_ref.shape[-1] // COLUMNS):
-        piece = matrix_ref[:, :, :, i * COLUMNS : (i + 1) * COLUMNS].reshape(-1, COLUMNS)
-        store_row_blocks(contract_rows(vectors, piece), i * COLUMNS // out_ref.shape[1], out_ref)
+    own_ref[...] = vectors_ref[plane, lax.axis_index("core")]
 
 
 def even_kernel(matrix_ref, mine_ref, other_ref, out_ref):
@@ -172,21 +191,36 @@
     copies_ref[...] = jnp.broadcast_to(total.astype(copies_ref.dtype)[None], copies_ref.shape)
 
 
-def next_share_kernel(scale_ref, parts_ref, previous_ref, share_ref, copies_ref):
+def next_share_kernel(scale_ref, parts_ref, previous_ref, *out_refs):
     total = 2.0 * scale_ref[:1] * sum_copies(parts_ref) - previous_ref[...]
-    share_ref[...] = total
+    copies_ref = out_refs[-1]
     copies_ref[...] = jnp.broadcast_to(total.astype(copies_ref.dtype)[None], copies_ref.shape)
+    if len(out_refs) == 2:
+        out_refs[0][...] = total
+
+
+def times_inverse(block, inverse):
+    total = None
+    for _ in range(3):
+        term = inverse.astype(jnp.bfloat16)
+        inverse = inverse - term.astype(jnp.float32)
+        product = lax.dot_general(
+            block, term, (((1,), (1,)), ((), ())), preferred_element_type=jnp.float32
+        )
+        total = product if total is None else total + product
+    return total
 
 
 def first_gram_kernel(mine_ref, other_ref, out_ref):
-    pack(gram_of(flat(mine_ref[...])) + gram_of(flat(other_ref[...])), out_ref)
+    mine, other = flat(mine_ref[...]), flat(other_ref[...])
+    pack(contract_rows(mine, mine) + contract_rows(other, other), out_ref)
 
 
 def second_gram_kernel(parts_ref, mine_ref, other_ref, out_ref, upper_ref, inverse_ref):
     factor(unpack_sum(parts_ref), upper_ref, inverse_ref)
     inverse = inverse_ref[...]
-    mine = times_transposed(flat(mine_ref[...]), inverse)
-    other = times_transposed(flat(other_ref[...]), inverse)
+    mine = times_inverse(flat(mine_ref[...]), inverse)
+    other = times_inverse(flat(other_ref[...]), inverse)
     pack(gram_of(mine) + gram_of(other), out_ref)
 
 
@@ -195,7 +229,7 @@
 ):
     factor(unpack_sum(parts_ref), upper_ref, inverse_ref)
     root = math.sqrt(N)
-    first_basis = times_transposed(block_ref[...], inverse_one_ref[...])
+    first_basis = times_inverse(block_ref[0], inverse_one_ref[...])
     basis_ref[...] = times_transposed(first_basis, inverse_ref[...]) * root
     product = jnp.dot(
         upper_ref[...], upper_one_ref[...], precision=HIGHEST, preferred_element_type=jnp.float32
@@ -232,24 +266,29 @@
         (pair,) = local_call(pair_kernel, [(half, bf16)], mine, received, name="pair")
         return exchange(pair, PLANE)
 
-    def next_share(parts, previous, dtype):
-        types = [(previous.shape, f32), (parts.shape, dtype)]
+    def next_share(parts, previous, keep):
+        types = [(previous.shape, f32)] * keep + [(parts.shape, bf16)]
         return local_call(next_share_kernel, types, scale, parts, previous, name="next_share")
 
-    parts, zeroth = local_call(
-        start_kernel, [(columns, bf16), ((share, K), f32)], matrix, start, name="start"
+    pieces = plane_count // PLANES
+    parts, zeroth, matrix = local_call(
+        start_kernel, [(columns, bf16), ((share, K), f32), (matrix.shape, bf16)], matrix, start,
+        name="start", in_space=pltpu.HBM, scratch_shapes=[
+            pltpu.VMEM(start.shape, f32), pltpu.VMEM((K, block_cols), f32),
+            pltpu.SemaphoreType.DMA((pieces,)), pltpu.SemaphoreType.DMA((pieces,)),
+        ],
     )
     first, copies = local_call(
         first_share_kernel, [((col_share, K), f32), (columns, bf16)], scale, exchange(parts, "row"),
         name="first_share",
     )
-    second, copies = next_share(odd_parts(exchange(copies, "row")), zeroth, bf16)
+    second, copies = next_share(odd_parts(exchange(copies, "row")), zeroth, True)
     mine = exchange(copies, PLANE)
     (parts,) = local_call(
         even_kernel, [(columns, bf16)], matrix, mine, swap_core(mine), name="even"
     )
-    third, copies = next_share(exchange(parts, "row"), first, bf16)
-    fourth, copies = next_share(odd_parts(exchange(copies, "row")), second, f32)
+    (copies,) = next_share(exchange(parts, "row"), first, False)
+    (copies,) = next_share(odd_parts(exchange(copies, "row")), second, False)
 
     mine = exchange(copies, PLANE)
     other = swap_core(mine)
@@ -261,7 +300,7 @@
         name="second_gram",
     )
     return local_call(
-        last_kernel, [((share, K), f32), square], exchange(parts, "row"), upper, inverse, fourth,
+        last_kernel, [((share, K), f32), square], exchange(parts, "row"), upper, inverse, copies,
         name="last", out_space=jax.ShapeDtypeStruct, scratch_shapes=[pltpu.VMEM((K, K), f32)] * 2,
     )
 

time: 199 us -> 191 us (0.960)
  blocking collectives: 132 us -> 126 us
    all_to_all x9, blocking collectives: 132 us -> 126 us  [exchange(): return lax.all_to_all(blocks, axes, 0, 0, tiled=True)]
    unnamed x10 -> x8, local copies, waits for them, and re-layouts: 8.36 us -> 6.6 us
where the time goes in v4:
time: 191 us; the launch traced here: 190 us
  blocking collectives  126 us (66%)
  Pallas kernels  23.8 us (12%)
  starting transfers between devices  19.7 us (10%)
  waiting for transfers between devices  13.3 us (7%)
  local copies, waits for them, and re-layouts  6.6 us (3%)
    all_to_all x9, blocking collectives, exchange(): return lax.all_to_all(blocks, axes, 0, 0, tiled=True)  126 us
    pallas_call x15, Pallas kernels, local_call(): pl.pallas_call(kernel, in_specs=[pl.BlockSpec(memory_space=in_space)] * l...  23.8 us
    ppermute x4, starting transfers between devices, swap_core(): return lax.ppermute(block, 'core', ((0, 1), (1, 0)))  10.6 us
    all_to_all x1, waiting for transfers between devices, exchange(): return lax.all_to_all(blocks, axes, 0, 0, tiled=True)  9.66 us
    all_to_all x1, starting transfers between devices, exchange(): return lax.all_to_all(blocks, axes, 0, 0, tiled=True)  9.01 us
    unnamed x8, local copies, waits for them, and re-layouts  6.6 us
  transfers between devices with their start and end apart: 5, of which 5 were waited for; matrix products, arithmetic and copies ran while one was open for 0% of the time, Pallas kernels for 1%

profile of v4, /device:TPU:1, one launch (start us, length us, event | category | flops | bytes accessed | tf_op | source)
XLA Modules:
  0.0 190.4 jit_solution(15432697834426115422)
XLA Ops:
  0.6 5.3 %start.1 = (bf16[8,128,128]{2,1,0:T(8,128)(2,1)}, f32[128,128]{1,0:T(8,128)S(1)}, bf16[16,2,128,1024]{3,2,1,0:T(8,128)(2,1)S(1)}) custom-call(bf16[16,2,128,1024]{3,2,1,0:T(8,128)(2,1)} %bitcast.5, f32[16,2,128,128]{3,2,1,0:T(8,128)} %bitcast.6), custom_call_target="tpu_custom_call" | custom-call | tf_op jit(solution)/shard_map/start/pallas_call | solution.py:28
  5.9 0.0 copy-start
  5.9 3.2 %copy-done = bf16[16,2,128,1024]{3,2,1,0:T(8,128)(2,1)} copy-done((bf16[16,2,128,1024]{3,2,1,0:T(8,128)(2,1)}, bf16[16,2,128,1024]{3,2,1,0:T(8,128)(2,1)S(1)}, u32[]{:S(2)}) %copy-start) | copy-done | bytes 8388632
  9.1 9.0 %all-to-all-start = ((bf16[8,128,128]{2,1,0:T(8,128)(2,1)}), bf16[8,128,128]{2,1,0:T(8,128)(2,1)S(1)}, u32[]{:S(2)}, u32[]{:S(2)}) async-start(bf16[8,128,128]{2,1,0:T(8,128)(2,1)} %get-tuple-element.13), calls=%async_computation | async-start | bytes 524288 | tf_op jit(solution)/shard_map/all_to_all | solution.py:245
  18.8 9.7 %all-to-all-done.parts_ref = bf16[8,128,128]{2,1,0:T(8,128)(2,1)S(1)} async-done(((bf16[8,128,128]{2,1,0:T(8,128)(2,1)}), bf16[8,128,128]{2,1,0:T(8,128)(2,1)S(1)}, u32[]{:S(2)}, u32[]{:S(2)}) %all-to-all-start) | async-done | bytes 262176 | tf_op jit(solution)/shard_map/all_to_all | solution.py:245
  28.5 12.0 %all_to_all.50.vectors_ref = bf16[8,128,128]{2,1,0:T(8,128)(2,1)S(1)} all-to-all(bf16[8,128,128]{2,1,0:T(8,128)(2,1)S(1)} %get-tuple-element.14), channel_id=1, replica_groups=mesh['row'=8,'x'=4,'y'=4,'core'=2] {'row'}, dimensions={0} | all-to-all | bytes 524288 | tf_op jit(solution)/shard_map/all_to_all | solution.py:245
  40.6 0.0 copy-start.1
  40.6 3.4 %copy-done.1 = bf16[16,2,128,1024]{3,2,1,0:T(8,128)(2,1)S(1)} copy-done((bf16[16,2,128,1024]{3,2,1,0:T(8,128)(2,1)S(1)}, bf16[16,2,128,1024]{3,2,1,0:T(8,128)(2,1)}, u32[]{:S(2)}) %copy-start.1) | copy-done | bytes 8388632
  44.0 0.0 slice-start
  44.0 1.2 odd_other.2
  45.2 0.0 slice-start.1
  45.2 3.5 %collective-permute-start = (bf16[16,128,128]{2,1,0:T(8,128)(2,1)S(1)}, bf16[16,128,128]{2,1,0:T(8,128)(2,1)S(1)}, u32[]{:S(2)}, u32[]{:S(2)}) collective-permute-start(bf16[16,128,128]{2,1,0:T(8,128)(2,1)S(1)} %odd_other.2), channel_id=1, source_target_pairs={{0,1},{1,0},{2,3},{3,2},{4,5},{5,4},{6,7},{7,6},{8,9},{9,8},{10,11... | collective-permute-start | bytes 1572872 | tf_op jit(solution)/shard_map/ppermute | solution.py:241
  48.7 1.2 odd_mine.2.mine_ref
  49.9 0.3 collective-permute-done.received_ref
  50.2 0.1 pair.2
  50.3 16.9 %all_to_all.51.parts_ref = bf16[16,128,128]{2,1,0:T(8,128)(2,1)S(1)} all-to-all(bf16[16,128,128]{2,1,0:T(8,128)(2,1)S(1)} %pair.2), channel_id=1, replica_groups=mesh['row'=8,'x'=4,'y'=4,'core'=2] {'x','y'}, dimensions={0} | all-to-all | bytes 1048576 | tf_op jit(solution)/shard_map/all_to_all | solution.py:245
  67.2 0.1 next_share.3
  67.3 12.7 %all_to_all.52.mine_ref = bf16[16,128,128]{2,1,0:T(8,128)(2,1)S(1)} all-to-all(bf16[16,128,128]{2,1,0:T(8,128)(2,1)S(1)} %get-tuple-element.16), channel_id=1, replica_groups=mesh['row'=8,'x'=4,'y'=4,'core'=2] {'x','y'}, dimensions={0} | all-to-all | bytes 1048576 | tf_op jit(solution)/shard_map/all_to_all | solution.py:245
  80.0 3.3 %collective-permute-start.1 = (bf16[16,128,128]{2,1,0:T(8,128)(2,1)S(1)}, bf16[16,128,128]{2,1,0:T(8,128)(2,1)S(1)}, u32[]{:S(2)}, u32[]{:S(2)}) collective-permute-start(bf16[16,128,128]{2,1,0:T(8,128)(2,1)S(1)} %all_to_all.52.mine_ref), channel_id=1, source_target_pairs={{0,1},{1,0},{2,3},{3,2},{4,5},{5,4},{6,7},{7,6},{8,9},{9,8},{10,11... | collective-permute-start | bytes 1572872 | tf_op jit(solution)/shard_map/ppermute | solution.py:241
  83.3 1.5 collective-permute-done.1.other_ref
  84.8 0.0 slice-done
  84.8 0.0 slice-done.1
  84.8 1.4 even.1
  86.2 14.8 %all_to_all.53.parts_ref = bf16[8,128,128]{2,1,0:T(8,128)(2,1)S(1)} all-to-all(bf16[8,128,128]{2,1,0:T(8,128)(2,1)S(1)} %even.1), channel_id=1, replica_groups=mesh['row'=8,'x'=4,'y'=4,'core'=2] {'row'}, dimensions={0} | all-to-all | bytes 524288 | tf_op jit(solution)/shard_map/all_to_all | solution.py:245
  101.0 14.6 %all_to_all.54.vectors_ref = bf16[8,128,128]{2,1,0:T(8,128)(2,1)S(1)} all-to-all(bf16[8,128,128]{2,1,0:T(8,128)(2,1)S(1)} %next_share.4), channel_id=1, replica_groups=mesh['row'=8,'x'=4,'y'=4,'core'=2] {'row'}, dimensions={0} | all-to-all | bytes 524288 | tf_op jit(solution)/shard_map/all_to_all | solution.py:245
  115.6 1.2 odd_other.3
  116.9 0.7 collective-permute-start.2
  117.6 1.2 odd_mine.3.mine_ref
  118.8 0.3 collective-permute-done.2.received_ref
  119.1 0.1 pair.3
  119.2 13.3 %all_to_all.55.parts_ref = bf16[16,128,128]{2,1,0:T(8,128)(2,1)S(1)} all-to-all(bf16[16,128,128]{2,1,0:T(8,128)(2,1)S(1)} %pair.3), channel_id=1, replica_groups=mesh['row'=8,'x'=4,'y'=4,'core'=2] {'x','y'}, dimensions={0} | all-to-all | bytes 1048576 | tf_op jit(solution)/shard_map/all_to_all | solution.py:245
  132.5 0.1 next_share.5.block_ref
  132.6 12.7 %all_to_all.56.mine_ref = bf16[16,128,128]{2,1,0:T(8,128)(2,1)S(1)} all-to-all(bf16[16,128,128]{2,1,0:T(8,128)(2,1)S(1)} %next_share.5.block_ref), channel_id=1, replica_groups=mesh['row'=8,'x'=4,'y'=4,'core'=2] {'x','y'}, dimensions={0} | all-to-all | bytes 1048576 | tf_op jit(solution)/shard_map/all_to_all | solution.py:245
  145.4 3.3 %collective-permute-start.3 = (bf16[16,128,128]{2,1,0:T(8,128)(2,1)S(1)}, bf16[16,128,128]{2,1,0:T(8,128)(2,1)S(1)}, u32[]{:S(2)}, u32[]{:S(2)}) collective-permute-start(bf16[16,128,128]{2,1,0:T(8,128)(2,1)S(1)} %all_to_all.56.mine_ref), channel_id=1, source_target_pairs={{0,1},{1,0},{2,3},{3,2},{4,5},{5,4},{6,7},{7,6},{8,9},{9,8},{10,11... | collective-permute-start | bytes 1572872 | tf_op jit(solution)/shard_map/ppermute | solution.py:241
  148.6 1.5 collective-permute-done.3.other_ref
  150.1 0.5 first_gram.1
  150.7 15.0 %all_to_all.57.parts_ref = f32[8,72,128]{2,1,0:T(8,128)S(1)} all-to-all(f32[8,72,128]{2,1,0:T(8,128)S(1)} %first_gram.1), channel_id=1, replica_groups=mesh['row'=8,'x'=4,'y'=4,'core'=2] {'row'}, dimensions={0} | all-to-all | bytes 589824 | tf_op jit(solution)/shard_map/all_to_all | solution.py:245
  165.7 6.6 %second_gram.1 = (f32[8,72,128]{2,1,0:T(8,128)S(1)}, f32[128,128]{1,0:T(8,128)S(1)}, f32[128,128]{1,0:T(8,128)S(1)}) custom-call(f32[8,72,128]{2,1,0:T(8,128)S(1)} %all_to_all.57.parts_ref, bf16[16,128,128]{2,1,0:T(8,128)(2,1)S(1)} %all_to_all.56.mine_ref, bf16[16,128,128]{2,1,0:T(8,128)(2,1)S(1)} %collective-permute-done.3.other_ref), custom_call_target="tpu_custom_call" | custom-call | tf_op jit(solution)/shard_map/second_gram/pallas_call | solution.py:28
  172.3 13.4 %all_to_all.58.parts_ref = f32[8,72,128]{2,1,0:T(8,128)S(1)} all-to-all(f32[8,72,128]{2,1,0:T(8,128)S(1)} %get-tuple-element.19), channel_id=1, replica_groups=mesh['row'=8,'x'=4,'y'=4,'core'=2] {'row'}, dimensions={0} | all-to-all | bytes 589824 | tf_op jit(solution)/shard_map/all_to_all | solution.py:245
  185.7 4.6 %last.1 = (f32[128,128]{1,0:T(8,128)}, f32[128,128]{1,0:T(8,128)}) custom-call(f32[8,72,128]{2,1,0:T(8,128)S(1)} %all_to_all.58.parts_ref, f32[128,128]{1,0:T(8,128)S(1)} %get-tuple-element.20.upper_one_ref, f32[128,128]{1,0:T(8,128)S(1)} %get-tuple-element.21.inverse_one_ref, bf16[16,128,128]{2,1,0:T(8,128)(2,1)S(1)} %next_share.5.block_ref), custom_call_target="tpu_custom_call" | custom-call | tf_op jit(solution)/shard_map/last/pallas_call | solution.py:28
  (4 shorter events, 0.1 us)
Async XLA Ops:
  5.9 3.2 %copy-start = (bf16[16,2,128,1024]{3,2,1,0:T(8,128)(2,1)}, bf16[16,2,128,1024]{3,2,1,0:T(8,128)(2,1)S(1)}, u32[]{:S(2)}) copy-start(bf16[16,2,128,1024]{3,2,1,0:T(8,128)(2,1)S(1)} %get-tuple-element.12.matrix_ref) | copy-start | bytes 25165828
  9.1 19.4 %all-to-all-start = ((bf16[8,128,128]{2,1,0:T(8,128)(2,1)}), bf16[8,128,128]{2,1,0:T(8,128)(2,1)S(1)}, u32[]{:S(2)}, u32[]{:S(2)}) async-start(bf16[8,128,128]{2,1,0:T(8,128)(2,1)} %get-tuple-element.13), calls=%async_computation | async-start | bytes 524288 | tf_op jit(solution)/shard_map/all_to_all | solution.py:245
  40.6 3.4 %copy-start.1 = (bf16[16,2,128,1024]{3,2,1,0:T(8,128)(2,1)S(1)}, bf16[16,2,128,1024]{3,2,1,0:T(8,128)(2,1)}, u32[]{:S(2)}) copy-start(bf16[16,2,128,1024]{3,2,1,0:T(8,128)(2,1)} %copy-done) | copy-start | bytes 25165828
  44.0 40.9 %slice-start = ((s8[8388608]{0:T(1024)(128)(4,1)}), s8[4194304]{0:T(1024)(128)(4,1)S(1)}, s32[]{:S(2)}) async-start(s8[8388608]{0:T(1024)(128)(4,1)} %bitcast.3), calls=%async_computation.10 | async-start | bytes 8388608
  45.2 39.6 %slice-start.1 = ((s8[8388608]{0:T(1024)(128)(4,1)}), s8[4194304]{0:T(1024)(128)(4,1)S(1)}, s32[]{:S(2)}) async-start(s8[8388608]{0:T(1024)(128)(4,1)} %bitcast.3), calls=%async_computation.11 | async-start | bytes 8388608
  45.2 5.0 %collective-permute-start = (bf16[16,128,128]{2,1,0:T(8,128)(2,1)S(1)}, bf16[16,128,128]{2,1,0:T(8,128)(2,1)S(1)}, u32[]{:S(2)}, u32[]{:S(2)}) collective-permute-start(bf16[16,128,128]{2,1,0:T(8,128)(2,1)S(1)} %odd_other.2), channel_id=1, source_target_pairs={{0,1},{1,0},{2,3},{3,2},{4,5},{5,4},{6,7},{7,6},{8,9},{9,8},{10,11... | collective-permute-start | bytes 1572872 | tf_op jit(solution)/shard_map/ppermute | solution.py:241
  80.0 4.8 %collective-permute-start.1 = (bf16[16,128,128]{2,1,0:T(8,128)(2,1)S(1)}, bf16[16,128,128]{2,1,0:T(8,128)(2,1)S(1)}, u32[]{:S(2)}, u32[]{:S(2)}) collective-permute-start(bf16[16,128,128]{2,1,0:T(8,128)(2,1)S(1)} %all_to_all.52.mine_ref), channel_id=1, source_target_pairs={{0,1},{1,0},{2,3},{3,2},{4,5},{5,4},{6,7},{7,6},{8,9},{9,8},{10,11... | collective-permute-start | bytes 1572872 | tf_op jit(solution)/shard_map/ppermute | solution.py:241
  116.9 2.2 %collective-permute-start.2 = (bf16[16,128,128]{2,1,0:T(8,128)(2,1)S(1)}, bf16[16,128,128]{2,1,0:T(8,128)(2,1)S(1)}, u32[]{:S(2)}, u32[]{:S(2)}) collective-permute-start(bf16[16,128,128]{2,1,0:T(8,128)(2,1)S(1)} %odd_other.3), channel_id=1, source_target_pairs={{0,1},{1,0},{2,3},{3,2},{4,5},{5,4},{6,7},{7,6},{8,9},{9,8},{10,11... | collective-permute-start | bytes 1572872 | tf_op jit(solution)/shard_map/ppermute | solution.py:241
  145.4 4.8 %collective-permute-start.3 = (bf16[16,128,128]{2,1,0:T(8,128)(2,1)S(1)}, bf16[16,128,128]{2,1,0:T(8,128)(2,1)S(1)}, u32[]{:S(2)}, u32[]{:S(2)}) collective-permute-start(bf16[16,128,128]{2,1,0:T(8,128)(2,1)S(1)} %all_to_all.56.mine_ref), channel_id=1, source_target_pairs={{0,1},{1,0},{2,3},{3,2},{4,5},{5,4},{6,7},{7,6},{8,9},{9,8},{10,11... | collective-permute-start | bytes 1572872 | tf_op jit(solution)/shard_map/ppermute | solution.py:241

commit v5 on v4

--- a/solution.py
+++ b/solution.py
@@ -22,18 +22,19 @@
 
 
 def local_call(
-    kernel, out_types, *args, name, in_space=pltpu.VMEM, out_space=pltpu.VMEM, scratch_shapes=()
+    kernel, out_types, *args, name, in_spaces=None, out_space=pltpu.VMEM, scratch_shapes=()
 ):
     vmem = pl.BlockSpec(memory_space=pltpu.VMEM)
+    in_spaces = in_spaces or [pltpu.VMEM] * len(args)
     return pl.pallas_call(
         kernel,
-        in_specs=[pl.BlockSpec(memory_space=in_space)] * len(args),
+        in_specs=[pl.BlockSpec(memory_space=space) for space in in_spaces],
         out_specs=[vmem] * len(out_types),
         out_shape=[out_space(*out_type) for out_type in out_types],
         scratch_shapes=list(scratch_shapes),
         compiler_params=pltpu.CompilerParams(vmem_limit_bytes=VMEM_LIMIT),
         name=name,
-    )(*(pltpu.with_memory_space_constraint(arg, in_space) for arg in args))
+    )(*(pltpu.with_memory_space_constraint(*pair) for pair in zip(args, in_spaces)))
 
 
 def gram_of(block):
@@ -137,7 +138,8 @@
 
 
 def start_kernel(
-    matrix_ref, start_ref, out_ref, own_ref, kept_ref, vectors_ref, total_ref, matrix_sems, start_sems
+    matrix_ref, start_ref, bound_ref, out_ref, own_ref, kept_ref, scale_ref,
+    vectors_ref, total_ref, matrix_sems, start_sems,
 ):
     pieces = []
     for i in range(0, matrix_ref.shape[0], PLANES):
@@ -149,6 +151,7 @@
         for copy in copies:
             copy.start()
         pieces.append(copies)
+    scale_ref[...] = 1.0 / jnp.full(scale_ref.shape, bound_ref[0], jnp.float32)
     for n, copies in enumerate(pieces):
         for copy in copies:
             copy.wait()
@@ -252,7 +255,6 @@
     plane_count = lax.axis_size("x") * lax.axis_size("y")
     share = block_rows // (2 * plane_count)
     col_share = block_cols // row_count
-    scale = jnp.broadcast_to(1.0 / spectral_bound[0], (8, K))
     matrix = hamiltonian.reshape(plane_count, 2, share, block_cols)
     start = start_block.reshape(plane_count, 2, share, K)
     half = (plane_count, share, K)
@@ -271,9 +273,10 @@
         return local_call(next_share_kernel, types, scale, parts, previous, name="next_share")
 
     pieces = plane_count // PLANES
-    parts, zeroth, matrix = local_call(
-        start_kernel, [(columns, bf16), ((share, K), f32), (matrix.shape, bf16)], matrix, start,
-        name="start", in_space=pltpu.HBM, scratch_shapes=[
+    parts, zeroth, matrix, scale = local_call(
+        start_kernel, [(columns, bf16), ((share, K), f32), (matrix.shape, bf16), ((8, K), f32)],
+        matrix, start, spectral_bound, name="start", in_spaces=[pltpu.HBM, pltpu.HBM, pltpu.SMEM],
+        scratch_shapes=[
             pltpu.VMEM(start.shape, f32), pltpu.VMEM((K, block_cols), f32),
             pltpu.SemaphoreType.DMA((pieces,)), pltpu.SemaphoreType.DMA((pieces,)),
         ],

time: 191 us -> 184 us (0.963)
  blocking collectives: 126 us -> 145 us
  waiting for transfers between devices: 13.3 us -> 3.66 us
  starting transfers between devices: 19.7 us -> 10.6 us
  local copies, waits for them, and re-layouts: 6.6 us -> 0 us
    all_to_all x9 -> x10, blocking collectives: 126 us -> 145 us  [exchange(): return lax.all_to_all(blocks, axes, 0, 0, tiled=True)]
    all_to_all x1 -> x0, waiting for transfers between devices: 9.66 us -> none  [exchange(): return lax.all_to_all(blocks, axes, 0, 0, tiled=True)]
    all_to_all x1 -> x0, starting transfers between devices: 9.01 us -> none  [exchange(): return lax.all_to_all(blocks, axes, 0, 0, tiled=True)]
    unnamed x8 -> x0, local copies, waits for them, and re-layouts: 6.6 us -> none
  transfers between devices with their start and end apart: 5 -> 4, of which waited for: 5 -> 4; matrix products, arithmetic and copies ran while one was open for 0% -> 0% of each run, Pallas kernels for 1% -> 1%
where the time goes in v5:
time: 184 us; the launch traced here: 183 us
  blocking collectives  145 us (79%)
  Pallas kernels  23.1 us (13%)
  starting transfers between devices  10.6 us (6%)
  waiting for transfers between devices  3.66 us (2%)
    all_to_all x10, blocking collectives, exchange(): return lax.all_to_all(blocks, axes, 0, 0, tiled=True)  145 us
    pallas_call x15, Pallas kernels, local_call(): pl.pallas_call(kernel, in_specs=[pl.BlockSpec(memory_space=space) for spa...  23.1 us
    ppermute x4, starting transfers between devices, swap_core(): return lax.ppermute(block, 'core', ((0, 1), (1, 0)))  10.6 us
  transfers between devices with their start and end apart: 4, of which 4 were waited for; matrix products, arithmetic and copies ran while one was open for 0% of the time, Pallas kernels for 1%

profile of v5, /device:TPU:1, one launch (start us, length us, event | category | flops | bytes accessed | tf_op | source)
XLA Modules:
  0.0 183.5 jit_solution(18129995449532894534)
XLA Ops:
  1.3 4.6 %start.1 = (bf16[8,128,128]{2,1,0:T(8,128)(2,1)S(1)}, f32[128,128]{1,0:T(8,128)S(1)}, bf16[16,2,128,1024]{3,2,1,0:T(8,128)(2,1)S(1)}, f32[8,128]{1,0:T(8,128)S(1)}) custom-call(bf16[16,2,128,1024]{3,2,1,0:T(8,128)(2,1)} %bitcast.2, f32[16,2,128,128]{3,2,1,0:T(8,128)} %bitcast.3, f32[1]{0:T(128)S(6)} %copy.5.bound_ref), custom_call_target="tpu_custom_call" | custom-call | tf_op jit(solution)/shard_map/start/pallas_call | solution.py:29
  5.8 19.2 %all_to_all.50.parts_ref = bf16[8,128,128]{2,1,0:T(8,128)(2,1)S(1)} all-to-all(bf16[8,128,128]{2,1,0:T(8,128)(2,1)S(1)} %get-tuple-element.15), channel_id=1, replica_groups=mesh['row'=8,'x'=4,'y'=4,'core'=2] {'row'}, dimensions={0} | all-to-all | bytes 524288 | tf_op jit(solution)/shard_map/all_to_all | solution.py:248
  25.1 12.0 %all_to_all.51.vectors_ref = bf16[8,128,128]{2,1,0:T(8,128)(2,1)S(1)} all-to-all(bf16[8,128,128]{2,1,0:T(8,128)(2,1)S(1)} %get-tuple-element.16), channel_id=1, replica_groups=mesh['row'=8,'x'=4,'y'=4,'core'=2] {'row'}, dimensions={0} | all-to-all | bytes 524288 | tf_op jit(solution)/shard_map/all_to_all | solution.py:248
  37.1 1.2 odd_other.2
  38.4 3.4 %collective-permute-start = (bf16[16,128,128]{2,1,0:T(8,128)(2,1)S(1)}, bf16[16,128,128]{2,1,0:T(8,128)(2,1)S(1)}, u32[]{:S(2)}, u32[]{:S(2)}) collective-permute-start(bf16[16,128,128]{2,1,0:T(8,128)(2,1)S(1)} %odd_other.2), channel_id=1, source_target_pairs={{0,1},{1,0},{2,3},{3,2},{4,5},{5,4},{6,7},{7,6},{8,9},{9,8},{10,11... | collective-permute-start | bytes 1572872 | tf_op jit(solution)/shard_map/ppermute | solution.py:244
  41.8 1.2 odd_mine.2.mine_ref
  43.0 0.3 collective-permute-done.received_ref
  43.3 0.1 pair.2
  43.4 16.9 %all_to_all.52.parts_ref = bf16[16,128,128]{2,1,0:T(8,128)(2,1)S(1)} all-to-all(bf16[16,128,128]{2,1,0:T(8,128)(2,1)S(1)} %pair.2), channel_id=1, replica_groups=mesh['row'=8,'x'=4,'y'=4,'core'=2] {'x','y'}, dimensions={0} | all-to-all | bytes 1048576 | tf_op jit(solution)/shard_map/all_to_all | solution.py:248
  60.3 0.1 next_share.3
  60.4 12.7 %all_to_all.53.mine_ref = bf16[16,128,128]{2,1,0:T(8,128)(2,1)S(1)} all-to-all(bf16[16,128,128]{2,1,0:T(8,128)(2,1)S(1)} %get-tuple-element.18), channel_id=1, replica_groups=mesh['row'=8,'x'=4,'y'=4,'core'=2] {'x','y'}, dimensions={0} | all-to-all | bytes 1048576 | tf_op jit(solution)/shard_map/all_to_all | solution.py:248
  73.2 3.3 %collective-permute-start.1 = (bf16[16,128,128]{2,1,0:T(8,128)(2,1)S(1)}, bf16[16,128,128]{2,1,0:T(8,128)(2,1)S(1)}, u32[]{:S(2)}, u32[]{:S(2)}) collective-permute-start(bf16[16,128,128]{2,1,0:T(8,128)(2,1)S(1)} %all_to_all.53.mine_ref), channel_id=1, source_target_pairs={{0,1},{1,0},{2,3},{3,2},{4,5},{5,4},{6,7},{7,6},{8,9},{9,8},{10,11... | collective-permute-start | bytes 1572872 | tf_op jit(solution)/shard_map/ppermute | solution.py:244
  76.4 1.5 collective-permute-done.1.other_ref
  78.0 1.4 even.1
  79.3 14.8 %all_to_all.54.parts_ref = bf16[8,128,128]{2,1,0:T(8,128)(2,1)S(1)} all-to-all(bf16[8,128,128]{2,1,0:T(8,128)(2,1)S(1)} %even.1), channel_id=1, replica_groups=mesh['row'=8,'x'=4,'y'=4,'core'=2] {'row'}, dimensions={0} | all-to-all | bytes 524288 | tf_op jit(solution)/shard_map/all_to_all | solution.py:248
  94.1 14.6 %all_to_all.55.vectors_ref = bf16[8,128,128]{2,1,0:T(8,128)(2,1)S(1)} all-to-all(bf16[8,128,128]{2,1,0:T(8,128)(2,1)S(1)} %next_share.4), channel_id=1, replica_groups=mesh['row'=8,'x'=4,'y'=4,'core'=2] {'row'}, dimensions={0} | all-to-all | bytes 524288 | tf_op jit(solution)/shard_map/all_to_all | solution.py:248
  108.8 1.2 odd_other.3
  110.0 0.7 collective-permute-start.2
  110.7 1.2 odd_mine.3.mine_ref
  111.9 0.3 collective-permute-done.2.received_ref
  112.2 0.1 pair.3
  112.3 13.3 %all_to_all.56.parts_ref = bf16[16,128,128]{2,1,0:T(8,128)(2,1)S(1)} all-to-all(bf16[16,128,128]{2,1,0:T(8,128)(2,1)S(1)} %pair.3), channel_id=1, replica_groups=mesh['row'=8,'x'=4,'y'=4,'core'=2] {'x','y'}, dimensions={0} | all-to-all | bytes 1048576 | tf_op jit(solution)/shard_map/all_to_all | solution.py:248
  125.7 0.1 next_share.5.block_ref
  125.8 12.7 %all_to_all.57.mine_ref = bf16[16,128,128]{2,1,0:T(8,128)(2,1)S(1)} all-to-all(bf16[16,128,128]{2,1,0:T(8,128)(2,1)S(1)} %next_share.5.block_ref), channel_id=1, replica_groups=mesh['row'=8,'x'=4,'y'=4,'core'=2] {'x','y'}, dimensions={0} | all-to-all | bytes 1048576 | tf_op jit(solution)/shard_map/all_to_all | solution.py:248
  138.5 3.3 %collective-permute-start.3 = (bf16[16,128,128]{2,1,0:T(8,128)(2,1)S(1)}, bf16[16,128,128]{2,1,0:T(8,128)(2,1)S(1)}, u32[]{:S(2)}, u32[]{:S(2)}) collective-permute-start(bf16[16,128,128]{2,1,0:T(8,128)(2,1)S(1)} %all_to_all.57.mine_ref), channel_id=1, source_target_pairs={{0,1},{1,0},{2,3},{3,2},{4,5},{5,4},{6,7},{7,6},{8,9},{9,8},{10,11... | collective-permute-start | bytes 1572872 | tf_op jit(solution)/shard_map/ppermute | solution.py:244
  141.7 1.5 collective-permute-done.3.other_ref
  143.3 0.5 first_gram.1
  143.8 15.0 %all_to_all.58.parts_ref = f32[8,72,128]{2,1,0:T(8,128)S(1)} all-to-all(f32[8,72,128]{2,1,0:T(8,128)S(1)} %first_gram.1), channel_id=1, replica_groups=mesh['row'=8,'x'=4,'y'=4,'core'=2] {'row'}, dimensions={0} | all-to-all | bytes 589824 | tf_op jit(solution)/shard_map/all_to_all | solution.py:248
  158.9 6.6 %second_gram.1 = (f32[8,72,128]{2,1,0:T(8,128)S(1)}, f32[128,128]{1,0:T(8,128)S(1)}, f32[128,128]{1,0:T(8,128)S(1)}) custom-call(f32[8,72,128]{2,1,0:T(8,128)S(1)} %all_to_all.58.parts_ref, bf16[16,128,128]{2,1,0:T(8,128)(2,1)S(1)} %all_to_all.57.mine_ref, bf16[16,128,128]{2,1,0:T(8,128)(2,1)S(1)} %collective-permute-done.3.other_ref), custom_call_target="tpu_custom_call" | custom-call | tf_op jit(solution)/shard_map/second_gram/pallas_call | solution.py:29
  165.4 13.4 %all_to_all.59.parts_ref = f32[8,72,128]{2,1,0:T(8,128)S(1)} all-to-all(f32[8,72,128]{2,1,0:T(8,128)S(1)} %get-tuple-element.21), channel_id=1, replica_groups=mesh['row'=8,'x'=4,'y'=4,'core'=2] {'row'}, dimensions={0} | all-to-all | bytes 589824 | tf_op jit(solution)/shard_map/all_to_all | solution.py:248
  178.8 4.6 %last.1 = (f32[128,128]{1,0:T(8,128)}, f32[128,128]{1,0:T(8,128)}) custom-call(f32[8,72,128]{2,1,0:T(8,128)S(1)} %all_to_all.59.parts_ref, f32[128,128]{1,0:T(8,128)S(1)} %get-tuple-element.22.upper_one_ref, f32[128,128]{1,0:T(8,128)S(1)} %get-tuple-element.23.inverse_one_ref, bf16[16,128,128]{2,1,0:T(8,128)(2,1)S(1)} %next_share.5.block_ref), custom_call_target="tpu_custom_call" | custom-call | tf_op jit(solution)/shard_map/last/pallas_call | solution.py:29
  (2 shorter events, 0.1 us)
Async XLA Ops:
  38.4 5.0 %collective-permute-start = (bf16[16,128,128]{2,1,0:T(8,128)(2,1)S(1)}, bf16[16,128,128]{2,1,0:T(8,128)(2,1)S(1)}, u32[]{:S(2)}, u32[]{:S(2)}) collective-permute-start(bf16[16,128,128]{2,1,0:T(8,128)(2,1)S(1)} %odd_other.2), channel_id=1, source_target_pairs={{0,1},{1,0},{2,3},{3,2},{4,5},{5,4},{6,7},{7,6},{8,9},{9,8},{10,11... | collective-permute-start | bytes 1572872 | tf_op jit(solution)/shard_map/ppermute | solution.py:244
  73.2 4.8 %collective-permute-start.1 = (bf16[16,128,128]{2,1,0:T(8,128)(2,1)S(1)}, bf16[16,128,128]{2,1,0:T(8,128)(2,1)S(1)}, u32[]{:S(2)}, u32[]{:S(2)}) collective-permute-start(bf16[16,128,128]{2,1,0:T(8,128)(2,1)S(1)} %all_to_all.53.mine_ref), channel_id=1, source_target_pairs={{0,1},{1,0},{2,3},{3,2},{4,5},{5,4},{6,7},{7,6},{8,9},{9,8},{10,11... | collective-permute-start | bytes 1572872 | tf_op jit(solution)/shard_map/ppermute | solution.py:244
  110.0 2.2 %collective-permute-start.2 = (bf16[16,128,128]{2,1,0:T(8,128)(2,1)S(1)}, bf16[16,128,128]{2,1,0:T(8,128)(2,1)S(1)}, u32[]{:S(2)}, u32[]{:S(2)}) collective-permute-start(bf16[16,128,128]{2,1,0:T(8,128)(2,1)S(1)} %odd_other.3), channel_id=1, source_target_pairs={{0,1},{1,0},{2,3},{3,2},{4,5},{5,4},{6,7},{7,6},{8,9},{9,8},{10,11... | collective-permute-start | bytes 1572872 | tf_op jit(solution)/shard_map/ppermute | solution.py:244
  138.5 4.8 %collective-permute-start.3 = (bf16[16,128,128]{2,1,0:T(8,128)(2,1)S(1)}, bf16[16,128,128]{2,1,0:T(8,128)(2,1)S(1)}, u32[]{:S(2)}, u32[]{:S(2)}) collective-permute-start(bf16[16,128,128]{2,1,0:T(8,128)(2,1)S(1)} %all_to_all.57.mine_ref), channel_id=1, source_target_pairs={{0,1},{1,0},{2,3},{3,2},{4,5},{5,4},{6,7},{7,6},{8,9},{9,8},{10,11... | collective-permute-start | bytes 1572872 | tf_op jit(solution)/shard_map/ppermute | solution.py:244

commit v6 on v5

--- a/solution.py
+++ b/solution.py
@@ -137,8 +137,13 @@
         out_ref[first + i] = block.T.astype(out_ref.dtype)
 
 
+def pair_half():
+    row = lax.axis_index("row")
+    return lax.rem(row + lax.div(row, 4), 2)
+
+
 def start_kernel(
-    matrix_ref, start_ref, bound_ref, out_ref, own_ref, kept_ref, scale_ref,
+    matrix_ref, start_ref, bound_ref, other_ref, mine_ref, own_ref, kept_ref, scale_ref,
     vectors_ref, total_ref, matrix_sems, start_sems,
 ):
     pieces = []
@@ -159,39 +164,79 @@
         vectors = vectors_ref[part].astype(jnp.bfloat16).reshape(-1, K)
         product = contract_rows(vectors, kept_ref[part].reshape(-1, kept_ref.shape[-1]))
         total_ref[...] = product if n == 0 else total_ref[...] + product
-    store_row_blocks(total_ref[...], 0, out_ref)
+    half = total_ref.shape[1] // 2
+    for own in (0, 1):
+
+        @pl.when(pair_half() == own)
+        def _():
+            store_row_blocks(total_ref[:, own * half : (own + 1) * half], 0, mine_ref)
+            store_row_blocks(total_ref[:, (1 - own) * half : (2 - own) * half], 0, other_ref)
+
     plane = lax.axis_index("x") * lax.axis_size("y") + lax.axis_index("y")
     own_ref[...] = vectors_ref[plane, lax.axis_index("core")]
 
 
-def even_kernel(matrix_ref, mine_ref, other_ref, out_ref):
+def even_kernel(offset, matrix_ref, mine_ref, other_ref, out_ref):
     core = lax.axis_index("core")
     mine, other = flat(mine_ref[...]), flat(other_ref[...])
-    for i in range(matrix_ref.shape[-1] // COLUMNS):
-        lanes = slice(i * COLUMNS, (i + 1) * COLUMNS)
-        product = contract_rows(mine, flat(matrix_ref[:, core, :, lanes]))
-        product = product + contract_rows(other, flat(matrix_ref[:, 1 - core, :, lanes]))
-        store_row_blocks(product, i * COLUMNS // out_ref.shape[1], out_ref)
-
-
-def odd_kernel(offset, matrix_ref, vectors_ref, out_ref):
+    half = matrix_ref.shape[-1] // 2
+    for own in (0, 1):
+
+        @pl.when(pair_half() == own)
+        def _():
+            base = (own ^ offset) * half
+            for i in range(0, half, COLUMNS):
+                lanes = slice(base + i, base + i + COLUMNS)
+                product = contract_rows(mine, flat(matrix_ref[:, core, :, lanes]))
+                product = product + contract_rows(other, flat(matrix_ref[:, 1 - core, :, lanes]))
+                store_row_blocks(product, i // out_ref.shape[1], out_ref)
+
+
+def odd_half(offset, column_offset, matrix_ref, vectors_ref, base_ref, out_ref):
     core = lax.axis_index("core")
     which = core if offset == 0 else 1 - core
     vectors = flat(vectors_ref[...])
-    for i in range(0, out_ref.shape[0], CHUNKS):
-        rows = flat(matrix_ref[i : i + CHUNKS, which])
-        product = jnp.dot(rows, vectors, preferred_element_type=jnp.float32)
-        out_ref[i : i + CHUNKS] = product.reshape(CHUNKS, -1, K).astype(out_ref.dtype)
+    half = matrix_ref.shape[-1] // 2
+    for own in (0, 1):
+
+        @pl.when(pair_half() == own)
+        def _():
+            base = (own ^ column_offset) * half
+            for i in range(0, out_ref.shape[0], CHUNKS):
+                rows = flat(matrix_ref[i : i + CHUNKS, which, :, base : base + half])
+                product = jnp.dot(rows, vectors, preferred_element_type=jnp.float32)
+                product = product.reshape(CHUNKS, -1, K)
+                if base_ref is not None:
+                    product = product + base_ref[i : i + CHUNKS]
+                out_ref[i : i + CHUNKS] = product.astype(out_ref.dtype)
+
+
+def odd_first_kernel(matrix_ref, vectors_ref, other_ref, mine_ref):
+    odd_half(1, 0, matrix_ref, vectors_ref, None, other_ref)
+    odd_half(0, 0, matrix_ref, vectors_ref, None, mine_ref)
+
+
+def odd_last_kernel(offset, matrix_ref, vectors_ref, base_ref, out_ref):
+    odd_half(offset, 1, matrix_ref, vectors_ref, base_ref, out_ref)
 
 
 def pair_kernel(mine_ref, received_ref, out_ref):
     out_ref[...] = (mine_ref[...] + received_ref[...].astype(jnp.float32)).astype(out_ref.dtype)
 
 
-def first_share_kernel(scale_ref, parts_ref, share_ref, copies_ref):
-    total = sum_copies(parts_ref) * scale_ref[:1]
-    share_ref[...] = total
-    copies_ref[...] = jnp.broadcast_to(total.astype(copies_ref.dtype)[None], copies_ref.shape)
+def four_sum_kernel(first, scale_ref, own_ref, two_ref, five_ref, seven_ref, *refs):
+    own, two, five, seven = (
+        ref[...].astype(jnp.float32) for ref in (own_ref, two_ref, five_ref, seven_ref)
+    )
+    total = (own + two) + (five + seven)
+    if first:
+        share_ref, rounded_ref = refs
+        total = total * scale_ref[:1]
+        share_ref[...] = total
+    else:
+        previous_ref, rounded_ref = refs
+        total = 2.0 * scale_ref[:1] * total - previous_ref[...]
+    rounded_ref[...] = total.astype(rounded_ref.dtype)
 
 
 def next_share_kernel(scale_ref, parts_ref, previous_ref, *out_refs):
@@ -244,6 +289,11 @@
     return lax.ppermute(block, "core", ((0, 1), (1, 0)))
 
 
+def swap_row(block, mask):
+    count = lax.axis_size("row")
+    return lax.ppermute(block, "row", [(i, i ^ mask) for i in range(count)])
+
+
 def exchange(blocks, axes):
     return lax.all_to_all(blocks, axes, 0, 0, tiled=True)
 
@@ -254,18 +304,33 @@
     row_count = lax.axis_size("row")
     plane_count = lax.axis_size("x") * lax.axis_size("y")
     share = block_rows // (2 * plane_count)
-    col_share = block_cols // row_count
     matrix = hamiltonian.reshape(plane_count, 2, share, block_cols)
     start = start_block.reshape(plane_count, 2, share, K)
-    half = (plane_count, share, K)
-    columns = (row_count, col_share, K)
-
-    def odd_parts(vectors):
-        kernels = [functools.partial(odd_kernel, offset) for offset in (0, 1)]
-        (other,) = local_call(kernels[1], [(half, bf16)], matrix, vectors, name="odd_other")
-        received = swap_core(other)
-        (mine,) = local_call(kernels[0], [(half, f32)], matrix, vectors, name="odd_mine")
-        (pair,) = local_call(pair_kernel, [(half, bf16)], mine, received, name="pair")
+    rows = (plane_count, share, K)
+    columns = (block_cols // (2 * share), share, K)
+
+    def sum_rows(other, mine_of, previous=None):
+        received = swap_row(other, 1)
+        (own,) = local_call(pair_kernel, [(columns, bf16)], mine_of(), received, name="pair_row")
+        parts = [own, *(swap_row(own, mask) for mask in (2, 5, 7))]
+        first = previous is None
+        types = [(columns, f32)] * first + [(columns, bf16)]
+        args = parts if first else [*parts, previous]
+        kernel = functools.partial(four_sum_kernel, first)
+        return local_call(kernel, types, scale, *args, name="four_sum")
+
+    def odd_parts(own):
+        received = swap_row(own, 1)
+        other, mine = local_call(
+            odd_first_kernel, [(rows, f32), (rows, f32)], matrix, own, name="odd_first"
+        )
+        kernels = [functools.partial(odd_last_kernel, offset) for offset in (0, 1)]
+        (other,) = local_call(
+            kernels[1], [(rows, bf16)], matrix, received, other, name="odd_other"
+        )
+        swapped = swap_core(other)
+        (mine,) = local_call(kernels[0], [(rows, f32)], matrix, received, mine, name="odd_mine")
+        (pair,) = local_call(pair_kernel, [(rows, bf16)], mine, swapped, name="pair_core")
         return exchange(pair, PLANE)
 
     def next_share(parts, previous, keep):
@@ -273,25 +338,27 @@
         return local_call(next_share_kernel, types, scale, parts, previous, name="next_share")
 
     pieces = plane_count // PLANES
-    parts, zeroth, matrix, scale = local_call(
-        start_kernel, [(columns, bf16), ((share, K), f32), (matrix.shape, bf16), ((8, K), f32)],
+    other, mine, zeroth, matrix, scale = local_call(
+        start_kernel,
+        [(columns, f32), (columns, f32), ((share, K), f32), (matrix.shape, bf16), ((8, K), f32)],
         matrix, start, spectral_bound, name="start", in_spaces=[pltpu.HBM, pltpu.HBM, pltpu.SMEM],
         scratch_shapes=[
             pltpu.VMEM(start.shape, f32), pltpu.VMEM((K, block_cols), f32),
             pltpu.SemaphoreType.DMA((pieces,)), pltpu.SemaphoreType.DMA((pieces,)),
         ],
     )
-    first, copies = local_call(
-        first_share_kernel, [((col_share, K), f32), (columns, bf16)], scale, exchange(parts, "row"),
-        name="first_share",
-    )
-    second, copies = next_share(odd_parts(exchange(copies, "row")), zeroth, True)
-    mine = exchange(copies, PLANE)
-    (parts,) = local_call(
-        even_kernel, [(columns, bf16)], matrix, mine, swap_core(mine), name="even"
-    )
-    (copies,) = next_share(exchange(parts, "row"), first, False)
-    (copies,) = next_share(odd_parts(exchange(copies, "row")), second, False)
+    first, vectors = sum_rows(other, lambda: mine)
+    second, copies = next_share(odd_parts(vectors), zeroth, True)
+    own = exchange(copies, PLANE)
+    swapped = swap_core(own)
+
+    def even_part(offset):
+        kernel = functools.partial(even_kernel, offset)
+        dtype = bf16 if offset else f32
+        return local_call(kernel, [(columns, dtype)], matrix, own, swapped, name="even")[0]
+
+    (vectors,) = sum_rows(even_part(1), lambda: even_part(0), first)
+    (copies,) = next_share(odd_parts(vectors), second, False)
 
     mine = exchange(copies, PLANE)
     other = swap_core(mine)

time: 184 us -> 182 us (0.989)
  blocking collectives: 145 us -> 85.3 us
  waiting for transfers between devices: 3.66 us -> 39.6 us
  starting transfers between devices: 10.6 us -> 29.7 us
  Pallas kernels: 23.1 us -> 25 us
    all_to_all x10 -> x6, blocking collectives: 145 us -> 85.3 us  [exchange(): return lax.all_to_all(blocks, axes, 0, 0, tiled=True)]
    ppermute x0 -> x10, waiting for transfers between devices: none -> 34.9 us  [swap_row(): return lax.ppermute(block, 'row', [(i, i ^ mask) for i in range(count)])]
    ppermute x0 -> x10, starting transfers between devices: none -> 17.1 us  [swap_row(): return lax.ppermute(block, 'row', [(i, i ^ mask) for i in range(count)])]
    ppermute x4, starting transfers between devices: 10.6 us -> 12.6 us  [swap_core(): return lax.ppermute(block, 'core', ((0, 1), (1, 0)))]
    pallas_call x15 -> x20, Pallas kernels: 23.1 us -> 25 us  [local_call(): pl.pallas_call(kernel, in_specs=[pl.BlockSpec(memory_space=space) for spa...]
  transfers between devices with their start and end apart: 4 -> 14, of which waited for: 4 -> 13; matrix products, arithmetic and copies ran while one was open for 0% -> 0% of each run, Pallas kernels for 1% -> 3%
where the time goes in v6:
time: 182 us; the launch traced here: 181 us
  blocking collectives  85.3 us (47%)
  waiting for transfers between devices  39.6 us (22%)
  starting transfers between devices  29.7 us (16%)
  Pallas kernels  25 us (14%)
    all_to_all x6, blocking collectives, exchange(): return lax.all_to_all(blocks, axes, 0, 0, tiled=True)  85.3 us
    ppermute x10, waiting for transfers between devices, swap_row(): return lax.ppermute(block, 'row', [(i, i ^ mask) for i in range(count)])  34.9 us
    pallas_call x20, Pallas kernels, local_call(): pl.pallas_call(kernel, in_specs=[pl.BlockSpec(memory_space=space) for spa...  25 us
    ppermute x10, starting transfers between devices, swap_row(): return lax.ppermute(block, 'row', [(i, i ^ mask) for i in range(count)])  17.1 us
    ppermute x4, starting transfers between devices, swap_core(): return lax.ppermute(block, 'core', ((0, 1), (1, 0)))  12.6 us
    ppermute x4, waiting for transfers between devices, swap_core(): return lax.ppermute(block, 'core', ((0, 1), (1, 0)))  4.67 us
  transfers between devices with their start and end apart: 14, of which 13 were waited for; matrix products, arithmetic and copies ran while one was open for 0% of the time, Pallas kernels for 3%

profile of v6, /device:TPU:1, one launch (start us, length us, event | category | flops | bytes accessed | tf_op | source)
XLA Modules:
  0.0 181.0 jit_solution(94841348755447954)
XLA Ops:
  1.3 4.7 %start.1 = (f32[4,128,128]{2,1,0:T(8,128)S(1)}, f32[4,128,128]{2,1,0:T(8,128)S(1)}, f32[128,128]{1,0:T(8,128)S(1)}, bf16[16,2,128,1024]{3,2,1,0:T(8,128)(2,1)S(1)}, f32[8,128]{1,0:T(8,128)S(1)}) custom-call(bf16[16,2,128,1024]{3,2,1,0:T(8,128)(2,1)} %bitcast.2, f32[16,2,128,128]{3,2,1,0:T(8,128)} %bitcast.3, f32[1]{0:T(128)S(6)} %copy.5.bound_ref), custom_call_target="tpu_custom_call" | custom-call | tf_op jit(solution)/shard_map/start/pallas_call | solution.py:29
  5.9 2.6 %collective-permute-start = (f32[4,128,128]{2,1,0:T(8,128)S(1)}, f32[4,128,128]{2,1,0:T(8,128)S(1)}, u32[]{:S(2)}, u32[]{:S(2)}) collective-permute-start(f32[4,128,128]{2,1,0:T(8,128)S(1)} %get-tuple-element.21), channel_id=1, source_target_pairs={{0,32},{32,0},{64,96},{96,64},{128,160},{160,128},{192,224},{224,1... | collective-permute-start | bytes 786440 | tf_op jit(solution)/shard_map/ppermute | solution.py:294
  8.5 5.0 %collective-permute-done.received_ref = f32[4,128,128]{2,1,0:T(8,128)S(1)} collective-permute-done((f32[4,128,128]{2,1,0:T(8,128)S(1)}, f32[4,128,128]{2,1,0:T(8,128)S(1)}, u32[]{:S(2)}, u32[]{:S(2)}) %collective-permute-start) | collective-permute-done | bytes 262176 | tf_op jit(solution)/shard_map/ppermute | solution.py:294
  13.5 4.1 %collective-permute-start.1 = (bf16[4,128,128]{2,1,0:T(8,128)(2,1)S(1)}, bf16[4,128,128]{2,1,0:T(8,128)(2,1)S(1)}, u32[]{:S(2)}, u32[]{:S(2)}) collective-permute-start(bf16[4,128,128]{2,1,0:T(8,128)(2,1)S(1)} %pair_row.2.own_ref), channel_id=1, source_target_pairs={{0,64},{32,96},{64,0},{96,32},{128,192},{160,224},{192,128},{224,1... | collective-permute-start | bytes 393224 | tf_op jit(solution)/shard_map/ppermute | solution.py:294
  17.6 4.2 %collective-permute-start.2 = (bf16[4,128,128]{2,1,0:T(8,128)(2,1)S(1)}, bf16[4,128,128]{2,1,0:T(8,128)(2,1)S(1)}, u32[]{:S(2)}, u32[]{:S(2)}) collective-permute-start(bf16[4,128,128]{2,1,0:T(8,128)(2,1)S(1)} %pair_row.2.own_ref), channel_id=1, source_target_pairs={{0,160},{32,128},{64,224},{96,192},{128,32},{160,0},{192,96},{224,... | collective-permute-start | bytes 393224 | tf_op jit(solution)/shard_map/ppermute | solution.py:294
  21.8 1.5 collective-permute-done.1.two_ref
  23.3 10.1 %collective-permute-done.2.five_ref = bf16[4,128,128]{2,1,0:T(8,128)(2,1)S(1)} collective-permute-done((bf16[4,128,128]{2,1,0:T(8,128)(2,1)S(1)}, bf16[4,128,128]{2,1,0:T(8,128)(2,1)S(1)}, u32[]{:S(2)}, u32[]{:S(2)}) %collective-permute-start.2) | collective-permute-done | bytes 131104 | tf_op jit(solution)/shard_map/ppermute | solution.py:294
  33.5 0.1 collective-permute-start.4
  33.6 1.5 odd_first.2
  35.1 2.3 %collective-permute-done.4.vectors_ref = bf16[4,128,128]{2,1,0:T(8,128)(2,1)S(1)} collective-permute-done((bf16[4,128,128]{2,1,0:T(8,128)(2,1)S(1)}, bf16[4,128,128]{2,1,0:T(8,128)(2,1)S(1)}, u32[]{:S(2)}, u32[]{:S(2)}) %collective-permute-start.4) | collective-permute-done | bytes 131104 | tf_op jit(solution)/shard_map/ppermute | solution.py:294
  37.4 0.7 odd_other.2
  38.1 2.8 %collective-permute-start.5 = (bf16[16,128,128]{2,1,0:T(8,128)(2,1)S(1)}, bf16[16,128,128]{2,1,0:T(8,128)(2,1)S(1)}, u32[]{:S(2)}, u32[]{:S(2)}) collective-permute-start(bf16[16,128,128]{2,1,0:T(8,128)(2,1)S(1)} %odd_other.2), channel_id=1, source_target_pairs={{0,1},{1,0},{2,3},{3,2},{4,5},{5,4},{6,7},{7,6},{8,9},{9,8},{10,11... | collective-permute-start | bytes 1572872 | tf_op jit(solution)/shard_map/ppermute | solution.py:289
  40.9 0.7 odd_mine.2.mine_ref
  41.7 0.8 collective-permute-done.5.received_ref
  42.5 0.1 pair_core.2
  42.6 16.9 %all_to_all.30.parts_ref = bf16[16,128,128]{2,1,0:T(8,128)(2,1)S(1)} all-to-all(bf16[16,128,128]{2,1,0:T(8,128)(2,1)S(1)} %pair_core.2), channel_id=1, replica_groups=mesh['row'=8,'x'=4,'y'=4,'core'=2] {'x','y'}, dimensions={0} | all-to-all | bytes 1048576 | tf_op jit(solution)/shard_map/all_to_all | solution.py:298
  59.5 0.1 next_share.2
  59.6 12.7 %all_to_all.31.mine_ref = bf16[16,128,128]{2,1,0:T(8,128)(2,1)S(1)} all-to-all(bf16[16,128,128]{2,1,0:T(8,128)(2,1)S(1)} %get-tuple-element.26), channel_id=1, replica_groups=mesh['row'=8,'x'=4,'y'=4,'core'=2] {'x','y'}, dimensions={0} | all-to-all | bytes 1048576 | tf_op jit(solution)/shard_map/all_to_all | solution.py:298
  72.3 3.3 %collective-permute-start.6 = (bf16[16,128,128]{2,1,0:T(8,128)(2,1)S(1)}, bf16[16,128,128]{2,1,0:T(8,128)(2,1)S(1)}, u32[]{:S(2)}, u32[]{:S(2)}) collective-permute-start(bf16[16,128,128]{2,1,0:T(8,128)(2,1)S(1)} %all_to_all.31.mine_ref), channel_id=1, source_target_pairs={{0,1},{1,0},{2,3},{3,2},{4,5},{5,4},{6,7},{7,6},{8,9},{9,8},{10,11... | collective-permute-start | bytes 1572872 | tf_op jit(solution)/shard_map/ppermute | solution.py:289
  75.6 1.5 collective-permute-done.6.other_ref
  77.1 1.1 even.3
  78.2 1.1 collective-permute-start.7
  79.3 1.0 even.2.mine_ref
  80.3 2.7 %collective-permute-done.7.received_ref = bf16[4,128,128]{2,1,0:T(8,128)(2,1)S(1)} collective-permute-done((bf16[4,128,128]{2,1,0:T(8,128)(2,1)S(1)}, bf16[4,128,128]{2,1,0:T(8,128)(2,1)S(1)}, u32[]{:S(2)}, u32[]{:S(2)}) %collective-permute-start.7) | collective-permute-done | bytes 131104 | tf_op jit(solution)/shard_map/ppermute | solution.py:294
  83.1 2.5 %collective-permute-start.10 = (bf16[4,128,128]{2,1,0:T(8,128)(2,1)S(1)}, bf16[4,128,128]{2,1,0:T(8,128)(2,1)S(1)}, u32[]{:S(2)}, u32[]{:S(2)}) collective-permute-start(bf16[4,128,128]{2,1,0:T(8,128)(2,1)S(1)} %pair_row.3.own_ref), channel_id=1, source_target_pairs={{0,224},{32,192},{64,160},{96,128},{128,96},{160,64},{192,32},{224... | collective-permute-start | bytes 393224 | tf_op jit(solution)/shard_map/ppermute | solution.py:294
  85.6 1.4 collective-permute-start.8
  87.0 1.0 collective-permute-start.9
  87.9 1.3 collective-permute-done.10.seven_ref
  89.3 1.4 collective-permute-done.8.two_ref
  90.7 8.3 %collective-permute-done.9.five_ref = bf16[4,128,128]{2,1,0:T(8,128)(2,1)S(1)} collective-permute-done((bf16[4,128,128]{2,1,0:T(8,128)(2,1)S(1)}, bf16[4,128,128]{2,1,0:T(8,128)(2,1)S(1)}, u32[]{:S(2)}, u32[]{:S(2)}) %collective-permute-start.9) | collective-permute-done | bytes 131104 | tf_op jit(solution)/shard_map/ppermute | solution.py:294
  98.9 0.1 four_sum.3.vectors_ref
  99.0 0.1 collective-permute-start.11
  99.1 1.5 odd_first.3
  100.6 2.3 %collective-permute-done.11.vectors_ref = bf16[4,128,128]{2,1,0:T(8,128)(2,1)S(1)} collective-permute-done((bf16[4,128,128]{2,1,0:T(8,128)(2,1)S(1)}, bf16[4,128,128]{2,1,0:T(8,128)(2,1)S(1)}, u32[]{:S(2)}, u32[]{:S(2)}) %collective-permute-start.11) | collective-permute-done | bytes 131104 | tf_op jit(solution)/shard_map/ppermute | solution.py:294
  102.9 0.7 odd_other.3
  103.7 3.3 %collective-permute-start.12 = (bf16[16,128,128]{2,1,0:T(8,128)(2,1)S(1)}, bf16[16,128,128]{2,1,0:T(8,128)(2,1)S(1)}, u32[]{:S(2)}, u32[]{:S(2)}) collective-permute-start(bf16[16,128,128]{2,1,0:T(8,128)(2,1)S(1)} %odd_other.3), channel_id=1, source_target_pairs={{0,1},{1,0},{2,3},{3,2},{4,5},{5,4},{6,7},{7,6},{8,9},{9,8},{10,11... | collective-permute-start | bytes 1572872 | tf_op jit(solution)/shard_map/ppermute | solution.py:289
  107.0 0.7 odd_mine.3.mine_ref
  107.8 0.8 collective-permute-done.12.received_ref
  108.7 13.3 %all_to_all.32.parts_ref = bf16[16,128,128]{2,1,0:T(8,128)(2,1)S(1)} all-to-all(bf16[16,128,128]{2,1,0:T(8,128)(2,1)S(1)} %pair_core.3), channel_id=1, replica_groups=mesh['row'=8,'x'=4,'y'=4,'core'=2] {'x','y'}, dimensions={0} | all-to-all | bytes 1048576 | tf_op jit(solution)/shard_map/all_to_all | solution.py:298
  122.0 0.1 next_share.3.block_ref
  122.1 12.7 %all_to_all.33.mine_ref = bf16[16,128,128]{2,1,0:T(8,128)(2,1)S(1)} all-to-all(bf16[16,128,128]{2,1,0:T(8,128)(2,1)S(1)} %next_share.3.block_ref), channel_id=1, replica_groups=mesh['row'=8,'x'=4,'y'=4,'core'=2] {'x','y'}, dimensions={0} | all-to-all | bytes 1048576 | tf_op jit(solution)/shard_map/all_to_all | solution.py:298
  134.8 3.3 %collective-permute-start.13 = (bf16[16,128,128]{2,1,0:T(8,128)(2,1)S(1)}, bf16[16,128,128]{2,1,0:T(8,128)(2,1)S(1)}, u32[]{:S(2)}, u32[]{:S(2)}) collective-permute-start(bf16[16,128,128]{2,1,0:T(8,128)(2,1)S(1)} %all_to_all.33.mine_ref), channel_id=1, source_target_pairs={{0,1},{1,0},{2,3},{3,2},{4,5},{5,4},{6,7},{7,6},{8,9},{9,8},{10,11... | collective-permute-start | bytes 1572872 | tf_op jit(solution)/shard_map/ppermute | solution.py:289
  138.1 1.5 collective-permute-done.13.other_ref
  139.6 0.5 first_gram.1
  140.2 16.8 %all_to_all.34.parts_ref = f32[8,72,128]{2,1,0:T(8,128)S(1)} all-to-all(f32[8,72,128]{2,1,0:T(8,128)S(1)} %first_gram.1), channel_id=1, replica_groups=mesh['row'=8,'x'=4,'y'=4,'core'=2] {'row'}, dimensions={0} | all-to-all | bytes 589824 | tf_op jit(solution)/shard_map/all_to_all | solution.py:298
  156.9 6.6 %second_gram.1 = (f32[8,72,128]{2,1,0:T(8,128)S(1)}, f32[128,128]{1,0:T(8,128)S(1)}, f32[128,128]{1,0:T(8,128)S(1)}) custom-call(f32[8,72,128]{2,1,0:T(8,128)S(1)} %all_to_all.34.parts_ref, bf16[16,128,128]{2,1,0:T(8,128)(2,1)S(1)} %all_to_all.33.mine_ref, bf16[16,128,128]{2,1,0:T(8,128)(2,1)S(1)} %collective-permute-done.13.other_ref), custom_call_target="tpu_custom_call" | custom-call | tf_op jit(solution)/shard_map/second_gram/pallas_call | solution.py:29
  163.5 12.9 %all_to_all.35.parts_ref = f32[8,72,128]{2,1,0:T(8,128)S(1)} all-to-all(f32[8,72,128]{2,1,0:T(8,128)S(1)} %get-tuple-element.31), channel_id=1, replica_groups=mesh['row'=8,'x'=4,'y'=4,'core'=2] {'row'}, dimensions={0} | all-to-all | bytes 589824 | tf_op jit(solution)/shard_map/all_to_all | solution.py:298
  176.4 4.6 %last.1 = (f32[128,128]{1,0:T(8,128)}, f32[128,128]{1,0:T(8,128)}) custom-call(f32[8,72,128]{2,1,0:T(8,128)S(1)} %all_to_all.35.parts_ref, f32[128,128]{1,0:T(8,128)S(1)} %get-tuple-element.32.upper_one_ref, f32[128,128]{1,0:T(8,128)S(1)} %get-tuple-element.33.inverse_one_ref, bf16[16,128,128]{2,1,0:T(8,128)(2,1)S(1)} %next_share.3.block_ref), custom_call_target="tpu_custom_call" | custom-call | tf_op jit(solution)/shard_map/last/pallas_call | solution.py:29
  (6 shorter events, 0.2 us)
Async XLA Ops:
  5.9 7.6 %collective-permute-start = (f32[4,128,128]{2,1,0:T(8,128)S(1)}, f32[4,128,128]{2,1,0:T(8,128)S(1)}, u32[]{:S(2)}, u32[]{:S(2)}) collective-permute-start(f32[4,128,128]{2,1,0:T(8,128)S(1)} %get-tuple-element.21), channel_id=1, source_target_pairs={{0,32},{32,0},{64,96},{96,64},{128,160},{160,128},{192,224},{224,1... | collective-permute-start | bytes 786440 | tf_op jit(solution)/shard_map/ppermute | solution.py:294
  13.5 9.8 %collective-permute-start.1 = (bf16[4,128,128]{2,1,0:T(8,128)(2,1)S(1)}, bf16[4,128,128]{2,1,0:T(8,128)(2,1)S(1)}, u32[]{:S(2)}, u32[]{:S(2)}) collective-permute-start(bf16[4,128,128]{2,1,0:T(8,128)(2,1)S(1)} %pair_row.2.own_ref), channel_id=1, source_target_pairs={{0,64},{32,96},{64,0},{96,32},{128,192},{160,224},{192,128},{224,1... | collective-permute-start | bytes 393224 | tf_op jit(solution)/shard_map/ppermute | solution.py:294
  17.6 15.8 %collective-permute-start.2 = (bf16[4,128,128]{2,1,0:T(8,128)(2,1)S(1)}, bf16[4,128,128]{2,1,0:T(8,128)(2,1)S(1)}, u32[]{:S(2)}, u32[]{:S(2)}) collective-permute-start(bf16[4,128,128]{2,1,0:T(8,128)(2,1)S(1)} %pair_row.2.own_ref), channel_id=1, source_target_pairs={{0,160},{32,128},{64,224},{96,192},{128,32},{160,0},{192,96},{224,... | collective-permute-start | bytes 393224 | tf_op jit(solution)/shard_map/ppermute | solution.py:294
  21.8 11.6 %collective-permute-start.3 = (bf16[4,128,128]{2,1,0:T(8,128)(2,1)S(1)}, bf16[4,128,128]{2,1,0:T(8,128)(2,1)S(1)}, u32[]{:S(2)}, u32[]{:S(2)}) collective-permute-start(bf16[4,128,128]{2,1,0:T(8,128)(2,1)S(1)} %pair_row.2.own_ref), channel_id=1, source_target_pairs={{0,224},{32,192},{64,160},{96,128},{128,96},{160,64},{192,32},{224... | collective-permute-start | bytes 393224 | tf_op jit(solution)/shard_map/ppermute | solution.py:294
  33.5 3.9 %collective-permute-start.4 = (bf16[4,128,128]{2,1,0:T(8,128)(2,1)S(1)}, bf16[4,128,128]{2,1,0:T(8,128)(2,1)S(1)}, u32[]{:S(2)}, u32[]{:S(2)}) collective-permute-start(bf16[4,128,128]{2,1,0:T(8,128)(2,1)S(1)} %get-tuple-element.22.vectors_ref), channel_id=1, source_target_pairs={{0,32},{32,0},{64,96},{96,64},{128,160},{160,128},{192,224},{224,1... | collective-permute-start | bytes 393224 | tf_op jit(solution)/shard_map/ppermute | solution.py:294
  38.1 4.3 %collective-permute-start.5 = (bf16[16,128,128]{2,1,0:T(8,128)(2,1)S(1)}, bf16[16,128,128]{2,1,0:T(8,128)(2,1)S(1)}, u32[]{:S(2)}, u32[]{:S(2)}) collective-permute-start(bf16[16,128,128]{2,1,0:T(8,128)(2,1)S(1)} %odd_other.2), channel_id=1, source_target_pairs={{0,1},{1,0},{2,3},{3,2},{4,5},{5,4},{6,7},{7,6},{8,9},{9,8},{10,11... | collective-permute-start | bytes 1572872 | tf_op jit(solution)/shard_map/ppermute | solution.py:289
  72.3 4.8 %collective-permute-start.6 = (bf16[16,128,128]{2,1,0:T(8,128)(2,1)S(1)}, bf16[16,128,128]{2,1,0:T(8,128)(2,1)S(1)}, u32[]{:S(2)}, u32[]{:S(2)}) collective-permute-start(bf16[16,128,128]{2,1,0:T(8,128)(2,1)S(1)} %all_to_all.31.mine_ref), channel_id=1, source_target_pairs={{0,1},{1,0},{2,3},{3,2},{4,5},{5,4},{6,7},{7,6},{8,9},{9,8},{10,11... | collective-permute-start | bytes 1572872 | tf_op jit(solution)/shard_map/ppermute | solution.py:289
  78.2 4.8 %collective-permute-start.7 = (bf16[4,128,128]{2,1,0:T(8,128)(2,1)S(1)}, bf16[4,128,128]{2,1,0:T(8,128)(2,1)S(1)}, u32[]{:S(2)}, u32[]{:S(2)}) collective-permute-start(bf16[4,128,128]{2,1,0:T(8,128)(2,1)S(1)} %even.3), channel_id=1, source_target_pairs={{0,32},{32,0},{64,96},{96,64},{128,160},{160,128},{192,224},{224,1... | collective-permute-start | bytes 393224 | tf_op jit(solution)/shard_map/ppermute | solution.py:294
  83.1 6.2 %collective-permute-start.10 = (bf16[4,128,128]{2,1,0:T(8,128)(2,1)S(1)}, bf16[4,128,128]{2,1,0:T(8,128)(2,1)S(1)}, u32[]{:S(2)}, u32[]{:S(2)}) collective-permute-start(bf16[4,128,128]{2,1,0:T(8,128)(2,1)S(1)} %pair_row.3.own_ref), channel_id=1, source_target_pairs={{0,224},{32,192},{64,160},{96,128},{128,96},{160,64},{192,32},{224... | collective-permute-start | bytes 393224 | tf_op jit(solution)/shard_map/ppermute | solution.py:294
  85.6 5.1 %collective-permute-start.8 = (bf16[4,128,128]{2,1,0:T(8,128)(2,1)S(1)}, bf16[4,128,128]{2,1,0:T(8,128)(2,1)S(1)}, u32[]{:S(2)}, u32[]{:S(2)}) collective-permute-start(bf16[4,128,128]{2,1,0:T(8,128)(2,1)S(1)} %pair_row.3.own_ref), channel_id=1, source_target_pairs={{0,64},{32,96},{64,0},{96,32},{128,192},{160,224},{192,128},{224,1... | collective-permute-start | bytes 393224 | tf_op jit(solution)/shard_map/ppermute | solution.py:294
  87.0 12.0 %collective-permute-start.9 = (bf16[4,128,128]{2,1,0:T(8,128)(2,1)S(1)}, bf16[4,128,128]{2,1,0:T(8,128)(2,1)S(1)}, u32[]{:S(2)}, u32[]{:S(2)}) collective-permute-start(bf16[4,128,128]{2,1,0:T(8,128)(2,1)S(1)} %pair_row.3.own_ref), channel_id=1, source_target_pairs={{0,160},{32,128},{64,224},{96,192},{128,32},{160,0},{192,96},{224,... | collective-permute-start | bytes 393224 | tf_op jit(solution)/shard_map/ppermute | solution.py:294
  99.0 3.9 %collective-permute-start.11 = (bf16[4,128,128]{2,1,0:T(8,128)(2,1)S(1)}, bf16[4,128,128]{2,1,0:T(8,128)(2,1)S(1)}, u32[]{:S(2)}, u32[]{:S(2)}) collective-permute-start(bf16[4,128,128]{2,1,0:T(8,128)(2,1)S(1)} %four_sum.3.vectors_ref), channel_id=1, source_target_pairs={{0,32},{32,0},{64,96},{96,64},{128,160},{160,128},{192,224},{224,1... | collective-permute-start | bytes 393224 | tf_op jit(solution)/shard_map/ppermute | solution.py:294
  103.7 4.9 %collective-permute-start.12 = (bf16[16,128,128]{2,1,0:T(8,128)(2,1)S(1)}, bf16[16,128,128]{2,1,0:T(8,128)(2,1)S(1)}, u32[]{:S(2)}, u32[]{:S(2)}) collective-permute-start(bf16[16,128,128]{2,1,0:T(8,128)(2,1)S(1)} %odd_other.3), channel_id=1, source_target_pairs={{0,1},{1,0},{2,3},{3,2},{4,5},{5,4},{6,7},{7,6},{8,9},{9,8},{10,11... | collective-permute-start | bytes 1572872 | tf_op jit(solution)/shard_map/ppermute | solution.py:289
  134.8 4.8 %collective-permute-start.13 = (bf16[16,128,128]{2,1,0:T(8,128)(2,1)S(1)}, bf16[16,128,128]{2,1,0:T(8,128)(2,1)S(1)}, u32[]{:S(2)}, u32[]{:S(2)}) collective-permute-start(bf16[16,128,128]{2,1,0:T(8,128)(2,1)S(1)} %all_to_all.33.mine_ref), channel_id=1, source_target_pairs={{0,1},{1,0},{2,3},{3,2},{4,5},{5,4},{6,7},{7,6},{8,9},{9,8},{10,11... | collective-permute-start | bytes 1572872 | tf_op jit(solution)/shard_map/ppermute | solution.py:289

commit v7 on v6

--- a/solution.py
+++ b/solution.py
@@ -37,10 +37,25 @@
     )(*(pltpu.with_memory_space_constraint(*pair) for pair in zip(args, in_spaces)))
 
 
+def contract_rows(left, right):
+    return lax.dot_general(
+        left, right, (((0,), (0,)), ((), ())), preferred_element_type=jnp.float32
+    )
+
+
+def bf16_terms(block):
+    terms = []
+    for _ in range(3):
+        terms.append(block.astype(jnp.bfloat16))
+        block = block - terms[-1].astype(jnp.float32)
+    return terms
+
+
 def gram_of(block):
-    return lax.dot_general(
-        block, block, (((0,), (0,)), ((), ())), precision=HIGHEST, preferred_element_type=jnp.float32
-    )
+    high, middle, low = bf16_terms(block)
+    wide = contract_rows(high, jnp.concatenate([high, middle], axis=1))
+    cross = wide[:, K:] + contract_rows(high, low)
+    return wide[:, :K] + (cross + cross.T + contract_rows(middle, middle))
 
 
 def times_transposed(block, matrix):
@@ -66,14 +81,15 @@
         ]
         for k in range(PANEL):
             j = base + k
-            root = lax.rsqrt(cols[k][0][k : k + 1, :])
-            left_row = left[b][k : k + 1, :] * root
-            right_row = right[b][k : k + 1, :] * root
-            upper_ref[j : j + 1, :] = jnp.where(lane[:1] >= j, left_row, 0.0)
-            inverse_ref[j : j + 1, :] = right_row
-            left_row = left_row * root
-            right_row = right_row * root
-            heads = [cols[m][0][k : k + 1, :] * (root * root) for m in range(k + 1, PANEL)]
+            pivot = cols[k][0][k : k + 1, :]
+            root, reciprocal = lax.rsqrt(pivot), 1.0 / pivot
+            left_row = left[b][k : k + 1, :]
+            right_row = right[b][k : k + 1, :]
+            upper_ref[j : j + 1, :] = jnp.where(lane[:1] >= j, left_row * root, 0.0)
+            inverse_ref[j : j + 1, :] = right_row * root
+            left_row = left_row * reciprocal
+            right_row = right_row * reciprocal
+            heads = [cols[m][0][k : k + 1, :] * reciprocal for m in range(k + 1, PANEL)]
             for i in range(b, count):
                 col = cols[k][i - b]
                 if i == b:
@@ -124,17 +140,13 @@
     return value.reshape(-1, value.shape[-1])
 
 
-def contract_rows(left, right):
-    return lax.dot_general(
-        left, right, (((0,), (0,)), ((), ())), preferred_element_type=jnp.float32
-    )
-
-
-def store_row_blocks(product, first, out_ref):
+def store_row_blocks(product, first, out_ref, base_ref=None):
     rows = out_ref.shape[1]
     for i in range(product.shape[1] // rows):
-        block = product[:, i * rows : (i + 1) * rows]
-        out_ref[first + i] = block.T.astype(out_ref.dtype)
+        block = product[:, i * rows : (i + 1) * rows].T
+        if base_ref is not None:
+            block = block + base_ref[first + i]
+        out_ref[first + i] = block.astype(out_ref.dtype)
 
 
 def pair_half():
@@ -142,82 +154,92 @@
     return lax.rem(row + lax.div(row, 4), 2)
 
 
+def stream_columns(matrix_ref, half, kept_ref, sems):
+    width = kept_ref.shape[-1]
+    columns = pl.ds(pl.multiple_of(half * width, width), width)
+    copies = []
+    for n in range(matrix_ref.shape[0] // PLANES):
+        part = pl.ds(n * PLANES, PLANES)
+        copies.append(
+            pltpu.make_async_copy(
+                matrix_ref.at[part, :, :, columns], kept_ref.at[part], sems.at[n]
+            )
+        )
+        copies[-1].start()
+    return copies
+
+
 def start_kernel(
-    matrix_ref, start_ref, bound_ref, other_ref, mine_ref, own_ref, kept_ref, scale_ref,
-    vectors_ref, total_ref, matrix_sems, start_sems,
+    matrix_ref, start_ref, bound_ref, out_ref, vectors_ref, own_ref, kept_ref, scale_ref,
+    whole_ref, total_ref, matrix_sems, start_sems,
 ):
-    pieces = []
-    for i in range(0, matrix_ref.shape[0], PLANES):
-        part, n = pl.ds(i, PLANES), i // PLANES
-        copies = (
-            pltpu.make_async_copy(start_ref.at[part], vectors_ref.at[part], start_sems.at[n]),
-            pltpu.make_async_copy(matrix_ref.at[part], kept_ref.at[part], matrix_sems.at[n]),
+    start_copies = []
+    for n in range(start_ref.shape[0] // PLANES):
+        part = pl.ds(n * PLANES, PLANES)
+        start_copies.append(
+            pltpu.make_async_copy(start_ref.at[part], whole_ref.at[part], start_sems.at[n])
         )
-        for copy in copies:
-            copy.start()
-        pieces.append(copies)
+        start_copies[-1].start()
+    matrix_copies = stream_columns(matrix_ref, 1 - pair_half(), kept_ref, matrix_sems)
     scale_ref[...] = 1.0 / jnp.full(scale_ref.shape, bound_ref[0], jnp.float32)
-    for n, copies in enumerate(pieces):
-        for copy in copies:
-            copy.wait()
+    for n, copies in enumerate(zip(start_copies, matrix_copies)):
         part = slice(n * PLANES, (n + 1) * PLANES)
-        vectors = vectors_ref[part].astype(jnp.bfloat16).reshape(-1, K)
-        product = contract_rows(vectors, kept_ref[part].reshape(-1, kept_ref.shape[-1]))
+        copies[0].wait()
+        vectors = whole_ref[part].astype(jnp.bfloat16)
+        vectors_ref[part] = vectors
+        copies[1].wait()
+        product = contract_rows(flat(vectors), flat(kept_ref[part]))
         total_ref[...] = product if n == 0 else total_ref[...] + product
-    half = total_ref.shape[1] // 2
-    for own in (0, 1):
-
-        @pl.when(pair_half() == own)
-        def _():
-            store_row_blocks(total_ref[:, own * half : (own + 1) * half], 0, mine_ref)
-            store_row_blocks(total_ref[:, (1 - own) * half : (2 - own) * half], 0, other_ref)
-
+    store_row_blocks(total_ref[...], 0, out_ref)
     plane = lax.axis_index("x") * lax.axis_size("y") + lax.axis_index("y")
-    own_ref[...] = vectors_ref[plane, lax.axis_index("core")]
-
-
-def even_kernel(offset, matrix_ref, mine_ref, other_ref, out_ref):
-    core = lax.axis_index("core")
-    mine, other = flat(mine_ref[...]), flat(other_ref[...])
-    half = matrix_ref.shape[-1] // 2
-    for own in (0, 1):
-
-        @pl.when(pair_half() == own)
-        def _():
-            base = (own ^ offset) * half
-            for i in range(0, half, COLUMNS):
-                lanes = slice(base + i, base + i + COLUMNS)
-                product = contract_rows(mine, flat(matrix_ref[:, core, :, lanes]))
-                product = product + contract_rows(other, flat(matrix_ref[:, 1 - core, :, lanes]))
-                store_row_blocks(product, i // out_ref.shape[1], out_ref)
-
-
-def odd_half(offset, column_offset, matrix_ref, vectors_ref, base_ref, out_ref):
+    own_ref[...] = whole_ref[plane, lax.axis_index("core")]
+
+
+def start_own_kernel(matrix_ref, vectors_ref, out_ref, kept_ref, total_ref, sems):
+    for n, copy in enumerate(stream_columns(matrix_ref, pair_half(), kept_ref, sems)):
+        part = slice(n * PLANES, (n + 1) * PLANES)
+        copy.wait()
+        product = contract_rows(flat(vectors_ref[part]), flat(kept_ref[part]))
+        total_ref[...] = product if n == 0 else total_ref[...] + product
+    store_row_blocks(total_ref[...], 0, out_ref)
+
+
+def even_product(matrix_ref, rows, vectors, base_ref, out_ref):
+    for i in range(0, matrix_ref.shape[-1], COLUMNS):
+        product = contract_rows(vectors, flat(matrix_ref[:, rows, :, i : i + COLUMNS]))
+        store_row_blocks(product, i // out_ref.shape[1], out_ref, base_ref)
+
+
+def even_first_kernel(pair_ref, matrix_ref, vectors_ref, pair_out_ref, out_ref):
+    core, vectors = lax.axis_index("core"), flat(vectors_ref[...])
+    even_product(pair_ref, core, vectors, None, pair_out_ref)
+    even_product(matrix_ref, core, vectors, None, out_ref)
+
+
+def even_last_kernel(matrix_ref, vectors_ref, base_ref, out_ref):
+    even_product(matrix_ref, 1 - lax.axis_index("core"), flat(vectors_ref[...]), base_ref, out_ref)
+
+
+def odd_product(offset, matrix_ref, vectors_ref, base_ref, out_ref):
     core = lax.axis_index("core")
     which = core if offset == 0 else 1 - core
     vectors = flat(vectors_ref[...])
-    half = matrix_ref.shape[-1] // 2
-    for own in (0, 1):
-
-        @pl.when(pair_half() == own)
-        def _():
-            base = (own ^ column_offset) * half
-            for i in range(0, out_ref.shape[0], CHUNKS):
-                rows = flat(matrix_ref[i : i + CHUNKS, which, :, base : base + half])
-                product = jnp.dot(rows, vectors, preferred_element_type=jnp.float32)
-                product = product.reshape(CHUNKS, -1, K)
-                if base_ref is not None:
-                    product = product + base_ref[i : i + CHUNKS]
-                out_ref[i : i + CHUNKS] = product.astype(out_ref.dtype)
+    for i in range(0, out_ref.shape[0], CHUNKS):
+        rows = flat(matrix_ref[i : i + CHUNKS, which])
+        product = jnp.dot(rows, vectors, preferred_element_type=jnp.float32)
+        product = product.reshape(CHUNKS, -1, K)
+        if base_ref is not None:
+            product = product + base_ref[i : i + CHUNKS]
+        out_ref[i : i + CHUNKS] = product.astype(out_ref.dtype)
 
 
 def odd_first_kernel(matrix_ref, vectors_ref, other_ref, mine_ref):
-    odd_half(1, 0, matrix_ref, vectors_ref, None, other_ref)
-    odd_half(0, 0, matrix_ref, vectors_ref, None, mine_ref)
+    odd_product(1, matrix_ref, vectors_ref, None, other_ref)
+    odd_product(0, matrix_ref, vectors_ref, None, mine_ref)
 
 
 def odd_last_kernel(offset, matrix_ref, vectors_ref, base_ref, out_ref):
-    odd_half(offset, 1, matrix_ref, vectors_ref, base_ref, out_ref)
+    odd_product(offset, matrix_ref, vectors_ref, base_ref, out_ref)
 
 
 def pair_kernel(mine_ref, received_ref, out_ref):
@@ -259,9 +281,14 @@
     return total
 
 
-def first_gram_kernel(mine_ref, other_ref, out_ref):
-    mine, other = flat(mine_ref[...]), flat(other_ref[...])
-    pack(contract_rows(mine, mine) + contract_rows(other, other), out_ref)
+def own_gram_kernel(mine_ref, out_ref):
+    mine = flat(mine_ref[...])
+    out_ref[...] = contract_rows(mine, mine)
+
+
+def first_gram_kernel(gram_ref, other_ref, out_ref):
+    other = flat(other_ref[...])
+    pack(gram_ref[...] + contract_rows(other, other), out_ref)
 
 
 def second_gram_kernel(parts_ref, mine_ref, other_ref, out_ref, upper_ref, inverse_ref):
@@ -304,17 +331,20 @@
     row_count = lax.axis_size("row")
     plane_count = lax.axis_size("x") * lax.axis_size("y")
     share = block_rows // (2 * plane_count)
-    matrix = hamiltonian.reshape(plane_count, 2, share, block_cols)
+    whole = hamiltonian.reshape(plane_count, 2, share, block_cols)
     start = start_block.reshape(plane_count, 2, share, K)
     rows = (plane_count, share, K)
-    columns = (block_cols // (2 * share), share, K)
+    half = (block_cols // (2 * share), share, K)
+    kept = ((plane_count, 2, share, block_cols // 2), bf16)
+
+    pieces = plane_count // PLANES
 
     def sum_rows(other, mine_of, previous=None):
         received = swap_row(other, 1)
-        (own,) = local_call(pair_kernel, [(columns, bf16)], mine_of(), received, name="pair_row")
+        (own,) = local_call(pair_kernel, [(half, bf16)], mine_of(), received, name="pair_row")
         parts = [own, *(swap_row(own, mask) for mask in (2, 5, 7))]
         first = previous is None
-        types = [(columns, f32)] * first + [(columns, bf16)]
+        types = [(half, f32)] * first + [(half, bf16)]
         args = parts if first else [*parts, previous]
         kernel = functools.partial(four_sum_kernel, first)
         return local_call(kernel, types, scale, *args, name="four_sum")
@@ -325,11 +355,9 @@
             odd_first_kernel, [(rows, f32), (rows, f32)], matrix, own, name="odd_first"
         )
         kernels = [functools.partial(odd_last_kernel, offset) for offset in (0, 1)]
-        (other,) = local_call(
-            kernels[1], [(rows, bf16)], matrix, received, other, name="odd_other"
-        )
+        (other,) = local_call(kernels[1], [(rows, bf16)], matrix_pair, received, other, name="odd_other")
         swapped = swap_core(other)
-        (mine,) = local_call(kernels[0], [(rows, f32)], matrix, received, mine, name="odd_mine")
+        (mine,) = local_call(kernels[0], [(rows, f32)], matrix_pair, received, mine, name="odd_mine")
         (pair,) = local_call(pair_kernel, [(rows, bf16)], mine, swapped, name="pair_core")
         return exchange(pair, PLANE)
 
@@ -337,34 +365,46 @@
         types = [(previous.shape, f32)] * keep + [(parts.shape, bf16)]
         return local_call(next_share_kernel, types, scale, parts, previous, name="next_share")
 
-    pieces = plane_count // PLANES
-    other, mine, zeroth, matrix, scale = local_call(
+    other, vectors, zeroth, matrix_pair, scale = local_call(
         start_kernel,
-        [(columns, f32), (columns, f32), ((share, K), f32), (matrix.shape, bf16), ((8, K), f32)],
-        matrix, start, spectral_bound, name="start", in_spaces=[pltpu.HBM, pltpu.HBM, pltpu.SMEM],
+        [(half, f32), (start.shape, bf16), ((share, K), f32), kept, ((8, K), f32)],
+        whole, start, spectral_bound, name="start",
+        in_spaces=[pltpu.HBM, pltpu.HBM, pltpu.SMEM],
         scratch_shapes=[
-            pltpu.VMEM(start.shape, f32), pltpu.VMEM((K, block_cols), f32),
+            pltpu.VMEM(start.shape, f32), pltpu.VMEM((K, block_cols // 2), f32),
             pltpu.SemaphoreType.DMA((pieces,)), pltpu.SemaphoreType.DMA((pieces,)),
+        ],
+    )
+    mine, matrix = local_call(
+        start_own_kernel, [(half, f32), kept], whole, vectors, name="start_own",
+        in_spaces=[pltpu.HBM, pltpu.VMEM],
+        scratch_shapes=[
+            pltpu.VMEM((K, block_cols // 2), f32), pltpu.SemaphoreType.DMA((pieces,)),
         ],
     )
     first, vectors = sum_rows(other, lambda: mine)
     second, copies = next_share(odd_parts(vectors), zeroth, True)
     own = exchange(copies, PLANE)
     swapped = swap_core(own)
-
-    def even_part(offset):
-        kernel = functools.partial(even_kernel, offset)
-        dtype = bf16 if offset else f32
-        return local_call(kernel, [(columns, dtype)], matrix, own, swapped, name="even")[0]
-
-    (vectors,) = sum_rows(even_part(1), lambda: even_part(0), first)
+    other, mine = local_call(
+        even_first_kernel, [(half, f32), (half, f32)], matrix_pair, matrix, own, name="even_first"
+    )
+
+    def even_last(half_matrix, base, dtype):
+        return local_call(
+            even_last_kernel, [(half, dtype)], half_matrix, swapped, base, name="even_last"
+        )[0]
+
+    other = even_last(matrix_pair, other, bf16)
+    (vectors,) = sum_rows(other, lambda: even_last(matrix, mine, f32), first)
     (copies,) = next_share(odd_parts(vectors), second, False)
 
     mine = exchange(copies, PLANE)
     other = swap_core(mine)
+    square = ((K, K), f32)
+    (gram,) = local_call(own_gram_kernel, [square], mine, name="own_gram")
     packed = ((row_count, PACK, K), f32)
-    square = ((K, K), f32)
-    (parts,) = local_call(first_gram_kernel, [packed], mine, other, name="first_gram")
+    (parts,) = local_call(first_gram_kernel, [packed], gram, other, name="first_gram")
     parts, upper, inverse = local_call(
         second_gram_kernel, [packed, square, square], exchange(parts, "row"), mine, other,
         name="second_gram",

time: 182 us -> 178 us (0.978)
  waiting for transfers between devices: 39.6 us -> 36.7 us
    pallas_call x20 -> x23, Pallas kernels: 25 us -> 24.2 us  [local_call(): pl.pallas_call(kernel, in_specs=[pl.BlockSpec(memory_space=space) for spa...]
  transfers between devices with their start and end apart: 14 -> 14, of which waited for: 13 -> 13; matrix products, arithmetic and copies ran while one was open for 0% -> 0% of each run, Pallas kernels for 3% -> 5%
where the time goes in v7:
time: 178 us; the launch traced here: 177 us
  blocking collectives  85.5 us (48%)
  waiting for transfers between devices  36.7 us (21%)
  starting transfers between devices  29.7 us (17%)
  Pallas kernels  24.2 us (14%)
    all_to_all x6, blocking collectives, exchange(): return lax.all_to_all(blocks, axes, 0, 0, tiled=True)  85.5 us
    ppermute x10, waiting for transfers between devices, swap_row(): return lax.ppermute(block, 'row', [(i, i ^ mask) for i in range(count)])  33.2 us
    pallas_call x23, Pallas kernels, local_call(): pl.pallas_call(kernel, in_specs=[pl.BlockSpec(memory_space=space) for spa...  24.2 us
    ppermute x10, starting transfers between devices, swap_row(): return lax.ppermute(block, 'row', [(i, i ^ mask) for i in range(count)])  17 us
    ppermute x4, starting transfers between devices, swap_core(): return lax.ppermute(block, 'core', ((0, 1), (1, 0)))  12.7 us
  transfers between devices with their start and end apart: 14, of which 13 were waited for; matrix products, arithmetic and copies ran while one was open for 0% of the time, Pallas kernels for 5%

profile of v7, /device:TPU:1, one launch (start us, length us, event | category | flops | bytes accessed | tf_op | source)
XLA Modules:
  0.0 177.5 jit_solution(17408307919825403081)
XLA Ops:
  1.3 3.3 %start.1 = (f32[4,128,128]{2,1,0:T(8,128)S(1)}, bf16[16,2,128,128]{3,2,1,0:T(8,128)(2,1)S(1)}, f32[128,128]{1,0:T(8,128)S(1)}, bf16[16,2,128,512]{3,2,1,0:T(8,128)(2,1)S(1)}, f32[8,128]{1,0:T(8,128)S(1)}) custom-call(bf16[16,2,128,1024]{3,2,1,0:T(8,128)(2,1)} %bitcast.2, f32[16,2,128,128]{3,2,1,0:T(8,128)} %bitcast.4, f32[1]{0:T(128)S(6)} %copy.5.bound_ref), custom_call_target="tpu_custom_call" | custom-call | tf_op jit(solution)/shard_map/start/pallas_call | solution.py:29
  4.6 2.6 %collective-permute-start = (f32[4,128,128]{2,1,0:T(8,128)S(1)}, f32[4,128,128]{2,1,0:T(8,128)S(1)}, u32[]{:S(2)}, u32[]{:S(2)}) collective-permute-start(f32[4,128,128]{2,1,0:T(8,128)S(1)} %get-tuple-element.27), channel_id=1, source_target_pairs={{0,32},{32,0},{64,96},{96,64},{128,160},{160,128},{192,224},{224,1... | collective-permute-start | bytes 786440 | tf_op jit(solution)/shard_map/ppermute | solution.py:321
  7.1 2.6 %start_own.1 = (f32[4,128,128]{2,1,0:T(8,128)S(1)}, bf16[16,2,128,512]{3,2,1,0:T(8,128)(2,1)S(1)}) custom-call(bf16[16,2,128,1024]{3,2,1,0:T(8,128)(2,1)} %bitcast.3, bf16[16,2,128,128]{3,2,1,0:T(8,128)(2,1)S(1)} %get-tuple-element.24.vectors_ref), custom_call_target="tpu_custom_call" | custom-call | tf_op jit(solution)/shard_map/start_own/pallas_call | solution.py:29
  9.7 2.4 %collective-permute-done.received_ref = f32[4,128,128]{2,1,0:T(8,128)S(1)} collective-permute-done((f32[4,128,128]{2,1,0:T(8,128)S(1)}, f32[4,128,128]{2,1,0:T(8,128)S(1)}, u32[]{:S(2)}, u32[]{:S(2)}) %collective-permute-start) | collective-permute-done | bytes 262176 | tf_op jit(solution)/shard_map/ppermute | solution.py:321
  12.1 4.0 %collective-permute-start.1 = (bf16[4,128,128]{2,1,0:T(8,128)(2,1)S(1)}, bf16[4,128,128]{2,1,0:T(8,128)(2,1)S(1)}, u32[]{:S(2)}, u32[]{:S(2)}) collective-permute-start(bf16[4,128,128]{2,1,0:T(8,128)(2,1)S(1)} %pair_row.2.own_ref), channel_id=1, source_target_pairs={{0,64},{32,96},{64,0},{96,32},{128,192},{160,224},{192,128},{224,1... | collective-permute-start | bytes 393224 | tf_op jit(solution)/shard_map/ppermute | solution.py:321
  16.1 4.3 %collective-permute-start.2 = (bf16[4,128,128]{2,1,0:T(8,128)(2,1)S(1)}, bf16[4,128,128]{2,1,0:T(8,128)(2,1)S(1)}, u32[]{:S(2)}, u32[]{:S(2)}) collective-permute-start(bf16[4,128,128]{2,1,0:T(8,128)(2,1)S(1)} %pair_row.2.own_ref), channel_id=1, source_target_pairs={{0,160},{32,128},{64,224},{96,192},{128,32},{160,0},{192,96},{224,... | collective-permute-start | bytes 393224 | tf_op jit(solution)/shard_map/ppermute | solution.py:321
  20.4 1.4 collective-permute-done.1.two_ref
  21.9 10.2 %collective-permute-done.2.five_ref = bf16[4,128,128]{2,1,0:T(8,128)(2,1)S(1)} collective-permute-done((bf16[4,128,128]{2,1,0:T(8,128)(2,1)S(1)}, bf16[4,128,128]{2,1,0:T(8,128)(2,1)S(1)}, u32[]{:S(2)}, u32[]{:S(2)}) %collective-permute-start.2) | collective-permute-done | bytes 131104 | tf_op jit(solution)/shard_map/ppermute | solution.py:321
  32.2 1.2 odd_first.2
  33.4 2.6 %collective-permute-done.4.vectors_ref = bf16[4,128,128]{2,1,0:T(8,128)(2,1)S(1)} collective-permute-done((bf16[4,128,128]{2,1,0:T(8,128)(2,1)S(1)}, bf16[4,128,128]{2,1,0:T(8,128)(2,1)S(1)}, u32[]{:S(2)}, u32[]{:S(2)}) %collective-permute-start.4) | collective-permute-done | bytes 131104 | tf_op jit(solution)/shard_map/ppermute | solution.py:321
  36.0 0.7 odd_other.2
  36.7 2.8 %collective-permute-start.5 = (bf16[16,128,128]{2,1,0:T(8,128)(2,1)S(1)}, bf16[16,128,128]{2,1,0:T(8,128)(2,1)S(1)}, u32[]{:S(2)}, u32[]{:S(2)}) collective-permute-start(bf16[16,128,128]{2,1,0:T(8,128)(2,1)S(1)} %odd_other.2), channel_id=1, source_target_pairs={{0,1},{1,0},{2,3},{3,2},{4,5},{5,4},{6,7},{7,6},{8,9},{9,8},{10,11... | collective-permute-start | bytes 1572872 | tf_op jit(solution)/shard_map/ppermute | solution.py:316
  39.6 0.7 odd_mine.2.mine_ref
  40.3 0.8 collective-permute-done.5.received_ref
  41.2 16.9 %all_to_all.30.parts_ref = bf16[16,128,128]{2,1,0:T(8,128)(2,1)S(1)} all-to-all(bf16[16,128,128]{2,1,0:T(8,128)(2,1)S(1)} %pair_core.2), channel_id=1, replica_groups=mesh['row'=8,'x'=4,'y'=4,'core'=2] {'x','y'}, dimensions={0} | all-to-all | bytes 1048576 | tf_op jit(solution)/shard_map/all_to_all | solution.py:325
  58.1 0.1 next_share.2
  58.2 12.7 %all_to_all.31.vectors_ref = bf16[16,128,128]{2,1,0:T(8,128)(2,1)S(1)} all-to-all(bf16[16,128,128]{2,1,0:T(8,128)(2,1)S(1)} %get-tuple-element.32), channel_id=1, replica_groups=mesh['row'=8,'x'=4,'y'=4,'core'=2] {'x','y'}, dimensions={0} | all-to-all | bytes 1048576 | tf_op jit(solution)/shard_map/all_to_all | solution.py:325
  70.9 3.3 %collective-permute-start.6 = (bf16[16,128,128]{2,1,0:T(8,128)(2,1)S(1)}, bf16[16,128,128]{2,1,0:T(8,128)(2,1)S(1)}, u32[]{:S(2)}, u32[]{:S(2)}) collective-permute-start(bf16[16,128,128]{2,1,0:T(8,128)(2,1)S(1)} %all_to_all.31.vectors_ref), channel_id=1, source_target_pairs={{0,1},{1,0},{2,3},{3,2},{4,5},{5,4},{6,7},{7,6},{8,9},{9,8},{10,11... | collective-permute-start | bytes 1572872 | tf_op jit(solution)/shard_map/ppermute | solution.py:316
  74.2 0.8 even_first.1
  75.0 0.7 collective-permute-done.6.vectors_ref
  75.7 0.6 even_last.3
  76.3 1.1 collective-permute-start.7
  77.4 0.6 even_last.2.mine_ref
  77.9 3.1 %collective-permute-done.7.received_ref = bf16[4,128,128]{2,1,0:T(8,128)(2,1)S(1)} collective-permute-done((bf16[4,128,128]{2,1,0:T(8,128)(2,1)S(1)}, bf16[4,128,128]{2,1,0:T(8,128)(2,1)S(1)}, u32[]{:S(2)}, u32[]{:S(2)}) %collective-permute-start.7) | collective-permute-done | bytes 131104 | tf_op jit(solution)/shard_map/ppermute | solution.py:321
  81.1 2.5 %collective-permute-start.10 = (bf16[4,128,128]{2,1,0:T(8,128)(2,1)S(1)}, bf16[4,128,128]{2,1,0:T(8,128)(2,1)S(1)}, u32[]{:S(2)}, u32[]{:S(2)}) collective-permute-start(bf16[4,128,128]{2,1,0:T(8,128)(2,1)S(1)} %pair_row.3.own_ref), channel_id=1, source_target_pairs={{0,224},{32,192},{64,160},{96,128},{128,96},{160,64},{192,32},{224... | collective-permute-start | bytes 393224 | tf_op jit(solution)/shard_map/ppermute | solution.py:321
  83.6 1.3 collective-permute-start.8
  84.9 1.0 collective-permute-start.9
  86.0 1.7 collective-permute-done.10.seven_ref
  87.6 1.1 collective-permute-done.8.two_ref
  88.7 8.2 %collective-permute-done.9.five_ref = bf16[4,128,128]{2,1,0:T(8,128)(2,1)S(1)} collective-permute-done((bf16[4,128,128]{2,1,0:T(8,128)(2,1)S(1)}, bf16[4,128,128]{2,1,0:T(8,128)(2,1)S(1)}, u32[]{:S(2)}, u32[]{:S(2)}) %collective-permute-start.9) | collective-permute-done | bytes 131104 | tf_op jit(solution)/shard_map/ppermute | solution.py:321
  97.0 0.1 collective-permute-start.11
  97.1 1.2 odd_first.3
  98.4 2.6 %collective-permute-done.11.vectors_ref = bf16[4,128,128]{2,1,0:T(8,128)(2,1)S(1)} collective-permute-done((bf16[4,128,128]{2,1,0:T(8,128)(2,1)S(1)}, bf16[4,128,128]{2,1,0:T(8,128)(2,1)S(1)}, u32[]{:S(2)}, u32[]{:S(2)}) %collective-permute-start.11) | collective-permute-done | bytes 131104 | tf_op jit(solution)/shard_map/ppermute | solution.py:321
  100.9 0.7 odd_other.3
  101.6 3.3 %collective-permute-start.12 = (bf16[16,128,128]{2,1,0:T(8,128)(2,1)S(1)}, bf16[16,128,128]{2,1,0:T(8,128)(2,1)S(1)}, u32[]{:S(2)}, u32[]{:S(2)}) collective-permute-start(bf16[16,128,128]{2,1,0:T(8,128)(2,1)S(1)} %odd_other.3), channel_id=1, source_target_pairs={{0,1},{1,0},{2,3},{3,2},{4,5},{5,4},{6,7},{7,6},{8,9},{9,8},{10,11... | collective-permute-start | bytes 1572872 | tf_op jit(solution)/shard_map/ppermute | solution.py:316
  105.0 0.7 odd_mine.3.mine_ref
  105.7 0.8 collective-permute-done.12.received_ref
  106.6 13.3 %all_to_all.32.parts_ref = bf16[16,128,128]{2,1,0:T(8,128)(2,1)S(1)} all-to-all(bf16[16,128,128]{2,1,0:T(8,128)(2,1)S(1)} %pair_core.3), channel_id=1, replica_groups=mesh['row'=8,'x'=4,'y'=4,'core'=2] {'x','y'}, dimensions={0} | all-to-all | bytes 1048576 | tf_op jit(solution)/shard_map/all_to_all | solution.py:325
  119.9 0.1 next_share.3.block_ref
  120.0 12.7 %all_to_all.33.mine_ref = bf16[16,128,128]{2,1,0:T(8,128)(2,1)S(1)} all-to-all(bf16[16,128,128]{2,1,0:T(8,128)(2,1)S(1)} %next_share.3.block_ref), channel_id=1, replica_groups=mesh['row'=8,'x'=4,'y'=4,'core'=2] {'x','y'}, dimensions={0} | all-to-all | bytes 1048576 | tf_op jit(solution)/shard_map/all_to_all | solution.py:325
  132.8 3.3 %collective-permute-start.13 = (bf16[16,128,128]{2,1,0:T(8,128)(2,1)S(1)}, bf16[16,128,128]{2,1,0:T(8,128)(2,1)S(1)}, u32[]{:S(2)}, u32[]{:S(2)}) collective-permute-start(bf16[16,128,128]{2,1,0:T(8,128)(2,1)S(1)} %all_to_all.33.mine_ref), channel_id=1, source_target_pairs={{0,1},{1,0},{2,3},{3,2},{4,5},{5,4},{6,7},{7,6},{8,9},{9,8},{10,11... | collective-permute-start | bytes 1572872 | tf_op jit(solution)/shard_map/ppermute | solution.py:316
  136.0 0.3 own_gram.1.gram_ref
  136.4 1.2 collective-permute-done.13.other_ref
  137.6 0.4 first_gram.1
  138.0 16.8 %all_to_all.34.parts_ref = f32[8,72,128]{2,1,0:T(8,128)S(1)} all-to-all(f32[8,72,128]{2,1,0:T(8,128)S(1)} %first_gram.1), channel_id=1, replica_groups=mesh['row'=8,'x'=4,'y'=4,'core'=2] {'row'}, dimensions={0} | all-to-all | bytes 589824 | tf_op jit(solution)/shard_map/all_to_all | solution.py:325
  154.7 5.1 %second_gram.1 = (f32[8,72,128]{2,1,0:T(8,128)S(1)}, f32[128,128]{1,0:T(8,128)S(1)}, f32[128,128]{1,0:T(8,128)S(1)}) custom-call(f32[8,72,128]{2,1,0:T(8,128)S(1)} %all_to_all.34.parts_ref, bf16[16,128,128]{2,1,0:T(8,128)(2,1)S(1)} %all_to_all.33.mine_ref, bf16[16,128,128]{2,1,0:T(8,128)(2,1)S(1)} %collective-permute-done.13.other_ref), custom_call_target="tpu_custom_call" | custom-call | tf_op jit(solution)/shard_map/second_gram/pallas_call | solution.py:29
  159.9 13.0 %all_to_all.35.parts_ref = f32[8,72,128]{2,1,0:T(8,128)S(1)} all-to-all(f32[8,72,128]{2,1,0:T(8,128)S(1)} %get-tuple-element.39), channel_id=1, replica_groups=mesh['row'=8,'x'=4,'y'=4,'core'=2] {'row'}, dimensions={0} | all-to-all | bytes 589824 | tf_op jit(solution)/shard_map/all_to_all | solution.py:325
  172.9 4.6 %last.1 = (f32[128,128]{1,0:T(8,128)}, f32[128,128]{1,0:T(8,128)}) custom-call(f32[8,72,128]{2,1,0:T(8,128)S(1)} %all_to_all.35.parts_ref, f32[128,128]{1,0:T(8,128)S(1)} %get-tuple-element.40.upper_one_ref, f32[128,128]{1,0:T(8,128)S(1)} %get-tuple-element.41.inverse_one_ref, bf16[16,128,128]{2,1,0:T(8,128)(2,1)S(1)} %next_share.3.block_ref), custom_call_target="tpu_custom_call" | custom-call | tf_op jit(solution)/shard_map/last/pallas_call | solution.py:29
  (9 shorter events, 0.5 us)
Async XLA Ops:
  4.6 7.5 %collective-permute-start = (f32[4,128,128]{2,1,0:T(8,128)S(1)}, f32[4,128,128]{2,1,0:T(8,128)S(1)}, u32[]{:S(2)}, u32[]{:S(2)}) collective-permute-start(f32[4,128,128]{2,1,0:T(8,128)S(1)} %get-tuple-element.27), channel_id=1, source_target_pairs={{0,32},{32,0},{64,96},{96,64},{128,160},{160,128},{192,224},{224,1... | collective-permute-start | bytes 786440 | tf_op jit(solution)/shard_map/ppermute | solution.py:321
  12.1 9.7 %collective-permute-start.1 = (bf16[4,128,128]{2,1,0:T(8,128)(2,1)S(1)}, bf16[4,128,128]{2,1,0:T(8,128)(2,1)S(1)}, u32[]{:S(2)}, u32[]{:S(2)}) collective-permute-start(bf16[4,128,128]{2,1,0:T(8,128)(2,1)S(1)} %pair_row.2.own_ref), channel_id=1, source_target_pairs={{0,64},{32,96},{64,0},{96,32},{128,192},{160,224},{192,128},{224,1... | collective-permute-start | bytes 393224 | tf_op jit(solution)/shard_map/ppermute | solution.py:321
  16.1 15.9 %collective-permute-start.2 = (bf16[4,128,128]{2,1,0:T(8,128)(2,1)S(1)}, bf16[4,128,128]{2,1,0:T(8,128)(2,1)S(1)}, u32[]{:S(2)}, u32[]{:S(2)}) collective-permute-start(bf16[4,128,128]{2,1,0:T(8,128)(2,1)S(1)} %pair_row.2.own_ref), channel_id=1, source_target_pairs={{0,160},{32,128},{64,224},{96,192},{128,32},{160,0},{192,96},{224,... | collective-permute-start | bytes 393224 | tf_op jit(solution)/shard_map/ppermute | solution.py:321
  20.4 11.6 %collective-permute-start.3 = (bf16[4,128,128]{2,1,0:T(8,128)(2,1)S(1)}, bf16[4,128,128]{2,1,0:T(8,128)(2,1)S(1)}, u32[]{:S(2)}, u32[]{:S(2)}) collective-permute-start(bf16[4,128,128]{2,1,0:T(8,128)(2,1)S(1)} %pair_row.2.own_ref), channel_id=1, source_target_pairs={{0,224},{32,192},{64,160},{96,128},{128,96},{160,64},{192,32},{224... | collective-permute-start | bytes 393224 | tf_op jit(solution)/shard_map/ppermute | solution.py:321
  32.1 3.9 %collective-permute-start.4 = (bf16[4,128,128]{2,1,0:T(8,128)(2,1)S(1)}, bf16[4,128,128]{2,1,0:T(8,128)(2,1)S(1)}, u32[]{:S(2)}, u32[]{:S(2)}) collective-permute-start(bf16[4,128,128]{2,1,0:T(8,128)(2,1)S(1)} %get-tuple-element.28.vectors_ref), channel_id=1, source_target_pairs={{0,32},{32,0},{64,96},{96,64},{128,160},{160,128},{192,224},{224,1... | collective-permute-start | bytes 393224 | tf_op jit(solution)/shard_map/ppermute | solution.py:321
  36.7 4.4 %collective-permute-start.5 = (bf16[16,128,128]{2,1,0:T(8,128)(2,1)S(1)}, bf16[16,128,128]{2,1,0:T(8,128)(2,1)S(1)}, u32[]{:S(2)}, u32[]{:S(2)}) collective-permute-start(bf16[16,128,128]{2,1,0:T(8,128)(2,1)S(1)} %odd_other.2), channel_id=1, source_target_pairs={{0,1},{1,0},{2,3},{3,2},{4,5},{5,4},{6,7},{7,6},{8,9},{9,8},{10,11... | collective-permute-start | bytes 1572872 | tf_op jit(solution)/shard_map/ppermute | solution.py:316
  70.9 4.8 %collective-permute-start.6 = (bf16[16,128,128]{2,1,0:T(8,128)(2,1)S(1)}, bf16[16,128,128]{2,1,0:T(8,128)(2,1)S(1)}, u32[]{:S(2)}, u32[]{:S(2)}) collective-permute-start(bf16[16,128,128]{2,1,0:T(8,128)(2,1)S(1)} %all_to_all.31.vectors_ref), channel_id=1, source_target_pairs={{0,1},{1,0},{2,3},{3,2},{4,5},{5,4},{6,7},{7,6},{8,9},{9,8},{10,11... | collective-permute-start | bytes 1572872 | tf_op jit(solution)/shard_map/ppermute | solution.py:316
  76.3 4.8 %collective-permute-start.7 = (bf16[4,128,128]{2,1,0:T(8,128)(2,1)S(1)}, bf16[4,128,128]{2,1,0:T(8,128)(2,1)S(1)}, u32[]{:S(2)}, u32[]{:S(2)}) collective-permute-start(bf16[4,128,128]{2,1,0:T(8,128)(2,1)S(1)} %even_last.3), channel_id=1, source_target_pairs={{0,32},{32,0},{64,96},{96,64},{128,160},{160,128},{192,224},{224,1... | collective-permute-start | bytes 393224 | tf_op jit(solution)/shard_map/ppermute | solution.py:321
  81.1 6.5 %collective-permute-start.10 = (bf16[4,128,128]{2,1,0:T(8,128)(2,1)S(1)}, bf16[4,128,128]{2,1,0:T(8,128)(2,1)S(1)}, u32[]{:S(2)}, u32[]{:S(2)}) collective-permute-start(bf16[4,128,128]{2,1,0:T(8,128)(2,1)S(1)} %pair_row.3.own_ref), channel_id=1, source_target_pairs={{0,224},{32,192},{64,160},{96,128},{128,96},{160,64},{192,32},{224... | collective-permute-start | bytes 393224 | tf_op jit(solution)/shard_map/ppermute | solution.py:321
  83.6 5.1 %collective-permute-start.8 = (bf16[4,128,128]{2,1,0:T(8,128)(2,1)S(1)}, bf16[4,128,128]{2,1,0:T(8,128)(2,1)S(1)}, u32[]{:S(2)}, u32[]{:S(2)}) collective-permute-start(bf16[4,128,128]{2,1,0:T(8,128)(2,1)S(1)} %pair_row.3.own_ref), channel_id=1, source_target_pairs={{0,64},{32,96},{64,0},{96,32},{128,192},{160,224},{192,128},{224,1... | collective-permute-start | bytes 393224 | tf_op jit(solution)/shard_map/ppermute | solution.py:321
  84.9 12.0 %collective-permute-start.9 = (bf16[4,128,128]{2,1,0:T(8,128)(2,1)S(1)}, bf16[4,128,128]{2,1,0:T(8,128)(2,1)S(1)}, u32[]{:S(2)}, u32[]{:S(2)}) collective-permute-start(bf16[4,128,128]{2,1,0:T(8,128)(2,1)S(1)} %pair_row.3.own_ref), channel_id=1, source_target_pairs={{0,160},{32,128},{64,224},{96,192},{128,32},{160,0},{192,96},{224,... | collective-permute-start | bytes 393224 | tf_op jit(solution)/shard_map/ppermute | solution.py:321
  97.0 3.9 %collective-permute-start.11 = (bf16[4,128,128]{2,1,0:T(8,128)(2,1)S(1)}, bf16[4,128,128]{2,1,0:T(8,128)(2,1)S(1)}, u32[]{:S(2)}, u32[]{:S(2)}) collective-permute-start(bf16[4,128,128]{2,1,0:T(8,128)(2,1)S(1)} %four_sum.3.vectors_ref), channel_id=1, source_target_pairs={{0,32},{32,0},{64,96},{96,64},{128,160},{160,128},{192,224},{224,1... | collective-permute-start | bytes 393224 | tf_op jit(solution)/shard_map/ppermute | solution.py:321
  101.6 4.9 %collective-permute-start.12 = (bf16[16,128,128]{2,1,0:T(8,128)(2,1)S(1)}, bf16[16,128,128]{2,1,0:T(8,128)(2,1)S(1)}, u32[]{:S(2)}, u32[]{:S(2)}) collective-permute-start(bf16[16,128,128]{2,1,0:T(8,128)(2,1)S(1)} %odd_other.3), channel_id=1, source_target_pairs={{0,1},{1,0},{2,3},{3,2},{4,5},{5,4},{6,7},{7,6},{8,9},{9,8},{10,11... | collective-permute-start | bytes 1572872 | tf_op jit(solution)/shard_map/ppermute | solution.py:316
  132.8 4.8 %collective-permute-start.13 = (bf16[16,128,128]{2,1,0:T(8,128)(2,1)S(1)}, bf16[16,128,128]{2,1,0:T(8,128)(2,1)S(1)}, u32[]{:S(2)}, u32[]{:S(2)}) collective-permute-start(bf16[16,128,128]{2,1,0:T(8,128)(2,1)S(1)} %all_to_all.33.mine_ref), channel_id=1, source_target_pairs={{0,1},{1,0},{2,3},{3,2},{4,5},{5,4},{6,7},{7,6},{8,9},{9,8},{10,11... | collective-permute-start | bytes 1572872 | tf_op jit(solution)/shard_map/ppermute | solution.py:316

commit v8 on v7

--- a/solution.py
+++ b/solution.py
@@ -64,42 +64,51 @@
     )
 
 
+def spread(block, lane):
+    return [jnp.broadcast_to(block[:, lane + k : lane + k + 1], block.shape) for k in range(PANEL)]
+
+
 def factor(gram, upper_ref, inverse_ref):
     count = K // PANEL
     lane = lax.broadcasted_iota(jnp.int32, (PANEL, K), 1)
     sub = lax.broadcasted_iota(jnp.int32, (PANEL, K), 0)
-    left = [gram[i * PANEL : (i + 1) * PANEL, :] for i in range(count)]
-    right = [jnp.where(lane == sub + i * PANEL, 1.0, 0.0).astype(jnp.float32) for i in range(count)]
+    rows = [gram[i * PANEL : (i + 1) * PANEL, :] for i in range(count)]
+    own = spread(rows[0], 0)
     for b in range(count):
         base = b * PANEL
-        cols = [
-            [
-                jnp.broadcast_to(left[i][:, base + k : base + k + 1], (PANEL, K))
-                for i in range(b, count)
-            ]
-            for k in range(PANEL)
-        ]
+        below = range(b + 1, count)
+        cols = {i: spread(rows[i], base) for i in below}
+        left = rows[b]
+        right = jnp.where(lane < base, left, jnp.where(lane == sub + base, 1.0, 0.0))
+        if below:
+            ahead, later = spread(left, base + PANEL), spread(rows[b + 1], base + PANEL)
+        for i in below:
+            rows[i] = jnp.where((lane >= base) & (lane < base + PANEL), 0.0, rows[i])
         for k in range(PANEL):
             j = base + k
-            pivot = cols[k][0][k : k + 1, :]
+            pivot = own[k][k : k + 1, :]
             root, reciprocal = lax.rsqrt(pivot), 1.0 / pivot
-            left_row = left[b][k : k + 1, :]
-            right_row = right[b][k : k + 1, :]
+            left_row, right_row = left[k : k + 1, :], right[k : k + 1, :]
             upper_ref[j : j + 1, :] = jnp.where(lane[:1] >= j, left_row * root, 0.0)
             inverse_ref[j : j + 1, :] = right_row * root
-            left_row = left_row * reciprocal
-            right_row = right_row * reciprocal
-            heads = [cols[m][0][k : k + 1, :] * reciprocal for m in range(k + 1, PANEL)]
-            for i in range(b, count):
-                col = cols[k][i - b]
-                if i == b:
-                    if k == PANEL - 1:
-                        continue
-                    col = jnp.where(sub > k, col, 0.0)
-                for m, head in zip(range(k + 1, PANEL), heads):
-                    cols[m][i - b] = cols[m][i - b] - col * head
-                left[i] = left[i] - col * left_row
-                right[i] = right[i] - col * right_row
+            left_row, right_row = left_row * reciprocal, right_row * reciprocal
+            both = jnp.where(lane[:1] < base + PANEL, right_row, left_row)
+            heads = {m: own[m][k : k + 1, :] * reciprocal for m in range(k + 1, PANEL)}
+            col = jnp.where(sub > k, own[k], 0.0)
+            if below:
+                ahead_heads = [block[k : k + 1, :] * reciprocal for block in ahead]
+                later = [x - cols[b + 1][k] * head for x, head in zip(later, ahead_heads)]
+                ahead = [x - col * head for x, head in zip(ahead, ahead_heads)]
+            for m, head in heads.items():
+                own[m] = own[m] - col * head
+            left, right = left - col * left_row, right - col * right_row
+            for i in below:
+                col = cols[i][k]
+                for m, head in heads.items():
+                    cols[i][m] = cols[i][m] - col * head
+                rows[i] = rows[i] - col * both
+        if below:
+            own = later
 
 
 def grids():
@@ -242,15 +251,15 @@
     odd_product(offset, matrix_ref, vectors_ref, base_ref, out_ref)
 
 
-def pair_kernel(mine_ref, received_ref, out_ref):
-    out_ref[...] = (mine_ref[...] + received_ref[...].astype(jnp.float32)).astype(out_ref.dtype)
+def pair_kernel(mine_ref, received_ref, *out_refs):
+    total = mine_ref[...] + received_ref[...].astype(jnp.float32)
+    for out_ref in out_refs:
+        out_ref[...] = total.astype(out_ref.dtype)
 
 
 def four_sum_kernel(first, scale_ref, own_ref, two_ref, five_ref, seven_ref, *refs):
-    own, two, five, seven = (
-        ref[...].astype(jnp.float32) for ref in (own_ref, two_ref, five_ref, seven_ref)
-    )
-    total = (own + two) + (five + seven)
+    two, five, seven = (ref[...].astype(jnp.float32) for ref in (two_ref, five_ref, seven_ref))
+    total = own_ref[...] + two + (five + seven)
     if first:
         share_ref, rounded_ref = refs
         total = total * scale_ref[:1]
@@ -341,8 +350,10 @@
 
     def sum_rows(other, mine_of, previous=None):
         received = swap_row(other, 1)
-        (own,) = local_call(pair_kernel, [(half, bf16)], mine_of(), received, name="pair_row")
-        parts = [own, *(swap_row(own, mask) for mask in (2, 5, 7))]
+        own, rounded = local_call(
+            pair_kernel, [(half, f32), (half, bf16)], mine_of(), received, name="pair_row"
+        )
+        parts = [own, *(swap_row(rounded, mask) for mask in (2, 5, 7))]
         first = previous is None
         types = [(half, f32)] * first + [(half, bf16)]
         args = parts if first else [*parts, previous]
@@ -367,7 +378,7 @@
 
     other, vectors, zeroth, matrix_pair, scale = local_call(
         start_kernel,
-        [(half, f32), (start.shape, bf16), ((share, K), f32), kept, ((8, K), f32)],
+        [(half, bf16), (start.shape, bf16), ((share, K), f32), kept, ((8, K), f32)],
         whole, start, spectral_bound, name="start",
         in_spaces=[pltpu.HBM, pltpu.HBM, pltpu.SMEM],
         scratch_shapes=[

time: 178 us -> 175 us (0.983)
  waiting for transfers between devices: 36.7 us -> 34.3 us
    ppermute x10, waiting for transfers between devices: 33.2 us -> 30.8 us  [swap_row(): return lax.ppermute(block, 'row', [(i, i ^ mask) for i in range(count)])]
  transfers between devices with their start and end apart: 14 -> 14, of which waited for: 13 -> 12; matrix products, arithmetic and copies ran while one was open for 0% -> 0% of each run, Pallas kernels for 5% -> 5%
where the time goes in v8:
time: 175 us
  blocking collectives  85.5 us (49%)
  waiting for transfers between devices  34.3 us (20%)
  starting transfers between devices  29.2 us (17%)
  Pallas kernels  24.3 us (14%)
    all_to_all x6, blocking collectives, exchange(): return lax.all_to_all(blocks, axes, 0, 0, tiled=True)  85.5 us
    ppermute x10, waiting for transfers between devices, swap_row(): return lax.ppermute(block, 'row', [(i, i ^ mask) for i in range(count)])  30.8 us
    pallas_call x23, Pallas kernels, local_call(): pl.pallas_call(kernel, in_specs=[pl.BlockSpec(memory_space=space) for spa...  24.3 us
    ppermute x10, starting transfers between devices, swap_row(): return lax.ppermute(block, 'row', [(i, i ^ mask) for i in range(count)])  16.5 us
    ppermute x4, starting transfers between devices, swap_core(): return lax.ppermute(block, 'core', ((0, 1), (1, 0)))  12.7 us
    ppermute x4, waiting for transfers between devices, swap_core(): return lax.ppermute(block, 'core', ((0, 1), (1, 0)))  3.52 us
  transfers between devices with their start and end apart: 14, of which 12 were waited for; matrix products, arithmetic and copies ran while one was open for 0% of the time, Pallas kernels for 5%

profile of v8, /device:TPU:1, one launch (start us, length us, event | category | flops | bytes accessed | tf_op | source)
XLA Modules:
  0.0 174.7 jit_solution(9903993620806891561)
XLA Ops:
  1.3 3.2 %start.1 = (bf16[4,128,128]{2,1,0:T(8,128)(2,1)S(1)}, bf16[16,2,128,128]{3,2,1,0:T(8,128)(2,1)S(1)}, f32[128,128]{1,0:T(8,128)S(1)}, bf16[16,2,128,512]{3,2,1,0:T(8,128)(2,1)S(1)}, f32[8,128]{1,0:T(8,128)S(1)}) custom-call(bf16[16,2,128,1024]{3,2,1,0:T(8,128)(2,1)} %bitcast.2, f32[16,2,128,128]{3,2,1,0:T(8,128)} %bitcast.4, f32[1]{0:T(128)S(6)} %copy.5.bound_ref), custom_call_target="tpu_custom_call" | custom-call | tf_op jit(solution)/shard_map/start/pallas_call | solution.py:29
  4.5 2.6 %collective-permute-start = (bf16[4,128,128]{2,1,0:T(8,128)(2,1)S(1)}, bf16[4,128,128]{2,1,0:T(8,128)(2,1)S(1)}, u32[]{:S(2)}, u32[]{:S(2)}) collective-permute-start(bf16[4,128,128]{2,1,0:T(8,128)(2,1)S(1)} %get-tuple-element.31), channel_id=1, source_target_pairs={{0,32},{32,0},{64,96},{96,64},{128,160},{160,128},{192,224},{224,1... | collective-permute-start | bytes 393224 | tf_op jit(solution)/shard_map/ppermute | solution.py:330
  7.1 2.6 %start_own.1 = (f32[4,128,128]{2,1,0:T(8,128)S(1)}, bf16[16,2,128,512]{3,2,1,0:T(8,128)(2,1)S(1)}) custom-call(bf16[16,2,128,1024]{3,2,1,0:T(8,128)(2,1)} %bitcast.3, bf16[16,2,128,128]{3,2,1,0:T(8,128)(2,1)S(1)} %get-tuple-element.28.vectors_ref), custom_call_target="tpu_custom_call" | custom-call | tf_op jit(solution)/shard_map/start_own/pallas_call | solution.py:29
  9.7 3.6 %collective-permute-start.1 = (bf16[4,128,128]{2,1,0:T(8,128)(2,1)S(1)}, bf16[4,128,128]{2,1,0:T(8,128)(2,1)S(1)}, u32[]{:S(2)}, u32[]{:S(2)}) collective-permute-start(bf16[4,128,128]{2,1,0:T(8,128)(2,1)S(1)} %get-tuple-element.33), channel_id=1, source_target_pairs={{0,64},{32,96},{64,0},{96,32},{128,192},{160,224},{192,128},{224,1... | collective-permute-start | bytes 393224 | tf_op jit(solution)/shard_map/ppermute | solution.py:330
  13.3 4.3 %collective-permute-start.2 = (bf16[4,128,128]{2,1,0:T(8,128)(2,1)S(1)}, bf16[4,128,128]{2,1,0:T(8,128)(2,1)S(1)}, u32[]{:S(2)}, u32[]{:S(2)}) collective-permute-start(bf16[4,128,128]{2,1,0:T(8,128)(2,1)S(1)} %get-tuple-element.33), channel_id=1, source_target_pairs={{0,160},{32,128},{64,224},{96,192},{128,32},{160,0},{192,96},{224,... | collective-permute-start | bytes 393224 | tf_op jit(solution)/shard_map/ppermute | solution.py:330
  17.6 1.4 collective-permute-done.1.two_ref
  19.0 10.2 %collective-permute-done.2.five_ref = bf16[4,128,128]{2,1,0:T(8,128)(2,1)S(1)} collective-permute-done((bf16[4,128,128]{2,1,0:T(8,128)(2,1)S(1)}, bf16[4,128,128]{2,1,0:T(8,128)(2,1)S(1)}, u32[]{:S(2)}, u32[]{:S(2)}) %collective-permute-start.2) | collective-permute-done | bytes 131104 | tf_op jit(solution)/shard_map/ppermute | solution.py:330
  29.3 0.1 collective-permute-start.4
  29.4 1.2 odd_first.2
  30.6 2.6 %collective-permute-done.4.vectors_ref = bf16[4,128,128]{2,1,0:T(8,128)(2,1)S(1)} collective-permute-done((bf16[4,128,128]{2,1,0:T(8,128)(2,1)S(1)}, bf16[4,128,128]{2,1,0:T(8,128)(2,1)S(1)}, u32[]{:S(2)}, u32[]{:S(2)}) %collective-permute-start.4) | collective-permute-done | bytes 131104 | tf_op jit(solution)/shard_map/ppermute | solution.py:330
  33.2 0.7 odd_other.2
  33.9 2.8 %collective-permute-start.5 = (bf16[16,128,128]{2,1,0:T(8,128)(2,1)S(1)}, bf16[16,128,128]{2,1,0:T(8,128)(2,1)S(1)}, u32[]{:S(2)}, u32[]{:S(2)}) collective-permute-start(bf16[16,128,128]{2,1,0:T(8,128)(2,1)S(1)} %odd_other.2), channel_id=1, source_target_pairs={{0,1},{1,0},{2,3},{3,2},{4,5},{5,4},{6,7},{7,6},{8,9},{9,8},{10,11... | collective-permute-start | bytes 1572872 | tf_op jit(solution)/shard_map/ppermute | solution.py:325
  36.7 0.7 odd_mine.2.mine_ref
  37.4 0.8 collective-permute-done.5.received_ref
  38.3 16.9 %all_to_all.30.parts_ref = bf16[16,128,128]{2,1,0:T(8,128)(2,1)S(1)} all-to-all(bf16[16,128,128]{2,1,0:T(8,128)(2,1)S(1)} %pair_core.2), channel_id=1, replica_groups=mesh['row'=8,'x'=4,'y'=4,'core'=2] {'x','y'}, dimensions={0} | all-to-all | bytes 1048576 | tf_op jit(solution)/shard_map/all_to_all | solution.py:334
  55.2 0.1 next_share.2
  55.4 12.7 %all_to_all.31.vectors_ref = bf16[16,128,128]{2,1,0:T(8,128)(2,1)S(1)} all-to-all(bf16[16,128,128]{2,1,0:T(8,128)(2,1)S(1)} %get-tuple-element.38), channel_id=1, replica_groups=mesh['row'=8,'x'=4,'y'=4,'core'=2] {'x','y'}, dimensions={0} | all-to-all | bytes 1048576 | tf_op jit(solution)/shard_map/all_to_all | solution.py:334
  68.1 3.3 %collective-permute-start.6 = (bf16[16,128,128]{2,1,0:T(8,128)(2,1)S(1)}, bf16[16,128,128]{2,1,0:T(8,128)(2,1)S(1)}, u32[]{:S(2)}, u32[]{:S(2)}) collective-permute-start(bf16[16,128,128]{2,1,0:T(8,128)(2,1)S(1)} %all_to_all.31.vectors_ref), channel_id=1, source_target_pairs={{0,1},{1,0},{2,3},{3,2},{4,5},{5,4},{6,7},{7,6},{8,9},{9,8},{10,11... | collective-permute-start | bytes 1572872 | tf_op jit(solution)/shard_map/ppermute | solution.py:325
  71.3 0.8 even_first.1
  72.2 0.7 collective-permute-done.6.vectors_ref
  72.9 0.6 even_last.3
  73.4 1.1 collective-permute-start.7
  74.5 0.6 even_last.2.mine_ref
  75.1 3.1 %collective-permute-done.7.received_ref = bf16[4,128,128]{2,1,0:T(8,128)(2,1)S(1)} collective-permute-done((bf16[4,128,128]{2,1,0:T(8,128)(2,1)S(1)}, bf16[4,128,128]{2,1,0:T(8,128)(2,1)S(1)}, u32[]{:S(2)}, u32[]{:S(2)}) %collective-permute-start.7) | collective-permute-done | bytes 131104 | tf_op jit(solution)/shard_map/ppermute | solution.py:330
  78.3 2.5 %collective-permute-start.10 = (bf16[4,128,128]{2,1,0:T(8,128)(2,1)S(1)}, bf16[4,128,128]{2,1,0:T(8,128)(2,1)S(1)}, u32[]{:S(2)}, u32[]{:S(2)}) collective-permute-start(bf16[4,128,128]{2,1,0:T(8,128)(2,1)S(1)} %get-tuple-element.42), channel_id=1, source_target_pairs={{0,224},{32,192},{64,160},{96,128},{128,96},{160,64},{192,32},{224... | collective-permute-start | bytes 393224 | tf_op jit(solution)/shard_map/ppermute | solution.py:330
  80.7 1.4 collective-permute-start.8
  82.1 1.0 collective-permute-start.9
  83.1 1.6 collective-permute-done.10.seven_ref
  84.8 1.1 collective-permute-done.8.two_ref
  85.9 8.2 %collective-permute-done.9.five_ref = bf16[4,128,128]{2,1,0:T(8,128)(2,1)S(1)} collective-permute-done((bf16[4,128,128]{2,1,0:T(8,128)(2,1)S(1)}, bf16[4,128,128]{2,1,0:T(8,128)(2,1)S(1)}, u32[]{:S(2)}, u32[]{:S(2)}) %collective-permute-start.9) | collective-permute-done | bytes 131104 | tf_op jit(solution)/shard_map/ppermute | solution.py:330
  94.2 0.1 collective-permute-start.11
  94.3 1.2 odd_first.3
  95.5 2.6 %collective-permute-done.11.vectors_ref = bf16[4,128,128]{2,1,0:T(8,128)(2,1)S(1)} collective-permute-done((bf16[4,128,128]{2,1,0:T(8,128)(2,1)S(1)}, bf16[4,128,128]{2,1,0:T(8,128)(2,1)S(1)}, u32[]{:S(2)}, u32[]{:S(2)}) %collective-permute-start.11) | collective-permute-done | bytes 131104 | tf_op jit(solution)/shard_map/ppermute | solution.py:330
  98.1 0.7 odd_other.3
  98.8 3.3 %collective-permute-start.12 = (bf16[16,128,128]{2,1,0:T(8,128)(2,1)S(1)}, bf16[16,128,128]{2,1,0:T(8,128)(2,1)S(1)}, u32[]{:S(2)}, u32[]{:S(2)}) collective-permute-start(bf16[16,128,128]{2,1,0:T(8,128)(2,1)S(1)} %odd_other.3), channel_id=1, source_target_pairs={{0,1},{1,0},{2,3},{3,2},{4,5},{5,4},{6,7},{7,6},{8,9},{9,8},{10,11... | collective-permute-start | bytes 1572872 | tf_op jit(solution)/shard_map/ppermute | solution.py:325
  102.1 0.7 odd_mine.3.mine_ref
  102.9 0.8 collective-permute-done.12.received_ref
  103.8 13.4 %all_to_all.32.parts_ref = bf16[16,128,128]{2,1,0:T(8,128)(2,1)S(1)} all-to-all(bf16[16,128,128]{2,1,0:T(8,128)(2,1)S(1)} %pair_core.3), channel_id=1, replica_groups=mesh['row'=8,'x'=4,'y'=4,'core'=2] {'x','y'}, dimensions={0} | all-to-all | bytes 1048576 | tf_op jit(solution)/shard_map/all_to_all | solution.py:334
  117.1 0.1 next_share.3.block_ref
  117.2 12.7 %all_to_all.33.mine_ref = bf16[16,128,128]{2,1,0:T(8,128)(2,1)S(1)} all-to-all(bf16[16,128,128]{2,1,0:T(8,128)(2,1)S(1)} %next_share.3.block_ref), channel_id=1, replica_groups=mesh['row'=8,'x'=4,'y'=4,'core'=2] {'x','y'}, dimensions={0} | all-to-all | bytes 1048576 | tf_op jit(solution)/shard_map/all_to_all | solution.py:334
  130.0 3.3 %collective-permute-start.13 = (bf16[16,128,128]{2,1,0:T(8,128)(2,1)S(1)}, bf16[16,128,128]{2,1,0:T(8,128)(2,1)S(1)}, u32[]{:S(2)}, u32[]{:S(2)}) collective-permute-start(bf16[16,128,128]{2,1,0:T(8,128)(2,1)S(1)} %all_to_all.33.mine_ref), channel_id=1, source_target_pairs={{0,1},{1,0},{2,3},{3,2},{4,5},{5,4},{6,7},{7,6},{8,9},{9,8},{10,11... | collective-permute-start | bytes 1572872 | tf_op jit(solution)/shard_map/ppermute | solution.py:325
  133.2 0.3 own_gram.1.gram_ref
  133.6 1.2 collective-permute-done.13.other_ref
  134.8 0.4 first_gram.1
  135.2 16.7 %all_to_all.34.parts_ref = f32[8,72,128]{2,1,0:T(8,128)S(1)} all-to-all(f32[8,72,128]{2,1,0:T(8,128)S(1)} %first_gram.1), channel_id=1, replica_groups=mesh['row'=8,'x'=4,'y'=4,'core'=2] {'row'}, dimensions={0} | all-to-all | bytes 589824 | tf_op jit(solution)/shard_map/all_to_all | solution.py:334
  151.9 5.4 %second_gram.1 = (f32[8,72,128]{2,1,0:T(8,128)S(1)}, f32[128,128]{1,0:T(8,128)S(1)}, f32[128,128]{1,0:T(8,128)S(1)}) custom-call(f32[8,72,128]{2,1,0:T(8,128)S(1)} %all_to_all.34.parts_ref, bf16[16,128,128]{2,1,0:T(8,128)(2,1)S(1)} %all_to_all.33.mine_ref, bf16[16,128,128]{2,1,0:T(8,128)(2,1)S(1)} %collective-permute-done.13.other_ref), custom_call_target="tpu_custom_call" | custom-call | tf_op jit(solution)/shard_map/second_gram/pallas_call | solution.py:29
  157.3 13.0 %all_to_all.35.parts_ref = f32[8,72,128]{2,1,0:T(8,128)S(1)} all-to-all(f32[8,72,128]{2,1,0:T(8,128)S(1)} %get-tuple-element.47), channel_id=1, replica_groups=mesh['row'=8,'x'=4,'y'=4,'core'=2] {'row'}, dimensions={0} | all-to-all | bytes 589824 | tf_op jit(solution)/shard_map/all_to_all | solution.py:334
  170.4 4.4 %last.1 = (f32[128,128]{1,0:T(8,128)}, f32[128,128]{1,0:T(8,128)}) custom-call(f32[8,72,128]{2,1,0:T(8,128)S(1)} %all_to_all.35.parts_ref, f32[128,128]{1,0:T(8,128)S(1)} %get-tuple-element.48.upper_one_ref, f32[128,128]{1,0:T(8,128)S(1)} %get-tuple-element.49.inverse_one_ref, bf16[16,128,128]{2,1,0:T(8,128)(2,1)S(1)} %next_share.3.block_ref), custom_call_target="tpu_custom_call" | custom-call | tf_op jit(solution)/shard_map/last/pallas_call | solution.py:29
  (9 shorter events, 0.4 us)
Async XLA Ops:
  4.5 5.1 %collective-permute-start = (bf16[4,128,128]{2,1,0:T(8,128)(2,1)S(1)}, bf16[4,128,128]{2,1,0:T(8,128)(2,1)S(1)}, u32[]{:S(2)}, u32[]{:S(2)}) collective-permute-start(bf16[4,128,128]{2,1,0:T(8,128)(2,1)S(1)} %get-tuple-element.31), channel_id=1, source_target_pairs={{0,32},{32,0},{64,96},{96,64},{128,160},{160,128},{192,224},{224,1... | collective-permute-start | bytes 393224 | tf_op jit(solution)/shard_map/ppermute | solution.py:330
  9.7 9.3 %collective-permute-start.1 = (bf16[4,128,128]{2,1,0:T(8,128)(2,1)S(1)}, bf16[4,128,128]{2,1,0:T(8,128)(2,1)S(1)}, u32[]{:S(2)}, u32[]{:S(2)}) collective-permute-start(bf16[4,128,128]{2,1,0:T(8,128)(2,1)S(1)} %get-tuple-element.33), channel_id=1, source_target_pairs={{0,64},{32,96},{64,0},{96,32},{128,192},{160,224},{192,128},{224,1... | collective-permute-start | bytes 393224 | tf_op jit(solution)/shard_map/ppermute | solution.py:330
  13.3 15.9 %collective-permute-start.2 = (bf16[4,128,128]{2,1,0:T(8,128)(2,1)S(1)}, bf16[4,128,128]{2,1,0:T(8,128)(2,1)S(1)}, u32[]{:S(2)}, u32[]{:S(2)}) collective-permute-start(bf16[4,128,128]{2,1,0:T(8,128)(2,1)S(1)} %get-tuple-element.33), channel_id=1, source_target_pairs={{0,160},{32,128},{64,224},{96,192},{128,32},{160,0},{192,96},{224,... | collective-permute-start | bytes 393224 | tf_op jit(solution)/shard_map/ppermute | solution.py:330
  17.6 11.6 %collective-permute-start.3 = (bf16[4,128,128]{2,1,0:T(8,128)(2,1)S(1)}, bf16[4,128,128]{2,1,0:T(8,128)(2,1)S(1)}, u32[]{:S(2)}, u32[]{:S(2)}) collective-permute-start(bf16[4,128,128]{2,1,0:T(8,128)(2,1)S(1)} %get-tuple-element.33), channel_id=1, source_target_pairs={{0,224},{32,192},{64,160},{96,128},{128,96},{160,64},{192,32},{224... | collective-permute-start | bytes 393224 | tf_op jit(solution)/shard_map/ppermute | solution.py:330
  29.3 3.9 %collective-permute-start.4 = (bf16[4,128,128]{2,1,0:T(8,128)(2,1)S(1)}, bf16[4,128,128]{2,1,0:T(8,128)(2,1)S(1)}, u32[]{:S(2)}, u32[]{:S(2)}) collective-permute-start(bf16[4,128,128]{2,1,0:T(8,128)(2,1)S(1)} %get-tuple-element.34.vectors_ref), channel_id=1, source_target_pairs={{0,32},{32,0},{64,96},{96,64},{128,160},{160,128},{192,224},{224,1... | collective-permute-start | bytes 393224 | tf_op jit(solution)/shard_map/ppermute | solution.py:330
  33.9 4.4 %collective-permute-start.5 = (bf16[16,128,128]{2,1,0:T(8,128)(2,1)S(1)}, bf16[16,128,128]{2,1,0:T(8,128)(2,1)S(1)}, u32[]{:S(2)}, u32[]{:S(2)}) collective-permute-start(bf16[16,128,128]{2,1,0:T(8,128)(2,1)S(1)} %odd_other.2), channel_id=1, source_target_pairs={{0,1},{1,0},{2,3},{3,2},{4,5},{5,4},{6,7},{7,6},{8,9},{9,8},{10,11... | collective-permute-start | bytes 1572872 | tf_op jit(solution)/shard_map/ppermute | solution.py:325
  68.1 4.8 %collective-permute-start.6 = (bf16[16,128,128]{2,1,0:T(8,128)(2,1)S(1)}, bf16[16,128,128]{2,1,0:T(8,128)(2,1)S(1)}, u32[]{:S(2)}, u32[]{:S(2)}) collective-permute-start(bf16[16,128,128]{2,1,0:T(8,128)(2,1)S(1)} %all_to_all.31.vectors_ref), channel_id=1, source_target_pairs={{0,1},{1,0},{2,3},{3,2},{4,5},{5,4},{6,7},{7,6},{8,9},{9,8},{10,11... | collective-permute-start | bytes 1572872 | tf_op jit(solution)/shard_map/ppermute | solution.py:325
  73.4 4.8 %collective-permute-start.7 = (bf16[4,128,128]{2,1,0:T(8,128)(2,1)S(1)}, bf16[4,128,128]{2,1,0:T(8,128)(2,1)S(1)}, u32[]{:S(2)}, u32[]{:S(2)}) collective-permute-start(bf16[4,128,128]{2,1,0:T(8,128)(2,1)S(1)} %even_last.3), channel_id=1, source_target_pairs={{0,32},{32,0},{64,96},{96,64},{128,160},{160,128},{192,224},{224,1... | collective-permute-start | bytes 393224 | tf_op jit(solution)/shard_map/ppermute | solution.py:330
  78.3 6.5 %collective-permute-start.10 = (bf16[4,128,128]{2,1,0:T(8,128)(2,1)S(1)}, bf16[4,128,128]{2,1,0:T(8,128)(2,1)S(1)}, u32[]{:S(2)}, u32[]{:S(2)}) collective-permute-start(bf16[4,128,128]{2,1,0:T(8,128)(2,1)S(1)} %get-tuple-element.42), channel_id=1, source_target_pairs={{0,224},{32,192},{64,160},{96,128},{128,96},{160,64},{192,32},{224... | collective-permute-start | bytes 393224 | tf_op jit(solution)/shard_map/ppermute | solution.py:330
  80.7 5.1 %collective-permute-start.8 = (bf16[4,128,128]{2,1,0:T(8,128)(2,1)S(1)}, bf16[4,128,128]{2,1,0:T(8,128)(2,1)S(1)}, u32[]{:S(2)}, u32[]{:S(2)}) collective-permute-start(bf16[4,128,128]{2,1,0:T(8,128)(2,1)S(1)} %get-tuple-element.42), channel_id=1, source_target_pairs={{0,64},{32,96},{64,0},{96,32},{128,192},{160,224},{192,128},{224,1... | collective-permute-start | bytes 393224 | tf_op jit(solution)/shard_map/ppermute | solution.py:330
  82.1 12.0 %collective-permute-start.9 = (bf16[4,128,128]{2,1,0:T(8,128)(2,1)S(1)}, bf16[4,128,128]{2,1,0:T(8,128)(2,1)S(1)}, u32[]{:S(2)}, u32[]{:S(2)}) collective-permute-start(bf16[4,128,128]{2,1,0:T(8,128)(2,1)S(1)} %get-tuple-element.42), channel_id=1, source_target_pairs={{0,160},{32,128},{64,224},{96,192},{128,32},{160,0},{192,96},{224,... | collective-permute-start | bytes 393224 | tf_op jit(solution)/shard_map/ppermute | solution.py:330
  94.2 3.9 %collective-permute-start.11 = (bf16[4,128,128]{2,1,0:T(8,128)(2,1)S(1)}, bf16[4,128,128]{2,1,0:T(8,128)(2,1)S(1)}, u32[]{:S(2)}, u32[]{:S(2)}) collective-permute-start(bf16[4,128,128]{2,1,0:T(8,128)(2,1)S(1)} %four_sum.3.vectors_ref), channel_id=1, source_target_pairs={{0,32},{32,0},{64,96},{96,64},{128,160},{160,128},{192,224},{224,1... | collective-permute-start | bytes 393224 | tf_op jit(solution)/shard_map/ppermute | solution.py:330
  98.8 4.9 %collective-permute-start.12 = (bf16[16,128,128]{2,1,0:T(8,128)(2,1)S(1)}, bf16[16,128,128]{2,1,0:T(8,128)(2,1)S(1)}, u32[]{:S(2)}, u32[]{:S(2)}) collective-permute-start(bf16[16,128,128]{2,1,0:T(8,128)(2,1)S(1)} %odd_other.3), channel_id=1, source_target_pairs={{0,1},{1,0},{2,3},{3,2},{4,5},{5,4},{6,7},{7,6},{8,9},{9,8},{10,11... | collective-permute-start | bytes 1572872 | tf_op jit(solution)/shard_map/ppermute | solution.py:325
  130.0 4.8 %collective-permute-start.13 = (bf16[16,128,128]{2,1,0:T(8,128)(2,1)S(1)}, bf16[16,128,128]{2,1,0:T(8,128)(2,1)S(1)}, u32[]{:S(2)}, u32[]{:S(2)}) collective-permute-start(bf16[16,128,128]{2,1,0:T(8,128)(2,1)S(1)} %all_to_all.33.mine_ref), channel_id=1, source_target_pairs={{0,1},{1,0},{2,3},{3,2},{4,5},{5,4},{6,7},{7,6},{8,9},{9,8},{10,11... | collective-permute-start | bytes 1572872 | tf_op jit(solution)/shard_map/ppermute | solution.py:325

commit v9 on v8

--- a/solution.py
+++ b/solution.py
@@ -11,7 +11,8 @@
 N = 32768
 K = 128
 HALF = K // 2
-PACK = HALF + 8
+PACK = HALF + 16
+SHARE = PACK // 2
 PANEL = 8
 HIGHEST = lax.Precision.HIGHEST
 VMEM_LIMIT = 24 * 2**20
@@ -116,14 +117,15 @@
     return lax.broadcasted_iota(jnp.int32, shape, 0), lax.broadcasted_iota(jnp.int32, shape, 1)
 
 
-def pack(gram, out_ref):
+def pack(gram, keep_ref, send_ref):
     top, bottom = gram[:HALF], gram[HALF:]
     row, lane = grids()
     triangles = jnp.where(lane >= row, top, pltpu.roll(bottom, HALF, 1))
     diagonal = jnp.sum(jnp.where(lane == row + HALF, bottom, 0.0), axis=0, keepdims=True)
-    for i in range(out_ref.shape[0]):
-        out_ref[i, :HALF] = triangles
-        out_ref[i, HALF:] = jnp.broadcast_to(diagonal, (PACK - HALF, K))
+    packed = jnp.concatenate([triangles, jnp.broadcast_to(diagonal, (PACK - HALF, K))], axis=0)
+    core = lax.axis_index("core")
+    keep_ref[...] = jnp.where(core == 0, packed[:SHARE], packed[SHARE:])
+    send_ref[...] = jnp.where(core == 0, packed[SHARE:], packed[:SHARE])
 
 
 def sum_copies(parts_ref):
@@ -133,8 +135,11 @@
     return total
 
 
-def unpack_sum(parts_ref):
-    packed = sum_copies(parts_ref)
+def unpack(mine_ref, other_ref):
+    core, mine, other = lax.axis_index("core"), mine_ref[...], other_ref[...]
+    packed = jnp.concatenate(
+        [jnp.where(core == 0, mine, other), jnp.where(core == 0, other, mine)], axis=0
+    )
     row, lane = grids()
     triangles, diagonal = packed[:HALF], packed[HALF : HALF + 1]
     last = pltpu.roll(jnp.where(lane < row, triangles, 0.0), HALF, 1)
@@ -290,28 +295,33 @@
     return total
 
 
-def own_gram_kernel(mine_ref, out_ref):
-    mine = flat(mine_ref[...])
-    out_ref[...] = contract_rows(mine, mine)
-
-
-def first_gram_kernel(gram_ref, other_ref, out_ref):
-    other = flat(other_ref[...])
-    pack(gram_ref[...] + contract_rows(other, other), out_ref)
-
-
-def second_gram_kernel(parts_ref, mine_ref, other_ref, out_ref, upper_ref, inverse_ref):
-    factor(unpack_sum(parts_ref), upper_ref, inverse_ref)
-    inverse = inverse_ref[...]
-    mine = times_inverse(flat(mine_ref[...]), inverse)
-    other = times_inverse(flat(other_ref[...]), inverse)
-    pack(gram_of(mine) + gram_of(other), out_ref)
+def first_gram_kernel(block_ref, keep_ref, send_ref):
+    block = flat(block_ref[...])
+    pack(contract_rows(block, block), keep_ref, send_ref)
+
+
+def copies_kernel(mine_ref, received_ref, out_ref):
+    total = mine_ref[...] + received_ref[...]
+    out_ref[...] = jnp.broadcast_to(total[None], out_ref.shape)
+
+
+def sum_kernel(parts_ref, out_ref):
+    out_ref[...] = sum_copies(parts_ref)
+
+
+def second_gram_kernel(
+    mine_ref, other_ref, block_ref, keep_ref, send_ref, upper_ref, inverse_ref
+):
+    factor(unpack(mine_ref, other_ref), upper_ref, inverse_ref)
+    block = times_inverse(flat(block_ref[...]), inverse_ref[...])
+    pack(gram_of(block), keep_ref, send_ref)
 
 
 def last_kernel(
-    parts_ref, upper_one_ref, inverse_one_ref, block_ref, basis_ref, triangle_ref, upper_ref, inverse_ref
+    mine_ref, other_ref, upper_one_ref, inverse_one_ref, block_ref, basis_ref, triangle_ref,
+    upper_ref, inverse_ref,
 ):
-    factor(unpack_sum(parts_ref), upper_ref, inverse_ref)
+    factor(unpack(mine_ref, other_ref), upper_ref, inverse_ref)
     root = math.sqrt(N)
     first_basis = times_inverse(block_ref[0], inverse_one_ref[...])
     basis_ref[...] = times_transposed(first_basis, inverse_ref[...]) * root
@@ -410,18 +420,23 @@
     (vectors,) = sum_rows(other, lambda: even_last(matrix, mine, f32), first)
     (copies,) = next_share(odd_parts(vectors), second, False)
 
-    mine = exchange(copies, PLANE)
-    other = swap_core(mine)
-    square = ((K, K), f32)
-    (gram,) = local_call(own_gram_kernel, [square], mine, name="own_gram")
-    packed = ((row_count, PACK, K), f32)
-    (parts,) = local_call(first_gram_kernel, [packed], gram, other, name="first_gram")
-    parts, upper, inverse = local_call(
-        second_gram_kernel, [packed, square, square], exchange(parts, "row"), mine, other,
+    def sum_gram(keep, send):
+        received = swap_core(send)
+        (parts,) = local_call(
+            copies_kernel, [((row_count, SHARE, K), f32)], keep, received, name="gram_copies"
+        )
+        (total,) = local_call(sum_kernel, [packed], exchange(parts, "row"), name="gram_sum")
+        return total, swap_core(total)
+
+    block = exchange(copies, PLANE)
+    packed, square = ((SHARE, K), f32), ((K, K), f32)
+    keep, send = local_call(first_gram_kernel, [packed, packed], block, name="first_gram")
+    keep, send, upper, inverse = local_call(
+        second_gram_kernel, [packed, packed, square, square], *sum_gram(keep, send), block,
         name="second_gram",
     )
     return local_call(
-        last_kernel, [((share, K), f32), square], exchange(parts, "row"), upper, inverse, copies,
+        last_kernel, [((share, K), f32), square], *sum_gram(keep, send), upper, inverse, copies,
         name="last", out_space=jax.ShapeDtypeStruct, scratch_shapes=[pltpu.VMEM((K, K), f32)] * 2,
     )
 

time: 175 us -> 176 us (level)
  blocking collectives: 85.5 us -> 80.5 us
  starting transfers between devices: 29.2 us -> 33.7 us
  waiting for transfers between devices: 34.3 us -> 36.5 us
    all_to_all x6, blocking collectives: 85.5 us -> 80.5 us  [exchange(): return lax.all_to_all(blocks, axes, 0, 0, tiled=True)]
    ppermute x4 -> x7, starting transfers between devices: 12.7 us -> 17.2 us  [swap_core(): return lax.ppermute(block, 'core', ((0, 1), (1, 0)))]
    ppermute x4 -> x7, waiting for transfers between devices: 3.52 us -> 5.7 us  [swap_core(): return lax.ppermute(block, 'core', ((0, 1), (1, 0)))]
    pallas_call x23 -> x26, Pallas kernels: 24.3 us -> 23.8 us  [local_call(): pl.pallas_call(kernel, in_specs=[pl.BlockSpec(memory_space=space) for spa...]
  transfers between devices with their start and end apart: 14 -> 17, of which waited for: 12 -> 15; matrix products, arithmetic and copies ran while one was open for 0% -> 0% of each run, Pallas kernels for 5% -> 4%
where the time goes in v9:
time: 176 us
  blocking collectives  80.5 us (46%)
  waiting for transfers between devices  36.5 us (21%)
  starting transfers between devices  33.7 us (19%)
  Pallas kernels  23.8 us (14%)
    all_to_all x6, blocking collectives, exchange(): return lax.all_to_all(blocks, axes, 0, 0, tiled=True)  80.5 us
    ppermute x10, waiting for transfers between devices, swap_row(): return lax.ppermute(block, 'row', [(i, i ^ mask) for i in range(count)])  30.8 us
    pallas_call x26, Pallas kernels, local_call(): pl.pallas_call(kernel, in_specs=[pl.BlockSpec(memory_space=space) for spa...  23.8 us
    ppermute x7, starting transfers between devices, swap_core(): return lax.ppermute(block, 'core', ((0, 1), (1, 0)))  17.2 us
    ppermute x10, starting transfers between devices, swap_row(): return lax.ppermute(block, 'row', [(i, i ^ mask) for i in range(count)])  16.5 us
    ppermute x7, waiting for transfers between devices, swap_core(): return lax.ppermute(block, 'core', ((0, 1), (1, 0)))  5.7 us
  transfers between devices with their start and end apart: 17, of which 15 were waited for; matrix products, arithmetic and copies ran while one was open for 0% of the time, Pallas kernels for 4%

profile of v9, /device:TPU:1, one launch (start us, length us, event | category | flops | bytes accessed | tf_op | source)
XLA Modules:
  0.0 176.0 jit_solution(17586764936218066193)
XLA Ops:
  1.3 3.2 %start.1 = (bf16[4,128,128]{2,1,0:T(8,128)(2,1)S(1)}, bf16[16,2,128,128]{3,2,1,0:T(8,128)(2,1)S(1)}, f32[128,128]{1,0:T(8,128)S(1)}, bf16[16,2,128,512]{3,2,1,0:T(8,128)(2,1)S(1)}, f32[8,128]{1,0:T(8,128)S(1)}) custom-call(bf16[16,2,128,1024]{3,2,1,0:T(8,128)(2,1)} %bitcast.2, f32[16,2,128,128]{3,2,1,0:T(8,128)} %bitcast.4, f32[1]{0:T(128)S(6)} %copy.5.bound_ref), custom_call_target="tpu_custom_call" | custom-call | tf_op jit(solution)/shard_map/start/pallas_call | solution.py:30
  4.5 2.6 %collective-permute-start = (bf16[4,128,128]{2,1,0:T(8,128)(2,1)S(1)}, bf16[4,128,128]{2,1,0:T(8,128)(2,1)S(1)}, u32[]{:S(2)}, u32[]{:S(2)}) collective-permute-start(bf16[4,128,128]{2,1,0:T(8,128)(2,1)S(1)} %get-tuple-element.34), channel_id=1, source_target_pairs={{0,32},{32,0},{64,96},{96,64},{128,160},{160,128},{192,224},{224,1... | collective-permute-start | bytes 393224 | tf_op jit(solution)/shard_map/ppermute | solution.py:340
  7.1 2.6 %start_own.1 = (f32[4,128,128]{2,1,0:T(8,128)S(1)}, bf16[16,2,128,512]{3,2,1,0:T(8,128)(2,1)S(1)}) custom-call(bf16[16,2,128,1024]{3,2,1,0:T(8,128)(2,1)} %bitcast.3, bf16[16,2,128,128]{3,2,1,0:T(8,128)(2,1)S(1)} %get-tuple-element.31.vectors_ref), custom_call_target="tpu_custom_call" | custom-call | tf_op jit(solution)/shard_map/start_own/pallas_call | solution.py:30
  9.7 3.6 %collective-permute-start.1 = (bf16[4,128,128]{2,1,0:T(8,128)(2,1)S(1)}, bf16[4,128,128]{2,1,0:T(8,128)(2,1)S(1)}, u32[]{:S(2)}, u32[]{:S(2)}) collective-permute-start(bf16[4,128,128]{2,1,0:T(8,128)(2,1)S(1)} %get-tuple-element.36), channel_id=1, source_target_pairs={{0,64},{32,96},{64,0},{96,32},{128,192},{160,224},{192,128},{224,1... | collective-permute-start | bytes 393224 | tf_op jit(solution)/shard_map/ppermute | solution.py:340
  13.3 4.3 %collective-permute-start.2 = (bf16[4,128,128]{2,1,0:T(8,128)(2,1)S(1)}, bf16[4,128,128]{2,1,0:T(8,128)(2,1)S(1)}, u32[]{:S(2)}, u32[]{:S(2)}) collective-permute-start(bf16[4,128,128]{2,1,0:T(8,128)(2,1)S(1)} %get-tuple-element.36), channel_id=1, source_target_pairs={{0,160},{32,128},{64,224},{96,192},{128,32},{160,0},{192,96},{224,... | collective-permute-start | bytes 393224 | tf_op jit(solution)/shard_map/ppermute | solution.py:340
  17.6 1.4 collective-permute-done.1.two_ref
  19.0 10.2 %collective-permute-done.2.five_ref = bf16[4,128,128]{2,1,0:T(8,128)(2,1)S(1)} collective-permute-done((bf16[4,128,128]{2,1,0:T(8,128)(2,1)S(1)}, bf16[4,128,128]{2,1,0:T(8,128)(2,1)S(1)}, u32[]{:S(2)}, u32[]{:S(2)}) %collective-permute-start.2) | collective-permute-done | bytes 131104 | tf_op jit(solution)/shard_map/ppermute | solution.py:340
  29.4 1.2 odd_first.2
  30.6 2.6 %collective-permute-done.4.vectors_ref = bf16[4,128,128]{2,1,0:T(8,128)(2,1)S(1)} collective-permute-done((bf16[4,128,128]{2,1,0:T(8,128)(2,1)S(1)}, bf16[4,128,128]{2,1,0:T(8,128)(2,1)S(1)}, u32[]{:S(2)}, u32[]{:S(2)}) %collective-permute-start.4) | collective-permute-done | bytes 131104 | tf_op jit(solution)/shard_map/ppermute | solution.py:340
  33.2 0.7 odd_other.2
  33.9 2.8 %collective-permute-start.5 = (bf16[16,128,128]{2,1,0:T(8,128)(2,1)S(1)}, bf16[16,128,128]{2,1,0:T(8,128)(2,1)S(1)}, u32[]{:S(2)}, u32[]{:S(2)}) collective-permute-start(bf16[16,128,128]{2,1,0:T(8,128)(2,1)S(1)} %odd_other.2), channel_id=1, source_target_pairs={{0,1},{1,0},{2,3},{3,2},{4,5},{5,4},{6,7},{7,6},{8,9},{9,8},{10,11... | collective-permute-start | bytes 1572872 | tf_op jit(solution)/shard_map/ppermute | solution.py:335
  36.7 0.7 odd_mine.2.mine_ref
  37.4 0.8 collective-permute-done.5.received_ref
  38.3 16.9 %all_to_all.30.parts_ref = bf16[16,128,128]{2,1,0:T(8,128)(2,1)S(1)} all-to-all(bf16[16,128,128]{2,1,0:T(8,128)(2,1)S(1)} %pair_core.2), channel_id=1, replica_groups=mesh['row'=8,'x'=4,'y'=4,'core'=2] {'x','y'}, dimensions={0} | all-to-all | bytes 1048576 | tf_op jit(solution)/shard_map/all_to_all | solution.py:344
  55.4 12.7 %all_to_all.31.vectors_ref = bf16[16,128,128]{2,1,0:T(8,128)(2,1)S(1)} all-to-all(bf16[16,128,128]{2,1,0:T(8,128)(2,1)S(1)} %get-tuple-element.41), channel_id=1, replica_groups=mesh['row'=8,'x'=4,'y'=4,'core'=2] {'x','y'}, dimensions={0} | all-to-all | bytes 1048576 | tf_op jit(solution)/shard_map/all_to_all | solution.py:344
  68.1 3.3 %collective-permute-start.6 = (bf16[16,128,128]{2,1,0:T(8,128)(2,1)S(1)}, bf16[16,128,128]{2,1,0:T(8,128)(2,1)S(1)}, u32[]{:S(2)}, u32[]{:S(2)}) collective-permute-start(bf16[16,128,128]{2,1,0:T(8,128)(2,1)S(1)} %all_to_all.31.vectors_ref), channel_id=1, source_target_pairs={{0,1},{1,0},{2,3},{3,2},{4,5},{5,4},{6,7},{7,6},{8,9},{9,8},{10,11... | collective-permute-start | bytes 1572872 | tf_op jit(solution)/shard_map/ppermute | solution.py:335
  71.3 0.8 even_first.1
  72.2 0.7 collective-permute-done.6.vectors_ref
  72.9 0.6 even_last.3
  73.4 1.1 collective-permute-start.7
  74.5 0.6 even_last.2.mine_ref
  75.1 3.1 %collective-permute-done.7.received_ref = bf16[4,128,128]{2,1,0:T(8,128)(2,1)S(1)} collective-permute-done((bf16[4,128,128]{2,1,0:T(8,128)(2,1)S(1)}, bf16[4,128,128]{2,1,0:T(8,128)(2,1)S(1)}, u32[]{:S(2)}, u32[]{:S(2)}) %collective-permute-start.7) | collective-permute-done | bytes 131104 | tf_op jit(solution)/shard_map/ppermute | solution.py:340
  78.3 2.5 %collective-permute-start.10 = (bf16[4,128,128]{2,1,0:T(8,128)(2,1)S(1)}, bf16[4,128,128]{2,1,0:T(8,128)(2,1)S(1)}, u32[]{:S(2)}, u32[]{:S(2)}) collective-permute-start(bf16[4,128,128]{2,1,0:T(8,128)(2,1)S(1)} %get-tuple-element.45), channel_id=1, source_target_pairs={{0,224},{32,192},{64,160},{96,128},{128,96},{160,64},{192,32},{224... | collective-permute-start | bytes 393224 | tf_op jit(solution)/shard_map/ppermute | solution.py:340
  80.7 1.4 collective-permute-start.8
  82.1 1.0 collective-permute-start.9
  83.1 1.6 collective-permute-done.10.seven_ref
  84.8 1.1 collective-permute-done.8.two_ref
  85.9 8.2 %collective-permute-done.9.five_ref = bf16[4,128,128]{2,1,0:T(8,128)(2,1)S(1)} collective-permute-done((bf16[4,128,128]{2,1,0:T(8,128)(2,1)S(1)}, bf16[4,128,128]{2,1,0:T(8,128)(2,1)S(1)}, u32[]{:S(2)}, u32[]{:S(2)}) %collective-permute-start.9) | collective-permute-done | bytes 131104 | tf_op jit(solution)/shard_map/ppermute | solution.py:340
  94.3 1.2 odd_first.3
  95.5 2.6 %collective-permute-done.11.vectors_ref = bf16[4,128,128]{2,1,0:T(8,128)(2,1)S(1)} collective-permute-done((bf16[4,128,128]{2,1,0:T(8,128)(2,1)S(1)}, bf16[4,128,128]{2,1,0:T(8,128)(2,1)S(1)}, u32[]{:S(2)}, u32[]{:S(2)}) %collective-permute-start.11) | collective-permute-done | bytes 131104 | tf_op jit(solution)/shard_map/ppermute | solution.py:340
  98.1 0.7 odd_other.3
  98.8 3.3 %collective-permute-start.12 = (bf16[16,128,128]{2,1,0:T(8,128)(2,1)S(1)}, bf16[16,128,128]{2,1,0:T(8,128)(2,1)S(1)}, u32[]{:S(2)}, u32[]{:S(2)}) collective-permute-start(bf16[16,128,128]{2,1,0:T(8,128)(2,1)S(1)} %odd_other.3), channel_id=1, source_target_pairs={{0,1},{1,0},{2,3},{3,2},{4,5},{5,4},{6,7},{7,6},{8,9},{9,8},{10,11... | collective-permute-start | bytes 1572872 | tf_op jit(solution)/shard_map/ppermute | solution.py:335
  102.1 0.7 odd_mine.3.mine_ref
  102.9 0.8 collective-permute-done.12.received_ref
  103.8 13.4 %all_to_all.32.parts_ref = bf16[16,128,128]{2,1,0:T(8,128)(2,1)S(1)} all-to-all(bf16[16,128,128]{2,1,0:T(8,128)(2,1)S(1)} %pair_core.3), channel_id=1, replica_groups=mesh['row'=8,'x'=4,'y'=4,'core'=2] {'x','y'}, dimensions={0} | all-to-all | bytes 1048576 | tf_op jit(solution)/shard_map/all_to_all | solution.py:344
  117.3 12.7 %all_to_all.33.block_ref = bf16[16,128,128]{2,1,0:T(8,128)(2,1)S(1)} all-to-all(bf16[16,128,128]{2,1,0:T(8,128)(2,1)S(1)} %next_share.3.block_ref), channel_id=1, replica_groups=mesh['row'=8,'x'=4,'y'=4,'core'=2] {'x','y'}, dimensions={0} | all-to-all | bytes 1048576 | tf_op jit(solution)/shard_map/all_to_all | solution.py:344
  130.4 3.3 %collective-permute-start.13 = (f32[40,128]{1,0:T(8,128)S(1)}, f32[40,128]{1,0:T(8,128)S(1)}, u32[]{:S(2)}, u32[]{:S(2)}) collective-permute-start(f32[40,128]{1,0:T(8,128)S(1)} %get-tuple-element.51), channel_id=1, source_target_pairs={{0,1},{1,0},{2,3},{3,2},{4,5},{5,4},{6,7},{7,6},{8,9},{9,8},{10,11... | collective-permute-start | bytes 61448 | tf_op jit(solution)/shard_map/ppermute | solution.py:335
  133.7 0.8 collective-permute-done.13.received_ref
  134.6 13.2 %all_to_all.34.parts_ref = f32[8,40,128]{2,1,0:T(8,128)S(1)} all-to-all(f32[8,40,128]{2,1,0:T(8,128)S(1)} %gram_copies.2), channel_id=1, replica_groups=mesh['row'=8,'x'=4,'y'=4,'core'=2] {'row'}, dimensions={0} | all-to-all | bytes 327680 | tf_op jit(solution)/shard_map/all_to_all | solution.py:344
  147.8 2.2 %collective-permute-start.14 = (f32[40,128]{1,0:T(8,128)S(1)}, f32[40,128]{1,0:T(8,128)S(1)}, u32[]{:S(2)}, u32[]{:S(2)}) collective-permute-start(f32[40,128]{1,0:T(8,128)S(1)} %gram_sum.2.mine_ref), channel_id=1, source_target_pairs={{0,1},{1,0},{2,3},{3,2},{4,5},{5,4},{6,7},{7,6},{8,9},{9,8},{10,11... | collective-permute-start | bytes 61448 | tf_op jit(solution)/shard_map/ppermute | solution.py:335
  149.9 0.8 collective-permute-done.14.other_ref
  150.8 5.3 %second_gram.1 = (f32[40,128]{1,0:T(8,128)S(1)}, f32[40,128]{1,0:T(8,128)S(1)}, f32[128,128]{1,0:T(8,128)S(1)}, f32[128,128]{1,0:T(8,128)S(1)}) custom-call(f32[40,128]{1,0:T(8,128)S(1)} %gram_sum.2.mine_ref, f32[40,128]{1,0:T(8,128)S(1)} %collective-permute-done.14.other_ref, bf16[16,128,128]{2,1,0:T(8,128)(2,1)S(1)} %all_to_all.33.block_ref), custom_call_target="tpu_custom_call" | custom-call | tf_op jit(solution)/shard_map/second_gram/pallas_call | solution.py:30
  156.1 0.4 collective-permute-start.15
  156.5 0.8 collective-permute-done.15.received_ref
  157.4 11.6 %all_to_all.35.parts_ref = f32[8,40,128]{2,1,0:T(8,128)S(1)} all-to-all(f32[8,40,128]{2,1,0:T(8,128)S(1)} %gram_copies.3), channel_id=1, replica_groups=mesh['row'=8,'x'=4,'y'=4,'core'=2] {'row'}, dimensions={0} | all-to-all | bytes 327680 | tf_op jit(solution)/shard_map/all_to_all | solution.py:344
  169.0 1.8 %collective-permute-start.16 = (f32[40,128]{1,0:T(8,128)S(1)}, f32[40,128]{1,0:T(8,128)S(1)}, u32[]{:S(2)}, u32[]{:S(2)}) collective-permute-start(f32[40,128]{1,0:T(8,128)S(1)} %gram_sum.3.mine_ref), channel_id=1, source_target_pairs={{0,1},{1,0},{2,3},{3,2},{4,5},{5,4},{6,7},{7,6},{8,9},{9,8},{10,11... | collective-permute-start | bytes 61448 | tf_op jit(solution)/shard_map/ppermute | solution.py:335
  170.8 0.8 collective-permute-done.16.other_ref
  171.6 4.4 %last.1 = (f32[128,128]{1,0:T(8,128)}, f32[128,128]{1,0:T(8,128)}) custom-call(f32[40,128]{1,0:T(8,128)S(1)} %gram_sum.3.mine_ref, f32[40,128]{1,0:T(8,128)S(1)} %collective-permute-done.16.other_ref, f32[128,128]{1,0:T(8,128)S(1)} %get-tuple-element.54.upper_one_ref, f32[128,128]{1,0:T(8,128)S(1)} %get-tuple-element.55.inverse_one_ref, ...), custom_call_target="tpu_custom_call" | custom-call | tf_op jit(solution)/shard_map/last/pallas_call | solution.py:30
  (18 shorter events, 1.3 us)
Async XLA Ops:
  4.5 5.1 %collective-permute-start = (bf16[4,128,128]{2,1,0:T(8,128)(2,1)S(1)}, bf16[4,128,128]{2,1,0:T(8,128)(2,1)S(1)}, u32[]{:S(2)}, u32[]{:S(2)}) collective-permute-start(bf16[4,128,128]{2,1,0:T(8,128)(2,1)S(1)} %get-tuple-element.34), channel_id=1, source_target_pairs={{0,32},{32,0},{64,96},{96,64},{128,160},{160,128},{192,224},{224,1... | collective-permute-start | bytes 393224 | tf_op jit(solution)/shard_map/ppermute | solution.py:340
  9.7 9.3 %collective-permute-start.1 = (bf16[4,128,128]{2,1,0:T(8,128)(2,1)S(1)}, bf16[4,128,128]{2,1,0:T(8,128)(2,1)S(1)}, u32[]{:S(2)}, u32[]{:S(2)}) collective-permute-start(bf16[4,128,128]{2,1,0:T(8,128)(2,1)S(1)} %get-tuple-element.36), channel_id=1, source_target_pairs={{0,64},{32,96},{64,0},{96,32},{128,192},{160,224},{192,128},{224,1... | collective-permute-start | bytes 393224 | tf_op jit(solution)/shard_map/ppermute | solution.py:340
  13.3 15.9 %collective-permute-start.2 = (bf16[4,128,128]{2,1,0:T(8,128)(2,1)S(1)}, bf16[4,128,128]{2,1,0:T(8,128)(2,1)S(1)}, u32[]{:S(2)}, u32[]{:S(2)}) collective-permute-start(bf16[4,128,128]{2,1,0:T(8,128)(2,1)S(1)} %get-tuple-element.36), channel_id=1, source_target_pairs={{0,160},{32,128},{64,224},{96,192},{128,32},{160,0},{192,96},{224,... | collective-permute-start | bytes 393224 | tf_op jit(solution)/shard_map/ppermute | solution.py:340
  17.6 11.6 %collective-permute-start.3 = (bf16[4,128,128]{2,1,0:T(8,128)(2,1)S(1)}, bf16[4,128,128]{2,1,0:T(8,128)(2,1)S(1)}, u32[]{:S(2)}, u32[]{:S(2)}) collective-permute-start(bf16[4,128,128]{2,1,0:T(8,128)(2,1)S(1)} %get-tuple-element.36), channel_id=1, source_target_pairs={{0,224},{32,192},{64,160},{96,128},{128,96},{160,64},{192,32},{224... | collective-permute-start | bytes 393224 | tf_op jit(solution)/shard_map/ppermute | solution.py:340
  29.3 3.9 %collective-permute-start.4 = (bf16[4,128,128]{2,1,0:T(8,128)(2,1)S(1)}, bf16[4,128,128]{2,1,0:T(8,128)(2,1)S(1)}, u32[]{:S(2)}, u32[]{:S(2)}) collective-permute-start(bf16[4,128,128]{2,1,0:T(8,128)(2,1)S(1)} %get-tuple-element.37.vectors_ref), channel_id=1, source_target_pairs={{0,32},{32,0},{64,96},{96,64},{128,160},{160,128},{192,224},{224,1... | collective-permute-start | bytes 393224 | tf_op jit(solution)/shard_map/ppermute | solution.py:340
  33.9 4.4 %collective-permute-start.5 = (bf16[16,128,128]{2,1,0:T(8,128)(2,1)S(1)}, bf16[16,128,128]{2,1,0:T(8,128)(2,1)S(1)}, u32[]{:S(2)}, u32[]{:S(2)}) collective-permute-start(bf16[16,128,128]{2,1,0:T(8,128)(2,1)S(1)} %odd_other.2), channel_id=1, source_target_pairs={{0,1},{1,0},{2,3},{3,2},{4,5},{5,4},{6,7},{7,6},{8,9},{9,8},{10,11... | collective-permute-start | bytes 1572872 | tf_op jit(solution)/shard_map/ppermute | solution.py:335
  68.1 4.8 %collective-permute-start.6 = (bf16[16,128,128]{2,1,0:T(8,128)(2,1)S(1)}, bf16[16,128,128]{2,1,0:T(8,128)(2,1)S(1)}, u32[]{:S(2)}, u32[]{:S(2)}) collective-permute-start(bf16[16,128,128]{2,1,0:T(8,128)(2,1)S(1)} %all_to_all.31.vectors_ref), channel_id=1, source_target_pairs={{0,1},{1,0},{2,3},{3,2},{4,5},{5,4},{6,7},{7,6},{8,9},{9,8},{10,11... | collective-permute-start | bytes 1572872 | tf_op jit(solution)/shard_map/ppermute | solution.py:335
  73.4 4.8 %collective-permute-start.7 = (bf16[4,128,128]{2,1,0:T(8,128)(2,1)S(1)}, bf16[4,128,128]{2,1,0:T(8,128)(2,1)S(1)}, u32[]{:S(2)}, u32[]{:S(2)}) collective-permute-start(bf16[4,128,128]{2,1,0:T(8,128)(2,1)S(1)} %even_last.3), channel_id=1, source_target_pairs={{0,32},{32,0},{64,96},{96,64},{128,160},{160,128},{192,224},{224,1... | collective-permute-start | bytes 393224 | tf_op jit(solution)/shard_map/ppermute | solution.py:340
  78.3 6.5 %collective-permute-start.10 = (bf16[4,128,128]{2,1,0:T(8,128)(2,1)S(1)}, bf16[4,128,128]{2,1,0:T(8,128)(2,1)S(1)}, u32[]{:S(2)}, u32[]{:S(2)}) collective-permute-start(bf16[4,128,128]{2,1,0:T(8,128)(2,1)S(1)} %get-tuple-element.45), channel_id=1, source_target_pairs={{0,224},{32,192},{64,160},{96,128},{128,96},{160,64},{192,32},{224... | collective-permute-start | bytes 393224 | tf_op jit(solution)/shard_map/ppermute | solution.py:340
  80.7 5.1 %collective-permute-start.8 = (bf16[4,128,128]{2,1,0:T(8,128)(2,1)S(1)}, bf16[4,128,128]{2,1,0:T(8,128)(2,1)S(1)}, u32[]{:S(2)}, u32[]{:S(2)}) collective-permute-start(bf16[4,128,128]{2,1,0:T(8,128)(2,1)S(1)} %get-tuple-element.45), channel_id=1, source_target_pairs={{0,64},{32,96},{64,0},{96,32},{128,192},{160,224},{192,128},{224,1... | collective-permute-start | bytes 393224 | tf_op jit(solution)/shard_map/ppermute | solution.py:340
  82.1 12.0 %collective-permute-start.9 = (bf16[4,128,128]{2,1,0:T(8,128)(2,1)S(1)}, bf16[4,128,128]{2,1,0:T(8,128)(2,1)S(1)}, u32[]{:S(2)}, u32[]{:S(2)}) collective-permute-start(bf16[4,128,128]{2,1,0:T(8,128)(2,1)S(1)} %get-tuple-element.45), channel_id=1, source_target_pairs={{0,160},{32,128},{64,224},{96,192},{128,32},{160,0},{192,96},{224,... | collective-permute-start | bytes 393224 | tf_op jit(solution)/shard_map/ppermute | solution.py:340
  94.2 3.9 %collective-permute-start.11 = (bf16[4,128,128]{2,1,0:T(8,128)(2,1)S(1)}, bf16[4,128,128]{2,1,0:T(8,128)(2,1)S(1)}, u32[]{:S(2)}, u32[]{:S(2)}) collective-permute-start(bf16[4,128,128]{2,1,0:T(8,128)(2,1)S(1)} %four_sum.3.vectors_ref), channel_id=1, source_target_pairs={{0,32},{32,0},{64,96},{96,64},{128,160},{160,128},{192,224},{224,1... | collective-permute-start | bytes 393224 | tf_op jit(solution)/shard_map/ppermute | solution.py:340
  98.8 4.9 %collective-permute-start.12 = (bf16[16,128,128]{2,1,0:T(8,128)(2,1)S(1)}, bf16[16,128,128]{2,1,0:T(8,128)(2,1)S(1)}, u32[]{:S(2)}, u32[]{:S(2)}) collective-permute-start(bf16[16,128,128]{2,1,0:T(8,128)(2,1)S(1)} %odd_other.3), channel_id=1, source_target_pairs={{0,1},{1,0},{2,3},{3,2},{4,5},{5,4},{6,7},{7,6},{8,9},{9,8},{10,11... | collective-permute-start | bytes 1572872 | tf_op jit(solution)/shard_map/ppermute | solution.py:335
  130.4 4.2 %collective-permute-start.13 = (f32[40,128]{1,0:T(8,128)S(1)}, f32[40,128]{1,0:T(8,128)S(1)}, u32[]{:S(2)}, u32[]{:S(2)}) collective-permute-start(f32[40,128]{1,0:T(8,128)S(1)} %get-tuple-element.51), channel_id=1, source_target_pairs={{0,1},{1,0},{2,3},{3,2},{4,5},{5,4},{6,7},{7,6},{8,9},{9,8},{10,11... | collective-permute-start | bytes 61448 | tf_op jit(solution)/shard_map/ppermute | solution.py:335
  147.8 3.0 %collective-permute-start.14 = (f32[40,128]{1,0:T(8,128)S(1)}, f32[40,128]{1,0:T(8,128)S(1)}, u32[]{:S(2)}, u32[]{:S(2)}) collective-permute-start(f32[40,128]{1,0:T(8,128)S(1)} %gram_sum.2.mine_ref), channel_id=1, source_target_pairs={{0,1},{1,0},{2,3},{3,2},{4,5},{5,4},{6,7},{7,6},{8,9},{9,8},{10,11... | collective-permute-start | bytes 61448 | tf_op jit(solution)/shard_map/ppermute | solution.py:335
  156.1 1.3 collective-permute-start.15
  169.0 2.7 %collective-permute-start.16 = (f32[40,128]{1,0:T(8,128)S(1)}, f32[40,128]{1,0:T(8,128)S(1)}, u32[]{:S(2)}, u32[]{:S(2)}) collective-permute-start(f32[40,128]{1,0:T(8,128)S(1)} %gram_sum.3.mine_ref), channel_id=1, source_target_pairs={{0,1},{1,0},{2,3},{3,2},{4,5},{5,4},{6,7},{7,6},{8,9},{9,8},{10,11... | collective-permute-start | bytes 61448 | tf_op jit(solution)/shard_map/ppermute | solution.py:335

commit v10 on v9

--- a/solution.py
+++ b/solution.py
@@ -309,10 +309,11 @@
     out_ref[...] = sum_copies(parts_ref)
 
 
-def second_gram_kernel(
-    mine_ref, other_ref, block_ref, keep_ref, send_ref, upper_ref, inverse_ref
-):
+def factor_kernel(mine_ref, other_ref, upper_ref, inverse_ref):
     factor(unpack(mine_ref, other_ref), upper_ref, inverse_ref)
+
+
+def second_gram_kernel(inverse_ref, block_ref, keep_ref, send_ref):
     block = times_inverse(flat(block_ref[...]), inverse_ref[...])
     pack(gram_of(block), keep_ref, send_ref)
 
@@ -431,9 +432,11 @@
     block = exchange(copies, PLANE)
     packed, square = ((SHARE, K), f32), ((K, K), f32)
     keep, send = local_call(first_gram_kernel, [packed, packed], block, name="first_gram")
-    keep, send, upper, inverse = local_call(
-        second_gram_kernel, [packed, packed, square, square], *sum_gram(keep, send), block,
-        name="second_gram",
+    upper, inverse = local_call(
+        factor_kernel, [square, square], *sum_gram(keep, send), name="factor"
+    )
+    keep, send = local_call(
+        second_gram_kernel, [packed, packed], inverse, block, name="second_gram"
     )
     return local_call(
         last_kernel, [((share, K), f32), square], *sum_gram(keep, send), upper, inverse, copies,

time: 176 us -> 176 us (level)
    pallas_call x26 -> x27, Pallas kernels: 23.8 us -> 23.5 us  [local_call(): pl.pallas_call(kernel, in_specs=[pl.BlockSpec(memory_space=space) for spa...]
where the time goes in v10:
time: 176 us
  blocking collectives  80.4 us (46%)
  waiting for transfers between devices  36.5 us (21%)
  starting transfers between devices  33.8 us (19%)
  Pallas kernels  23.5 us (13%)
    all_to_all x6, blocking collectives, exchange(): return lax.all_to_all(blocks, axes, 0, 0, tiled=True)  80.4 us
    ppermute x10, waiting for transfers between devices, swap_row(): return lax.ppermute(block, 'row', [(i, i ^ mask) for i in range(count)])  30.8 us
    pallas_call x27, Pallas kernels, local_call(): pl.pallas_call(kernel, in_specs=[pl.BlockSpec(memory_space=space) for spa...  23.5 us
    ppermute x7, starting transfers between devices, swap_core(): return lax.ppermute(block, 'core', ((0, 1), (1, 0)))  17.2 us
    ppermute x10, starting transfers between devices, swap_row(): return lax.ppermute(block, 'row', [(i, i ^ mask) for i in range(count)])  16.5 us
    ppermute x7, waiting for transfers between devices, swap_core(): return lax.ppermute(block, 'core', ((0, 1), (1, 0)))  5.7 us
  transfers between devices with their start and end apart: 17, of which 15 were waited for; matrix products, arithmetic and copies ran while one was open for 0% of the time, Pallas kernels for 4%

profile of v10, /device:TPU:1, one launch (start us, length us, event | category | flops | bytes accessed | tf_op | source)
XLA Modules:
  0.0 175.7 jit_solution(8719796008999675205)
XLA Ops:
  1.3 3.2 %start.1 = (bf16[4,128,128]{2,1,0:T(8,128)(2,1)S(1)}, bf16[16,2,128,128]{3,2,1,0:T(8,128)(2,1)S(1)}, f32[128,128]{1,0:T(8,128)S(1)}, bf16[16,2,128,512]{3,2,1,0:T(8,128)(2,1)S(1)}, f32[8,128]{1,0:T(8,128)S(1)}) custom-call(bf16[16,2,128,1024]{3,2,1,0:T(8,128)(2,1)} %bitcast.2, f32[16,2,128,128]{3,2,1,0:T(8,128)} %bitcast.4, f32[1]{0:T(128)S(6)} %copy.5.bound_ref), custom_call_target="tpu_custom_call" | custom-call | tf_op jit(solution)/shard_map/start/pallas_call | solution.py:30
  4.5 2.6 %collective-permute-start = (bf16[4,128,128]{2,1,0:T(8,128)(2,1)S(1)}, bf16[4,128,128]{2,1,0:T(8,128)(2,1)S(1)}, u32[]{:S(2)}, u32[]{:S(2)}) collective-permute-start(bf16[4,128,128]{2,1,0:T(8,128)(2,1)S(1)} %get-tuple-element.34), channel_id=1, source_target_pairs={{0,32},{32,0},{64,96},{96,64},{128,160},{160,128},{192,224},{224,1... | collective-permute-start | bytes 393224 | tf_op jit(solution)/shard_map/ppermute | solution.py:341
  7.1 2.6 %start_own.1 = (f32[4,128,128]{2,1,0:T(8,128)S(1)}, bf16[16,2,128,512]{3,2,1,0:T(8,128)(2,1)S(1)}) custom-call(bf16[16,2,128,1024]{3,2,1,0:T(8,128)(2,1)} %bitcast.3, bf16[16,2,128,128]{3,2,1,0:T(8,128)(2,1)S(1)} %get-tuple-element.31.vectors_ref), custom_call_target="tpu_custom_call" | custom-call | tf_op jit(solution)/shard_map/start_own/pallas_call | solution.py:30
  9.7 3.6 %collective-permute-start.1 = (bf16[4,128,128]{2,1,0:T(8,128)(2,1)S(1)}, bf16[4,128,128]{2,1,0:T(8,128)(2,1)S(1)}, u32[]{:S(2)}, u32[]{:S(2)}) collective-permute-start(bf16[4,128,128]{2,1,0:T(8,128)(2,1)S(1)} %get-tuple-element.36), channel_id=1, source_target_pairs={{0,64},{32,96},{64,0},{96,32},{128,192},{160,224},{192,128},{224,1... | collective-permute-start | bytes 393224 | tf_op jit(solution)/shard_map/ppermute | solution.py:341
  13.3 4.3 %collective-permute-start.2 = (bf16[4,128,128]{2,1,0:T(8,128)(2,1)S(1)}, bf16[4,128,128]{2,1,0:T(8,128)(2,1)S(1)}, u32[]{:S(2)}, u32[]{:S(2)}) collective-permute-start(bf16[4,128,128]{2,1,0:T(8,128)(2,1)S(1)} %get-tuple-element.36), channel_id=1, source_target_pairs={{0,160},{32,128},{64,224},{96,192},{128,32},{160,0},{192,96},{224,... | collective-permute-start | bytes 393224 | tf_op jit(solution)/shard_map/ppermute | solution.py:341
  17.6 1.4 collective-permute-done.1.two_ref
  19.0 10.2 %collective-permute-done.2.five_ref = bf16[4,128,128]{2,1,0:T(8,128)(2,1)S(1)} collective-permute-done((bf16[4,128,128]{2,1,0:T(8,128)(2,1)S(1)}, bf16[4,128,128]{2,1,0:T(8,128)(2,1)S(1)}, u32[]{:S(2)}, u32[]{:S(2)}) %collective-permute-start.2) | collective-permute-done | bytes 131104 | tf_op jit(solution)/shard_map/ppermute | solution.py:341
  29.4 1.2 odd_first.2
  30.6 2.6 %collective-permute-done.4.vectors_ref = bf16[4,128,128]{2,1,0:T(8,128)(2,1)S(1)} collective-permute-done((bf16[4,128,128]{2,1,0:T(8,128)(2,1)S(1)}, bf16[4,128,128]{2,1,0:T(8,128)(2,1)S(1)}, u32[]{:S(2)}, u32[]{:S(2)}) %collective-permute-start.4) | collective-permute-done | bytes 131104 | tf_op jit(solution)/shard_map/ppermute | solution.py:341
  33.2 0.7 odd_other.2
  33.9 2.8 %collective-permute-start.5 = (bf16[16,128,128]{2,1,0:T(8,128)(2,1)S(1)}, bf16[16,128,128]{2,1,0:T(8,128)(2,1)S(1)}, u32[]{:S(2)}, u32[]{:S(2)}) collective-permute-start(bf16[16,128,128]{2,1,0:T(8,128)(2,1)S(1)} %odd_other.2), channel_id=1, source_target_pairs={{0,1},{1,0},{2,3},{3,2},{4,5},{5,4},{6,7},{7,6},{8,9},{9,8},{10,11... | collective-permute-start | bytes 1572872 | tf_op jit(solution)/shard_map/ppermute | solution.py:336
  36.7 0.7 odd_mine.2.mine_ref
  37.4 0.8 collective-permute-done.5.received_ref
  38.3 16.9 %all_to_all.30.parts_ref = bf16[16,128,128]{2,1,0:T(8,128)(2,1)S(1)} all-to-all(bf16[16,128,128]{2,1,0:T(8,128)(2,1)S(1)} %pair_core.2), channel_id=1, replica_groups=mesh['row'=8,'x'=4,'y'=4,'core'=2] {'x','y'}, dimensions={0} | all-to-all | bytes 1048576 | tf_op jit(solution)/shard_map/all_to_all | solution.py:345
  55.4 12.7 %all_to_all.31.vectors_ref = bf16[16,128,128]{2,1,0:T(8,128)(2,1)S(1)} all-to-all(bf16[16,128,128]{2,1,0:T(8,128)(2,1)S(1)} %get-tuple-element.41), channel_id=1, replica_groups=mesh['row'=8,'x'=4,'y'=4,'core'=2] {'x','y'}, dimensions={0} | all-to-all | bytes 1048576 | tf_op jit(solution)/shard_map/all_to_all | solution.py:345
  68.1 3.3 %collective-permute-start.6 = (bf16[16,128,128]{2,1,0:T(8,128)(2,1)S(1)}, bf16[16,128,128]{2,1,0:T(8,128)(2,1)S(1)}, u32[]{:S(2)}, u32[]{:S(2)}) collective-permute-start(bf16[16,128,128]{2,1,0:T(8,128)(2,1)S(1)} %all_to_all.31.vectors_ref), channel_id=1, source_target_pairs={{0,1},{1,0},{2,3},{3,2},{4,5},{5,4},{6,7},{7,6},{8,9},{9,8},{10,11... | collective-permute-start | bytes 1572872 | tf_op jit(solution)/shard_map/ppermute | solution.py:336
  71.3 0.8 even_first.1
  72.2 0.7 collective-permute-done.6.vectors_ref
  72.9 0.6 even_last.3
  73.4 1.1 collective-permute-start.7
  74.5 0.6 even_last.2.mine_ref
  75.1 3.1 %collective-permute-done.7.received_ref = bf16[4,128,128]{2,1,0:T(8,128)(2,1)S(1)} collective-permute-done((bf16[4,128,128]{2,1,0:T(8,128)(2,1)S(1)}, bf16[4,128,128]{2,1,0:T(8,128)(2,1)S(1)}, u32[]{:S(2)}, u32[]{:S(2)}) %collective-permute-start.7) | collective-permute-done | bytes 131104 | tf_op jit(solution)/shard_map/ppermute | solution.py:341
  78.3 2.5 %collective-permute-start.10 = (bf16[4,128,128]{2,1,0:T(8,128)(2,1)S(1)}, bf16[4,128,128]{2,1,0:T(8,128)(2,1)S(1)}, u32[]{:S(2)}, u32[]{:S(2)}) collective-permute-start(bf16[4,128,128]{2,1,0:T(8,128)(2,1)S(1)} %get-tuple-element.45), channel_id=1, source_target_pairs={{0,224},{32,192},{64,160},{96,128},{128,96},{160,64},{192,32},{224... | collective-permute-start | bytes 393224 | tf_op jit(solution)/shard_map/ppermute | solution.py:341
  80.7 1.4 collective-permute-start.8
  82.1 1.0 collective-permute-start.9
  83.1 1.6 collective-permute-done.10.seven_ref
  84.8 1.1 collective-permute-done.8.two_ref
  85.9 8.2 %collective-permute-done.9.five_ref = bf16[4,128,128]{2,1,0:T(8,128)(2,1)S(1)} collective-permute-done((bf16[4,128,128]{2,1,0:T(8,128)(2,1)S(1)}, bf16[4,128,128]{2,1,0:T(8,128)(2,1)S(1)}, u32[]{:S(2)}, u32[]{:S(2)}) %collective-permute-start.9) | collective-permute-done | bytes 131104 | tf_op jit(solution)/shard_map/ppermute | solution.py:341
  94.3 1.2 odd_first.3
  95.5 2.6 %collective-permute-done.11.vectors_ref = bf16[4,128,128]{2,1,0:T(8,128)(2,1)S(1)} collective-permute-done((bf16[4,128,128]{2,1,0:T(8,128)(2,1)S(1)}, bf16[4,128,128]{2,1,0:T(8,128)(2,1)S(1)}, u32[]{:S(2)}, u32[]{:S(2)}) %collective-permute-start.11) | collective-permute-done | bytes 131104 | tf_op jit(solution)/shard_map/ppermute | solution.py:341
  98.1 0.7 odd_other.3
  98.8 3.3 %collective-permute-start.12 = (bf16[16,128,128]{2,1,0:T(8,128)(2,1)S(1)}, bf16[16,128,128]{2,1,0:T(8,128)(2,1)S(1)}, u32[]{:S(2)}, u32[]{:S(2)}) collective-permute-start(bf16[16,128,128]{2,1,0:T(8,128)(2,1)S(1)} %odd_other.3), channel_id=1, source_target_pairs={{0,1},{1,0},{2,3},{3,2},{4,5},{5,4},{6,7},{7,6},{8,9},{9,8},{10,11... | collective-permute-start | bytes 1572872 | tf_op jit(solution)/shard_map/ppermute | solution.py:336
  102.1 0.7 odd_mine.3.mine_ref
  102.9 0.8 collective-permute-done.12.received_ref
  103.8 13.4 %all_to_all.32.parts_ref = bf16[16,128,128]{2,1,0:T(8,128)(2,1)S(1)} all-to-all(bf16[16,128,128]{2,1,0:T(8,128)(2,1)S(1)} %pair_core.3), channel_id=1, replica_groups=mesh['row'=8,'x'=4,'y'=4,'core'=2] {'x','y'}, dimensions={0} | all-to-all | bytes 1048576 | tf_op jit(solution)/shard_map/all_to_all | solution.py:345
  117.2 12.7 %all_to_all.33.block_ref = bf16[16,128,128]{2,1,0:T(8,128)(2,1)S(1)} all-to-all(bf16[16,128,128]{2,1,0:T(8,128)(2,1)S(1)} %next_share.3.block_ref), channel_id=1, replica_groups=mesh['row'=8,'x'=4,'y'=4,'core'=2] {'x','y'}, dimensions={0} | all-to-all | bytes 1048576 | tf_op jit(solution)/shard_map/all_to_all | solution.py:345
  130.4 3.3 %collective-permute-start.13 = (f32[40,128]{1,0:T(8,128)S(1)}, f32[40,128]{1,0:T(8,128)S(1)}, u32[]{:S(2)}, u32[]{:S(2)}) collective-permute-start(f32[40,128]{1,0:T(8,128)S(1)} %get-tuple-element.51), channel_id=1, source_target_pairs={{0,1},{1,0},{2,3},{3,2},{4,5},{5,4},{6,7},{7,6},{8,9},{9,8},{10,11... | collective-permute-start | bytes 61448 | tf_op jit(solution)/shard_map/ppermute | solution.py:336
  133.7 0.8 collective-permute-done.13.received_ref
  134.6 13.2 %all_to_all.34.parts_ref = f32[8,40,128]{2,1,0:T(8,128)S(1)} all-to-all(f32[8,40,128]{2,1,0:T(8,128)S(1)} %gram_copies.2), channel_id=1, replica_groups=mesh['row'=8,'x'=4,'y'=4,'core'=2] {'row'}, dimensions={0} | all-to-all | bytes 327680 | tf_op jit(solution)/shard_map/all_to_all | solution.py:345
  147.8 2.2 %collective-permute-start.14 = (f32[40,128]{1,0:T(8,128)S(1)}, f32[40,128]{1,0:T(8,128)S(1)}, u32[]{:S(2)}, u32[]{:S(2)}) collective-permute-start(f32[40,128]{1,0:T(8,128)S(1)} %gram_sum.2.mine_ref), channel_id=1, source_target_pairs={{0,1},{1,0},{2,3},{3,2},{4,5},{5,4},{6,7},{7,6},{8,9},{9,8},{10,11... | collective-permute-start | bytes 61448 | tf_op jit(solution)/shard_map/ppermute | solution.py:336
  149.9 0.8 collective-permute-done.14.other_ref
  150.8 3.2 %factor.1 = (f32[128,128]{1,0:T(8,128)S(1)}, f32[128,128]{1,0:T(8,128)S(1)}) custom-call(f32[40,128]{1,0:T(8,128)S(1)} %gram_sum.2.mine_ref, f32[40,128]{1,0:T(8,128)S(1)} %collective-permute-done.14.other_ref), custom_call_target="tpu_custom_call" | custom-call | tf_op jit(solution)/shard_map/factor/pallas_call | solution.py:30
  153.9 1.8 %second_gram.1 = (f32[40,128]{1,0:T(8,128)S(1)}, f32[40,128]{1,0:T(8,128)S(1)}) custom-call(f32[128,128]{1,0:T(8,128)S(1)} %get-tuple-element.52.inverse_ref.inverse_one_ref, bf16[16,128,128]{2,1,0:T(8,128)(2,1)S(1)} %all_to_all.33.block_ref), custom_call_target="tpu_custom_call" | custom-call | tf_op jit(solution)/shard_map/second_gram/pallas_call | solution.py:30
  156.2 0.8 collective-permute-done.15.received_ref
  157.0 11.6 %all_to_all.35.parts_ref = f32[8,40,128]{2,1,0:T(8,128)S(1)} all-to-all(f32[8,40,128]{2,1,0:T(8,128)S(1)} %gram_copies.3), channel_id=1, replica_groups=mesh['row'=8,'x'=4,'y'=4,'core'=2] {'row'}, dimensions={0} | all-to-all | bytes 327680 | tf_op jit(solution)/shard_map/all_to_all | solution.py:345
  168.6 1.8 %collective-permute-start.16 = (f32[40,128]{1,0:T(8,128)S(1)}, f32[40,128]{1,0:T(8,128)S(1)}, u32[]{:S(2)}, u32[]{:S(2)}) collective-permute-start(f32[40,128]{1,0:T(8,128)S(1)} %gram_sum.3.mine_ref), channel_id=1, source_target_pairs={{0,1},{1,0},{2,3},{3,2},{4,5},{5,4},{6,7},{7,6},{8,9},{9,8},{10,11... | collective-permute-start | bytes 61448 | tf_op jit(solution)/shard_map/ppermute | solution.py:336
  170.5 0.8 collective-permute-done.16.other_ref
  171.3 4.4 %last.1 = (f32[128,128]{1,0:T(8,128)}, f32[128,128]{1,0:T(8,128)}) custom-call(f32[40,128]{1,0:T(8,128)S(1)} %gram_sum.3.mine_ref, f32[40,128]{1,0:T(8,128)S(1)} %collective-permute-done.16.other_ref, f32[128,128]{1,0:T(8,128)S(1)} %get-tuple-element.55.upper_one_ref, f32[128,128]{1,0:T(8,128)S(1)} %get-tuple-element.52.inverse_ref.inverse_one_ref, ...), custom_call_target="tpu_custom_call" | custom-call | tf_op jit(solution)/shard_map/last/pallas_call | solution.py:30
  (19 shorter events, 1.7 us)
Async XLA Ops:
  4.5 5.1 %collective-permute-start = (bf16[4,128,128]{2,1,0:T(8,128)(2,1)S(1)}, bf16[4,128,128]{2,1,0:T(8,128)(2,1)S(1)}, u32[]{:S(2)}, u32[]{:S(2)}) collective-permute-start(bf16[4,128,128]{2,1,0:T(8,128)(2,1)S(1)} %get-tuple-element.34), channel_id=1, source_target_pairs={{0,32},{32,0},{64,96},{96,64},{128,160},{160,128},{192,224},{224,1... | collective-permute-start | bytes 393224 | tf_op jit(solution)/shard_map/ppermute | solution.py:341
  9.7 9.3 %collective-permute-start.1 = (bf16[4,128,128]{2,1,0:T(8,128)(2,1)S(1)}, bf16[4,128,128]{2,1,0:T(8,128)(2,1)S(1)}, u32[]{:S(2)}, u32[]{:S(2)}) collective-permute-start(bf16[4,128,128]{2,1,0:T(8,128)(2,1)S(1)} %get-tuple-element.36), channel_id=1, source_target_pairs={{0,64},{32,96},{64,0},{96,32},{128,192},{160,224},{192,128},{224,1... | collective-permute-start | bytes 393224 | tf_op jit(solution)/shard_map/ppermute | solution.py:341
  13.3 15.9 %collective-permute-start.2 = (bf16[4,128,128]{2,1,0:T(8,128)(2,1)S(1)}, bf16[4,128,128]{2,1,0:T(8,128)(2,1)S(1)}, u32[]{:S(2)}, u32[]{:S(2)}) collective-permute-start(bf16[4,128,128]{2,1,0:T(8,128)(2,1)S(1)} %get-tuple-element.36), channel_id=1, source_target_pairs={{0,160},{32,128},{64,224},{96,192},{128,32},{160,0},{192,96},{224,... | collective-permute-start | bytes 393224 | tf_op jit(solution)/shard_map/ppermute | solution.py:341
  17.6 11.6 %collective-permute-start.3 = (bf16[4,128,128]{2,1,0:T(8,128)(2,1)S(1)}, bf16[4,128,128]{2,1,0:T(8,128)(2,1)S(1)}, u32[]{:S(2)}, u32[]{:S(2)}) collective-permute-start(bf16[4,128,128]{2,1,0:T(8,128)(2,1)S(1)} %get-tuple-element.36), channel_id=1, source_target_pairs={{0,224},{32,192},{64,160},{96,128},{128,96},{160,64},{192,32},{224... | collective-permute-start | bytes 393224 | tf_op jit(solution)/shard_map/ppermute | solution.py:341
  29.3 3.9 %collective-permute-start.4 = (bf16[4,128,128]{2,1,0:T(8,128)(2,1)S(1)}, bf16[4,128,128]{2,1,0:T(8,128)(2,1)S(1)}, u32[]{:S(2)}, u32[]{:S(2)}) collective-permute-start(bf16[4,128,128]{2,1,0:T(8,128)(2,1)S(1)} %get-tuple-element.37.vectors_ref), channel_id=1, source_target_pairs={{0,32},{32,0},{64,96},{96,64},{128,160},{160,128},{192,224},{224,1... | collective-permute-start | bytes 393224 | tf_op jit(solution)/shard_map/ppermute | solution.py:341
  33.9 4.4 %collective-permute-start.5 = (bf16[16,128,128]{2,1,0:T(8,128)(2,1)S(1)}, bf16[16,128,128]{2,1,0:T(8,128)(2,1)S(1)}, u32[]{:S(2)}, u32[]{:S(2)}) collective-permute-start(bf16[16,128,128]{2,1,0:T(8,128)(2,1)S(1)} %odd_other.2), channel_id=1, source_target_pairs={{0,1},{1,0},{2,3},{3,2},{4,5},{5,4},{6,7},{7,6},{8,9},{9,8},{10,11... | collective-permute-start | bytes 1572872 | tf_op jit(solution)/shard_map/ppermute | solution.py:336
  68.1 4.8 %collective-permute-start.6 = (bf16[16,128,128]{2,1,0:T(8,128)(2,1)S(1)}, bf16[16,128,128]{2,1,0:T(8,128)(2,1)S(1)}, u32[]{:S(2)}, u32[]{:S(2)}) collective-permute-start(bf16[16,128,128]{2,1,0:T(8,128)(2,1)S(1)} %all_to_all.31.vectors_ref), channel_id=1, source_target_pairs={{0,1},{1,0},{2,3},{3,2},{4,5},{5,4},{6,7},{7,6},{8,9},{9,8},{10,11... | collective-permute-start | bytes 1572872 | tf_op jit(solution)/shard_map/ppermute | solution.py:336
  73.4 4.8 %collective-permute-start.7 = (bf16[4,128,128]{2,1,0:T(8,128)(2,1)S(1)}, bf16[4,128,128]{2,1,0:T(8,128)(2,1)S(1)}, u32[]{:S(2)}, u32[]{:S(2)}) collective-permute-start(bf16[4,128,128]{2,1,0:T(8,128)(2,1)S(1)} %even_last.3), channel_id=1, source_target_pairs={{0,32},{32,0},{64,96},{96,64},{128,160},{160,128},{192,224},{224,1... | collective-permute-start | bytes 393224 | tf_op jit(solution)/shard_map/ppermute | solution.py:341
  78.3 6.5 %collective-permute-start.10 = (bf16[4,128,128]{2,1,0:T(8,128)(2,1)S(1)}, bf16[4,128,128]{2,1,0:T(8,128)(2,1)S(1)}, u32[]{:S(2)}, u32[]{:S(2)}) collective-permute-start(bf16[4,128,128]{2,1,0:T(8,128)(2,1)S(1)} %get-tuple-element.45), channel_id=1, source_target_pairs={{0,224},{32,192},{64,160},{96,128},{128,96},{160,64},{192,32},{224... | collective-permute-start | bytes 393224 | tf_op jit(solution)/shard_map/ppermute | solution.py:341
  80.7 5.1 %collective-permute-start.8 = (bf16[4,128,128]{2,1,0:T(8,128)(2,1)S(1)}, bf16[4,128,128]{2,1,0:T(8,128)(2,1)S(1)}, u32[]{:S(2)}, u32[]{:S(2)}) collective-permute-start(bf16[4,128,128]{2,1,0:T(8,128)(2,1)S(1)} %get-tuple-element.45), channel_id=1, source_target_pairs={{0,64},{32,96},{64,0},{96,32},{128,192},{160,224},{192,128},{224,1... | collective-permute-start | bytes 393224 | tf_op jit(solution)/shard_map/ppermute | solution.py:341
  82.1 12.0 %collective-permute-start.9 = (bf16[4,128,128]{2,1,0:T(8,128)(2,1)S(1)}, bf16[4,128,128]{2,1,0:T(8,128)(2,1)S(1)}, u32[]{:S(2)}, u32[]{:S(2)}) collective-permute-start(bf16[4,128,128]{2,1,0:T(8,128)(2,1)S(1)} %get-tuple-element.45), channel_id=1, source_target_pairs={{0,160},{32,128},{64,224},{96,192},{128,32},{160,0},{192,96},{224,... | collective-permute-start | bytes 393224 | tf_op jit(solution)/shard_map/ppermute | solution.py:341
  94.2 3.9 %collective-permute-start.11 = (bf16[4,128,128]{2,1,0:T(8,128)(2,1)S(1)}, bf16[4,128,128]{2,1,0:T(8,128)(2,1)S(1)}, u32[]{:S(2)}, u32[]{:S(2)}) collective-permute-start(bf16[4,128,128]{2,1,0:T(8,128)(2,1)S(1)} %four_sum.3.vectors_ref), channel_id=1, source_target_pairs={{0,32},{32,0},{64,96},{96,64},{128,160},{160,128},{192,224},{224,1... | collective-permute-start | bytes 393224 | tf_op jit(solution)/shard_map/ppermute | solution.py:341
  98.8 4.9 %collective-permute-start.12 = (bf16[16,128,128]{2,1,0:T(8,128)(2,1)S(1)}, bf16[16,128,128]{2,1,0:T(8,128)(2,1)S(1)}, u32[]{:S(2)}, u32[]{:S(2)}) collective-permute-start(bf16[16,128,128]{2,1,0:T(8,128)(2,1)S(1)} %odd_other.3), channel_id=1, source_target_pairs={{0,1},{1,0},{2,3},{3,2},{4,5},{5,4},{6,7},{7,6},{8,9},{9,8},{10,11... | collective-permute-start | bytes 1572872 | tf_op jit(solution)/shard_map/ppermute | solution.py:336
  130.4 4.2 %collective-permute-start.13 = (f32[40,128]{1,0:T(8,128)S(1)}, f32[40,128]{1,0:T(8,128)S(1)}, u32[]{:S(2)}, u32[]{:S(2)}) collective-permute-start(f32[40,128]{1,0:T(8,128)S(1)} %get-tuple-element.51), channel_id=1, source_target_pairs={{0,1},{1,0},{2,3},{3,2},{4,5},{5,4},{6,7},{7,6},{8,9},{9,8},{10,11... | collective-permute-start | bytes 61448 | tf_op jit(solution)/shard_map/ppermute | solution.py:336
  147.8 3.0 %collective-permute-start.14 = (f32[40,128]{1,0:T(8,128)S(1)}, f32[40,128]{1,0:T(8,128)S(1)}, u32[]{:S(2)}, u32[]{:S(2)}) collective-permute-start(f32[40,128]{1,0:T(8,128)S(1)} %gram_sum.2.mine_ref), channel_id=1, source_target_pairs={{0,1},{1,0},{2,3},{3,2},{4,5},{5,4},{6,7},{7,6},{8,9},{9,8},{10,11... | collective-permute-start | bytes 61448 | tf_op jit(solution)/shard_map/ppermute | solution.py:336
  155.7 1.3 collective-permute-start.15
  168.6 2.7 %collective-permute-start.16 = (f32[40,128]{1,0:T(8,128)S(1)}, f32[40,128]{1,0:T(8,128)S(1)}, u32[]{:S(2)}, u32[]{:S(2)}) collective-permute-start(f32[40,128]{1,0:T(8,128)S(1)} %gram_sum.3.mine_ref), channel_id=1, source_target_pairs={{0,1},{1,0},{2,3},{3,2},{4,5},{5,4},{6,7},{7,6},{8,9},{9,8},{10,11... | collective-permute-start | bytes 61448 | tf_op jit(solution)/shard_map/ppermute | solution.py:336

commit v11 on v10

--- a/solution.py
+++ b/solution.py
@@ -19,6 +19,7 @@
 COLUMNS = 256
 CHUNKS = 4
 PLANES = 2
+SPLIT = 2
 PLANE = ("x", "y")
 
 
@@ -234,10 +235,10 @@
     even_product(matrix_ref, 1 - lax.axis_index("core"), flat(vectors_ref[...]), base_ref, out_ref)
 
 
-def odd_product(offset, matrix_ref, vectors_ref, base_ref, out_ref):
+def odd_product(offset, matrix_ref, vectors_refs, base_ref, out_ref):
     core = lax.axis_index("core")
     which = core if offset == 0 else 1 - core
-    vectors = flat(vectors_ref[...])
+    vectors = jnp.concatenate([flat(ref[...]) for ref in vectors_refs], axis=0)
     for i in range(0, out_ref.shape[0], CHUNKS):
         rows = flat(matrix_ref[i : i + CHUNKS, which])
         product = jnp.dot(rows, vectors, preferred_element_type=jnp.float32)
@@ -247,24 +248,34 @@
         out_ref[i : i + CHUNKS] = product.astype(out_ref.dtype)
 
 
-def odd_first_kernel(matrix_ref, vectors_ref, other_ref, mine_ref):
-    odd_product(1, matrix_ref, vectors_ref, None, other_ref)
-    odd_product(0, matrix_ref, vectors_ref, None, mine_ref)
-
-
-def odd_last_kernel(offset, matrix_ref, vectors_ref, base_ref, out_ref):
-    odd_product(offset, matrix_ref, vectors_ref, base_ref, out_ref)
+def odd_first_kernel(matrix_ref, *refs):
+    *vectors_refs, other_ref, mine_ref = refs
+    odd_product(1, matrix_ref, vectors_refs, None, other_ref)
+    odd_product(0, matrix_ref, vectors_refs, None, mine_ref)
+
+
+def odd_last_kernel(offset, matrix_ref, *refs):
+    *vectors_refs, base_ref, out_ref = refs
+    odd_product(offset, matrix_ref, vectors_refs, base_ref, out_ref)
 
 
 def pair_kernel(mine_ref, received_ref, *out_refs):
     total = mine_ref[...] + received_ref[...].astype(jnp.float32)
+    first = 0
     for out_ref in out_refs:
-        out_ref[...] = total.astype(out_ref.dtype)
-
-
-def four_sum_kernel(first, scale_ref, own_ref, two_ref, five_ref, seven_ref, *refs):
+        out_ref[...] = total[first : first + out_ref.shape[0]].astype(out_ref.dtype)
+        first += out_ref.shape[0]
+
+
+def pair_row_kernel(mine_ref, received_ref, own_ref, *out_refs):
+    pair_kernel(mine_ref, received_ref, *out_refs)
+    own_ref[...] = mine_ref[...] + received_ref[...].astype(jnp.float32)
+
+
+def four_sum_kernel(first, chunk, scale_ref, own_ref, two_ref, five_ref, seven_ref, *refs):
     two, five, seven = (ref[...].astype(jnp.float32) for ref in (two_ref, five_ref, seven_ref))
-    total = own_ref[...] + two + (five + seven)
+    blocks = two.shape[0]
+    total = own_ref[chunk * blocks : (chunk + 1) * blocks] + two + (five + seven)
     if first:
         share_ref, rounded_ref = refs
         total = total * scale_ref[:1]
@@ -359,27 +370,33 @@
 
     pieces = plane_count // PLANES
 
+    chunk_shape = (half[0] // SPLIT, *half[1:])
+
     def sum_rows(other, mine_of, previous=None):
         received = swap_row(other, 1)
-        own, rounded = local_call(
-            pair_kernel, [(half, f32), (half, bf16)], mine_of(), received, name="pair_row"
-        )
-        parts = [own, *(swap_row(rounded, mask) for mask in (2, 5, 7))]
+        types = [(half, f32)] + [(chunk_shape, bf16)] * SPLIT
+        own, *rounded = local_call(pair_row_kernel, types, mine_of(), received, name="pair_row")
         first = previous is None
-        types = [(half, f32)] * first + [(half, bf16)]
-        args = parts if first else [*parts, previous]
-        kernel = functools.partial(four_sum_kernel, first)
-        return local_call(kernel, types, scale, *args, name="four_sum")
+        types = [(chunk_shape, f32)] * first + [(chunk_shape, bf16)]
+        moved = [[swap_row(block, mask) for mask in (2, 5, 7)] for block in rounded]
+        results = []
+        for chunk in range(SPLIT):
+            args = [own, *moved[chunk]] + ([] if first else [previous[chunk]])
+            kernel = functools.partial(four_sum_kernel, first, chunk)
+            results.append(local_call(kernel, types, scale, *args, name="four_sum"))
+        return zip(*results)
 
     def odd_parts(own):
-        received = swap_row(own, 1)
+        received = [swap_row(block, 1) for block in own]
         other, mine = local_call(
-            odd_first_kernel, [(rows, f32), (rows, f32)], matrix, own, name="odd_first"
+            odd_first_kernel, [(rows, f32), (rows, f32)], matrix, *own, name="odd_first"
         )
         kernels = [functools.partial(odd_last_kernel, offset) for offset in (0, 1)]
-        (other,) = local_call(kernels[1], [(rows, bf16)], matrix_pair, received, other, name="odd_other")
+        (other,) = local_call(
+            kernels[1], [(rows, bf16)], matrix_pair, *received, other, name="odd_other"
+        )
         swapped = swap_core(other)
-        (mine,) = local_call(kernels[0], [(rows, f32)], matrix_pair, received, mine, name="odd_mine")
+        (mine,) = local_call(kernels[0], [(rows, f32)], matrix_pair, *received, mine, name="odd_mine")
         (pair,) = local_call(pair_kernel, [(rows, bf16)], mine, swapped, name="pair_core")
         return exchange(pair, PLANE)
 

time: 176 us -> 178 us (1.011)
  starting transfers between devices: 33.8 us -> 56.4 us
  waiting for transfers between devices: 36.5 us -> 14.4 us
    ppermute x10 -> x18, waiting for transfers between devices: 30.8 us -> 8.66 us  [swap_row(): return lax.ppermute(block, 'row', [(i, i ^ mask) for i in range(count)])]
    ppermute x10 -> x18, starting transfers between devices: 16.5 us -> 37.7 us  [swap_row(): return lax.ppermute(block, 'row', [(i, i ^ mask) for i in range(count)])]
    pallas_call x27 -> x29, Pallas kernels: 23.5 us -> 23.5 us  [local_call(): pl.pallas_call(kernel, in_specs=[pl.BlockSpec(memory_space=space) for spa...]
  transfers between devices with their start and end apart: 17 -> 25, of which waited for: 15 -> 14; matrix products, arithmetic and copies ran while one was open for 0% -> 0% of each run, Pallas kernels for 4% -> 5%
where the time goes in v11:
time: 178 us; the launch traced here: 177 us
  blocking collectives  81.5 us (46%)
  starting transfers between devices  56.4 us (32%)
  Pallas kernels  23.5 us (13%)
  waiting for transfers between devices  14.4 us (8%)
    all_to_all x6, blocking collectives, exchange(): return lax.all_to_all(blocks, axes, 0, 0, tiled=True)  81.5 us
    ppermute x18, starting transfers between devices, swap_row(): return lax.ppermute(block, 'row', [(i, i ^ mask) for i in range(count)])  37.7 us
    pallas_call x29, Pallas kernels, local_call(): pl.pallas_call(kernel, in_specs=[pl.BlockSpec(memory_space=space) for spa...  23.5 us
    ppermute x7, starting transfers between devices, swap_core(): return lax.ppermute(block, 'core', ((0, 1), (1, 0)))  18.8 us
    ppermute x18, waiting for transfers between devices, swap_row(): return lax.ppermute(block, 'row', [(i, i ^ mask) for i in range(count)])  8.66 us
    ppermute x7, waiting for transfers between devices, swap_core(): return lax.ppermute(block, 'core', ((0, 1), (1, 0)))  5.7 us
  transfers between devices with their start and end apart: 25, of which 14 were waited for; matrix products, arithmetic and copies ran while one was open for 0% of the time, Pallas kernels for 5%

profile of v11, /device:TPU:1, one launch (start us, length us, event | category | flops | bytes accessed | tf_op | source)
XLA Modules:
  0.0 177.2 jit_solution(4891457071875604870)
XLA Ops:
  1.3 3.2 %start.1 = (bf16[4,128,128]{2,1,0:T(8,128)(2,1)S(1)}, bf16[16,2,128,128]{3,2,1,0:T(8,128)(2,1)S(1)}, f32[128,128]{1,0:T(8,128)S(1)}, bf16[16,2,128,512]{3,2,1,0:T(8,128)(2,1)S(1)}, f32[8,128]{1,0:T(8,128)S(1)}) custom-call(bf16[16,2,128,1024]{3,2,1,0:T(8,128)(2,1)} %bitcast.2, f32[16,2,128,128]{3,2,1,0:T(8,128)} %bitcast.4, f32[1]{0:T(128)S(6)} %copy.5.bound_ref), custom_call_target="tpu_custom_call" | custom-call | tf_op jit(solution)/shard_map/start/pallas_call | solution.py:31
  4.5 2.6 %collective-permute-start = (bf16[4,128,128]{2,1,0:T(8,128)(2,1)S(1)}, bf16[4,128,128]{2,1,0:T(8,128)(2,1)S(1)}, u32[]{:S(2)}, u32[]{:S(2)}) collective-permute-start(bf16[4,128,128]{2,1,0:T(8,128)(2,1)S(1)} %get-tuple-element.38), channel_id=1, source_target_pairs={{0,32},{32,0},{64,96},{96,64},{128,160},{160,128},{192,224},{224,1... | collective-permute-start | bytes 393224 | tf_op jit(solution)/shard_map/ppermute | solution.py:352
  7.1 2.6 %start_own.1 = (f32[4,128,128]{2,1,0:T(8,128)S(1)}, bf16[16,2,128,512]{3,2,1,0:T(8,128)(2,1)S(1)}) custom-call(bf16[16,2,128,1024]{3,2,1,0:T(8,128)(2,1)} %bitcast.3, bf16[16,2,128,128]{3,2,1,0:T(8,128)(2,1)S(1)} %get-tuple-element.35.vectors_ref), custom_call_target="tpu_custom_call" | custom-call | tf_op jit(solution)/shard_map/start_own/pallas_call | solution.py:31
  9.7 3.6 %collective-permute-start.5 = (bf16[2,128,128]{2,1,0:T(8,128)(2,1)S(1)}, bf16[2,128,128]{2,1,0:T(8,128)(2,1)S(1)}, u32[]{:S(2)}, u32[]{:S(2)}) collective-permute-start(bf16[2,128,128]{2,1,0:T(8,128)(2,1)S(1)} %get-tuple-element.42), channel_id=1, source_target_pairs={{0,64},{32,96},{64,0},{96,32},{128,192},{160,224},{192,128},{224,1... | collective-permute-start | bytes 196616 | tf_op jit(solution)/shard_map/ppermute | solution.py:352
  13.3 4.3 %collective-permute-start.6 = (bf16[2,128,128]{2,1,0:T(8,128)(2,1)S(1)}, bf16[2,128,128]{2,1,0:T(8,128)(2,1)S(1)}, u32[]{:S(2)}, u32[]{:S(2)}) collective-permute-start(bf16[2,128,128]{2,1,0:T(8,128)(2,1)S(1)} %get-tuple-element.42), channel_id=1, source_target_pairs={{0,160},{32,128},{64,224},{96,192},{128,32},{160,0},{192,96},{224,... | collective-permute-start | bytes 196616 | tf_op jit(solution)/shard_map/ppermute | solution.py:352
  17.6 1.4 collective-permute-start.1
  19.0 3.4 %collective-permute-start.2 = (bf16[2,128,128]{2,1,0:T(8,128)(2,1)S(1)}, bf16[2,128,128]{2,1,0:T(8,128)(2,1)S(1)}, u32[]{:S(2)}, u32[]{:S(2)}) collective-permute-start(bf16[2,128,128]{2,1,0:T(8,128)(2,1)S(1)} %get-tuple-element.40), channel_id=1, source_target_pairs={{0,160},{32,128},{64,224},{96,192},{128,32},{160,0},{192,96},{224,... | collective-permute-start | bytes 196616 | tf_op jit(solution)/shard_map/ppermute | solution.py:352
  22.4 3.2 %collective-permute-start.8 = (bf16[2,128,128]{2,1,0:T(8,128)(2,1)S(1)}, bf16[2,128,128]{2,1,0:T(8,128)(2,1)S(1)}, u32[]{:S(2)}, u32[]{:S(2)}) collective-permute-start(bf16[2,128,128]{2,1,0:T(8,128)(2,1)S(1)} %get-tuple-element.43.refs_1_), channel_id=1, source_target_pairs={{0,32},{32,0},{64,96},{96,64},{128,160},{160,128},{192,224},{224,1... | collective-permute-start | bytes 196616 | tf_op jit(solution)/shard_map/ppermute | solution.py:352
  25.9 1.7 collective-permute-done.3.seven_ref
  27.7 3.4 %collective-permute-start.4 = (bf16[2,128,128]{2,1,0:T(8,128)(2,1)S(1)}, bf16[2,128,128]{2,1,0:T(8,128)(2,1)S(1)}, u32[]{:S(2)}, u32[]{:S(2)}) collective-permute-start(bf16[2,128,128]{2,1,0:T(8,128)(2,1)S(1)} %get-tuple-element.41.refs_0_), channel_id=1, source_target_pairs={{0,32},{32,0},{64,96},{96,64},{128,160},{160,128},{192,224},{224,1... | collective-permute-start | bytes 196616 | tf_op jit(solution)/shard_map/ppermute | solution.py:352
  31.0 1.2 odd_first.2
  32.7 0.7 odd_other.2
  33.4 4.2 %collective-permute-start.9 = (bf16[16,128,128]{2,1,0:T(8,128)(2,1)S(1)}, bf16[16,128,128]{2,1,0:T(8,128)(2,1)S(1)}, u32[]{:S(2)}, u32[]{:S(2)}) collective-permute-start(bf16[16,128,128]{2,1,0:T(8,128)(2,1)S(1)} %odd_other.2), channel_id=1, source_target_pairs={{0,1},{1,0},{2,3},{3,2},{4,5},{5,4},{6,7},{7,6},{8,9},{9,8},{10,11... | collective-permute-start | bytes 1572872 | tf_op jit(solution)/shard_map/ppermute | solution.py:347
  37.7 0.7 odd_mine.2.mine_ref
  38.4 0.8 collective-permute-done.9.received_ref
  39.3 16.9 %all_to_all.30.parts_ref = bf16[16,128,128]{2,1,0:T(8,128)(2,1)S(1)} all-to-all(bf16[16,128,128]{2,1,0:T(8,128)(2,1)S(1)} %pair_core.2), channel_id=1, replica_groups=mesh['row'=8,'x'=4,'y'=4,'core'=2] {'x','y'}, dimensions={0} | all-to-all | bytes 1048576 | tf_op jit(solution)/shard_map/all_to_all | solution.py:356
  56.3 12.7 %all_to_all.31.vectors_ref = bf16[16,128,128]{2,1,0:T(8,128)(2,1)S(1)} all-to-all(bf16[16,128,128]{2,1,0:T(8,128)(2,1)S(1)} %get-tuple-element.47), channel_id=1, replica_groups=mesh['row'=8,'x'=4,'y'=4,'core'=2] {'x','y'}, dimensions={0} | all-to-all | bytes 1048576 | tf_op jit(solution)/shard_map/all_to_all | solution.py:356
  69.0 3.3 %collective-permute-start.10 = (bf16[16,128,128]{2,1,0:T(8,128)(2,1)S(1)}, bf16[16,128,128]{2,1,0:T(8,128)(2,1)S(1)}, u32[]{:S(2)}, u32[]{:S(2)}) collective-permute-start(bf16[16,128,128]{2,1,0:T(8,128)(2,1)S(1)} %all_to_all.31.vectors_ref), channel_id=1, source_target_pairs={{0,1},{1,0},{2,3},{3,2},{4,5},{5,4},{6,7},{7,6},{8,9},{9,8},{10,11... | collective-permute-start | bytes 1572872 | tf_op jit(solution)/shard_map/ppermute | solution.py:347
  72.3 0.8 even_first.1
  74.4 2.0 %collective-permute-start.11 = (bf16[4,128,128]{2,1,0:T(8,128)(2,1)S(1)}, bf16[4,128,128]{2,1,0:T(8,128)(2,1)S(1)}, u32[]{:S(2)}, u32[]{:S(2)}) collective-permute-start(bf16[4,128,128]{2,1,0:T(8,128)(2,1)S(1)} %even_last.3), channel_id=1, source_target_pairs={{0,32},{32,0},{64,96},{96,64},{128,160},{160,128},{192,224},{224,1... | collective-permute-start | bytes 393224 | tf_op jit(solution)/shard_map/ppermute | solution.py:352
  77.0 3.0 %collective-permute-done.11.received_ref = bf16[4,128,128]{2,1,0:T(8,128)(2,1)S(1)} collective-permute-done((bf16[4,128,128]{2,1,0:T(8,128)(2,1)S(1)}, bf16[4,128,128]{2,1,0:T(8,128)(2,1)S(1)}, u32[]{:S(2)}, u32[]{:S(2)}) %collective-permute-start.11) | collective-permute-done | bytes 131104 | tf_op jit(solution)/shard_map/ppermute | solution.py:352
  80.0 1.7 collective-permute-start.16
  82.2 2.6 %collective-permute-start.18 = (bf16[2,128,128]{2,1,0:T(8,128)(2,1)S(1)}, bf16[2,128,128]{2,1,0:T(8,128)(2,1)S(1)}, u32[]{:S(2)}, u32[]{:S(2)}) collective-permute-start(bf16[2,128,128]{2,1,0:T(8,128)(2,1)S(1)} %get-tuple-element.53), channel_id=1, source_target_pairs={{0,224},{32,192},{64,160},{96,128},{128,96},{160,64},{192,32},{224... | collective-permute-start | bytes 196616 | tf_op jit(solution)/shard_map/ppermute | solution.py:352
  84.8 2.5 %collective-permute-start.12 = (bf16[2,128,128]{2,1,0:T(8,128)(2,1)S(1)}, bf16[2,128,128]{2,1,0:T(8,128)(2,1)S(1)}, u32[]{:S(2)}, u32[]{:S(2)}) collective-permute-start(bf16[2,128,128]{2,1,0:T(8,128)(2,1)S(1)} %get-tuple-element.51), channel_id=1, source_target_pairs={{0,64},{32,96},{64,0},{96,32},{128,192},{160,224},{192,128},{224,1... | collective-permute-start | bytes 196616 | tf_op jit(solution)/shard_map/ppermute | solution.py:352
  87.4 2.4 %collective-permute-start.14 = (bf16[2,128,128]{2,1,0:T(8,128)(2,1)S(1)}, bf16[2,128,128]{2,1,0:T(8,128)(2,1)S(1)}, u32[]{:S(2)}, u32[]{:S(2)}) collective-permute-start(bf16[2,128,128]{2,1,0:T(8,128)(2,1)S(1)} %get-tuple-element.51), channel_id=1, source_target_pairs={{0,224},{32,192},{64,160},{96,128},{128,96},{160,64},{192,32},{224... | collective-permute-start | bytes 196616 | tf_op jit(solution)/shard_map/ppermute | solution.py:352
  89.8 2.9 %collective-permute-start.19 = (bf16[2,128,128]{2,1,0:T(8,128)(2,1)S(1)}, bf16[2,128,128]{2,1,0:T(8,128)(2,1)S(1)}, u32[]{:S(2)}, u32[]{:S(2)}) collective-permute-start(bf16[2,128,128]{2,1,0:T(8,128)(2,1)S(1)} %four_sum.7.refs_1_), channel_id=1, source_target_pairs={{0,32},{32,0},{64,96},{96,64},{128,160},{160,128},{192,224},{224,1... | collective-permute-start | bytes 196616 | tf_op jit(solution)/shard_map/ppermute | solution.py:352
  92.7 0.9 collective-permute-done.13.five_ref
  94.3 1.2 collective-permute-start.15
  95.5 1.2 odd_first.3
  96.8 1.7 collective-permute-done.15.refs_0_
  98.5 0.7 odd_other.3
  99.2 3.5 %collective-permute-start.20 = (bf16[16,128,128]{2,1,0:T(8,128)(2,1)S(1)}, bf16[16,128,128]{2,1,0:T(8,128)(2,1)S(1)}, u32[]{:S(2)}, u32[]{:S(2)}) collective-permute-start(bf16[16,128,128]{2,1,0:T(8,128)(2,1)S(1)} %odd_other.3), channel_id=1, source_target_pairs={{0,1},{1,0},{2,3},{3,2},{4,5},{5,4},{6,7},{7,6},{8,9},{9,8},{10,11... | collective-permute-start | bytes 1572872 | tf_op jit(solution)/shard_map/ppermute | solution.py:347
  102.7 0.7 odd_mine.3.mine_ref
  103.4 0.8 collective-permute-done.20.received_ref
  104.3 13.3 %all_to_all.32.parts_ref = bf16[16,128,128]{2,1,0:T(8,128)(2,1)S(1)} all-to-all(bf16[16,128,128]{2,1,0:T(8,128)(2,1)S(1)} %pair_core.3), channel_id=1, replica_groups=mesh['row'=8,'x'=4,'y'=4,'core'=2] {'x','y'}, dimensions={0} | all-to-all | bytes 1048576 | tf_op jit(solution)/shard_map/all_to_all | solution.py:356
  117.8 12.7 %all_to_all.33.block_ref = bf16[16,128,128]{2,1,0:T(8,128)(2,1)S(1)} all-to-all(bf16[16,128,128]{2,1,0:T(8,128)(2,1)S(1)} %next_share.3.block_ref), channel_id=1, replica_groups=mesh['row'=8,'x'=4,'y'=4,'core'=2] {'x','y'}, dimensions={0} | all-to-all | bytes 1048576 | tf_op jit(solution)/shard_map/all_to_all | solution.py:356
  130.9 3.3 %collective-permute-start.21 = (f32[40,128]{1,0:T(8,128)S(1)}, f32[40,128]{1,0:T(8,128)S(1)}, u32[]{:S(2)}, u32[]{:S(2)}) collective-permute-start(f32[40,128]{1,0:T(8,128)S(1)} %get-tuple-element.59), channel_id=1, source_target_pairs={{0,1},{1,0},{2,3},{3,2},{4,5},{5,4},{6,7},{7,6},{8,9},{9,8},{10,11... | collective-permute-start | bytes 61448 | tf_op jit(solution)/shard_map/ppermute | solution.py:347
  134.2 0.8 collective-permute-done.21.received_ref
  135.1 14.2 %all_to_all.34.parts_ref = f32[8,40,128]{2,1,0:T(8,128)S(1)} all-to-all(f32[8,40,128]{2,1,0:T(8,128)S(1)} %gram_copies.2), channel_id=1, replica_groups=mesh['row'=8,'x'=4,'y'=4,'core'=2] {'row'}, dimensions={0} | all-to-all | bytes 327680 | tf_op jit(solution)/shard_map/all_to_all | solution.py:356
  149.3 2.4 %collective-permute-start.22 = (f32[40,128]{1,0:T(8,128)S(1)}, f32[40,128]{1,0:T(8,128)S(1)}, u32[]{:S(2)}, u32[]{:S(2)}) collective-permute-start(f32[40,128]{1,0:T(8,128)S(1)} %gram_sum.2.mine_ref), channel_id=1, source_target_pairs={{0,1},{1,0},{2,3},{3,2},{4,5},{5,4},{6,7},{7,6},{8,9},{9,8},{10,11... | collective-permute-start | bytes 61448 | tf_op jit(solution)/shard_map/ppermute | solution.py:347
  151.7 0.8 collective-permute-done.22.other_ref
  152.6 3.2 %factor.1 = (f32[128,128]{1,0:T(8,128)S(1)}, f32[128,128]{1,0:T(8,128)S(1)}) custom-call(f32[40,128]{1,0:T(8,128)S(1)} %gram_sum.2.mine_ref, f32[40,128]{1,0:T(8,128)S(1)} %collective-permute-done.22.other_ref), custom_call_target="tpu_custom_call" | custom-call | tf_op jit(solution)/shard_map/factor/pallas_call | solution.py:31
  155.7 1.8 %second_gram.1 = (f32[40,128]{1,0:T(8,128)S(1)}, f32[40,128]{1,0:T(8,128)S(1)}) custom-call(f32[128,128]{1,0:T(8,128)S(1)} %get-tuple-element.60.inverse_ref.inverse_one_ref, bf16[16,128,128]{2,1,0:T(8,128)(2,1)S(1)} %all_to_all.33.block_ref), custom_call_target="tpu_custom_call" | custom-call | tf_op jit(solution)/shard_map/second_gram/pallas_call | solution.py:31
  157.9 0.8 collective-permute-done.23.received_ref
  158.8 11.6 %all_to_all.35.parts_ref = f32[8,40,128]{2,1,0:T(8,128)S(1)} all-to-all(f32[8,40,128]{2,1,0:T(8,128)S(1)} %gram_copies.3), channel_id=1, replica_groups=mesh['row'=8,'x'=4,'y'=4,'core'=2] {'row'}, dimensions={0} | all-to-all | bytes 327680 | tf_op jit(solution)/shard_map/all_to_all | solution.py:356
  170.4 1.6 collective-permute-start.24
  172.0 0.8 collective-permute-done.24.other_ref
  172.9 4.4 %last.1 = (f32[128,128]{1,0:T(8,128)}, f32[128,128]{1,0:T(8,128)}) custom-call(f32[40,128]{1,0:T(8,128)S(1)} %gram_sum.3.mine_ref, f32[40,128]{1,0:T(8,128)S(1)} %collective-permute-done.24.other_ref, f32[128,128]{1,0:T(8,128)S(1)} %get-tuple-element.63.upper_one_ref, f32[128,128]{1,0:T(8,128)S(1)} %get-tuple-element.60.inverse_ref.inverse_one_ref, ...), custom_call_target="tpu_custom_call" | custom-call | tf_op jit(solution)/shard_map/last/pallas_call | solution.py:31
  (37 shorter events, 5.2 us)
Async XLA Ops:
  4.5 5.1 %collective-permute-start = (bf16[4,128,128]{2,1,0:T(8,128)(2,1)S(1)}, bf16[4,128,128]{2,1,0:T(8,128)(2,1)S(1)}, u32[]{:S(2)}, u32[]{:S(2)}) collective-permute-start(bf16[4,128,128]{2,1,0:T(8,128)(2,1)S(1)} %get-tuple-element.38), channel_id=1, source_target_pairs={{0,32},{32,0},{64,96},{96,64},{128,160},{160,128},{192,224},{224,1... | collective-permute-start | bytes 393224 | tf_op jit(solution)/shard_map/ppermute | solution.py:352
  9.7 12.6 %collective-permute-start.5 = (bf16[2,128,128]{2,1,0:T(8,128)(2,1)S(1)}, bf16[2,128,128]{2,1,0:T(8,128)(2,1)S(1)}, u32[]{:S(2)}, u32[]{:S(2)}) collective-permute-start(bf16[2,128,128]{2,1,0:T(8,128)(2,1)S(1)} %get-tuple-element.42), channel_id=1, source_target_pairs={{0,64},{32,96},{64,0},{96,32},{128,192},{160,224},{192,128},{224,1... | collective-permute-start | bytes 196616 | tf_op jit(solution)/shard_map/ppermute | solution.py:352
  13.3 9.1 %collective-permute-start.6 = (bf16[2,128,128]{2,1,0:T(8,128)(2,1)S(1)}, bf16[2,128,128]{2,1,0:T(8,128)(2,1)S(1)}, u32[]{:S(2)}, u32[]{:S(2)}) collective-permute-start(bf16[2,128,128]{2,1,0:T(8,128)(2,1)S(1)} %get-tuple-element.42), channel_id=1, source_target_pairs={{0,160},{32,128},{64,224},{96,192},{128,32},{160,0},{192,96},{224,... | collective-permute-start | bytes 196616 | tf_op jit(solution)/shard_map/ppermute | solution.py:352
  17.6 4.8 %collective-permute-start.7 = (bf16[2,128,128]{2,1,0:T(8,128)(2,1)S(1)}, bf16[2,128,128]{2,1,0:T(8,128)(2,1)S(1)}, u32[]{:S(2)}, u32[]{:S(2)}) collective-permute-start(bf16[2,128,128]{2,1,0:T(8,128)(2,1)S(1)} %get-tuple-element.42), channel_id=1, source_target_pairs={{0,224},{32,192},{64,160},{96,128},{128,96},{160,64},{192,32},{224... | collective-permute-start | bytes 196616 | tf_op jit(solution)/shard_map/ppermute | solution.py:352
  17.6 8.1 %collective-permute-start.1 = (bf16[2,128,128]{2,1,0:T(8,128)(2,1)S(1)}, bf16[2,128,128]{2,1,0:T(8,128)(2,1)S(1)}, u32[]{:S(2)}, u32[]{:S(2)}) collective-permute-start(bf16[2,128,128]{2,1,0:T(8,128)(2,1)S(1)} %get-tuple-element.40), channel_id=1, source_target_pairs={{0,64},{32,96},{64,0},{96,32},{128,192},{160,224},{192,128},{224,1... | collective-permute-start | bytes 196616 | tf_op jit(solution)/shard_map/ppermute | solution.py:352
  19.0 7.0 %collective-permute-start.2 = (bf16[2,128,128]{2,1,0:T(8,128)(2,1)S(1)}, bf16[2,128,128]{2,1,0:T(8,128)(2,1)S(1)}, u32[]{:S(2)}, u32[]{:S(2)}) collective-permute-start(bf16[2,128,128]{2,1,0:T(8,128)(2,1)S(1)} %get-tuple-element.40), channel_id=1, source_target_pairs={{0,160},{32,128},{64,224},{96,192},{128,32},{160,0},{192,96},{224,... | collective-permute-start | bytes 196616 | tf_op jit(solution)/shard_map/ppermute | solution.py:352
  22.3 5.3 %collective-permute-start.3 = (bf16[2,128,128]{2,1,0:T(8,128)(2,1)S(1)}, bf16[2,128,128]{2,1,0:T(8,128)(2,1)S(1)}, u32[]{:S(2)}, u32[]{:S(2)}) collective-permute-start(bf16[2,128,128]{2,1,0:T(8,128)(2,1)S(1)} %get-tuple-element.40), channel_id=1, source_target_pairs={{0,224},{32,192},{64,160},{96,128},{128,96},{160,64},{192,32},{224... | collective-permute-start | bytes 196616 | tf_op jit(solution)/shard_map/ppermute | solution.py:352
  22.4 9.9 %collective-permute-start.8 = (bf16[2,128,128]{2,1,0:T(8,128)(2,1)S(1)}, bf16[2,128,128]{2,1,0:T(8,128)(2,1)S(1)}, u32[]{:S(2)}, u32[]{:S(2)}) collective-permute-start(bf16[2,128,128]{2,1,0:T(8,128)(2,1)S(1)} %get-tuple-element.43.refs_1_), channel_id=1, source_target_pairs={{0,32},{32,0},{64,96},{96,64},{128,160},{160,128},{192,224},{224,1... | collective-permute-start | bytes 196616 | tf_op jit(solution)/shard_map/ppermute | solution.py:352
  27.7 5.0 %collective-permute-start.4 = (bf16[2,128,128]{2,1,0:T(8,128)(2,1)S(1)}, bf16[2,128,128]{2,1,0:T(8,128)(2,1)S(1)}, u32[]{:S(2)}, u32[]{:S(2)}) collective-permute-start(bf16[2,128,128]{2,1,0:T(8,128)(2,1)S(1)} %get-tuple-element.41.refs_0_), channel_id=1, source_target_pairs={{0,32},{32,0},{64,96},{96,64},{128,160},{160,128},{192,224},{224,1... | collective-permute-start | bytes 196616 | tf_op jit(solution)/shard_map/ppermute | solution.py:352
  33.4 5.8 %collective-permute-start.9 = (bf16[16,128,128]{2,1,0:T(8,128)(2,1)S(1)}, bf16[16,128,128]{2,1,0:T(8,128)(2,1)S(1)}, u32[]{:S(2)}, u32[]{:S(2)}) collective-permute-start(bf16[16,128,128]{2,1,0:T(8,128)(2,1)S(1)} %odd_other.2), channel_id=1, source_target_pairs={{0,1},{1,0},{2,3},{3,2},{4,5},{5,4},{6,7},{7,6},{8,9},{9,8},{10,11... | collective-permute-start | bytes 1572872 | tf_op jit(solution)/shard_map/ppermute | solution.py:347
  69.0 4.8 %collective-permute-start.10 = (bf16[16,128,128]{2,1,0:T(8,128)(2,1)S(1)}, bf16[16,128,128]{2,1,0:T(8,128)(2,1)S(1)}, u32[]{:S(2)}, u32[]{:S(2)}) collective-permute-start(bf16[16,128,128]{2,1,0:T(8,128)(2,1)S(1)} %all_to_all.31.vectors_ref), channel_id=1, source_target_pairs={{0,1},{1,0},{2,3},{3,2},{4,5},{5,4},{6,7},{7,6},{8,9},{9,8},{10,11... | collective-permute-start | bytes 1572872 | tf_op jit(solution)/shard_map/ppermute | solution.py:347
  74.4 5.6 %collective-permute-start.11 = (bf16[4,128,128]{2,1,0:T(8,128)(2,1)S(1)}, bf16[4,128,128]{2,1,0:T(8,128)(2,1)S(1)}, u32[]{:S(2)}, u32[]{:S(2)}) collective-permute-start(bf16[4,128,128]{2,1,0:T(8,128)(2,1)S(1)} %even_last.3), channel_id=1, source_target_pairs={{0,32},{32,0},{64,96},{96,64},{128,160},{160,128},{192,224},{224,1... | collective-permute-start | bytes 393224 | tf_op jit(solution)/shard_map/ppermute | solution.py:352
  80.0 7.4 %collective-permute-start.16 = (bf16[2,128,128]{2,1,0:T(8,128)(2,1)S(1)}, bf16[2,128,128]{2,1,0:T(8,128)(2,1)S(1)}, u32[]{:S(2)}, u32[]{:S(2)}) collective-permute-start(bf16[2,128,128]{2,1,0:T(8,128)(2,1)S(1)} %get-tuple-element.53), channel_id=1, source_target_pairs={{0,64},{32,96},{64,0},{96,32},{128,192},{160,224},{192,128},{224,1... | collective-permute-start | bytes 196616 | tf_op jit(solution)/shard_map/ppermute | solution.py:352
  81.7 8.1 %collective-permute-start.17 = (bf16[2,128,128]{2,1,0:T(8,128)(2,1)S(1)}, bf16[2,128,128]{2,1,0:T(8,128)(2,1)S(1)}, u32[]{:S(2)}, u32[]{:S(2)}) collective-permute-start(bf16[2,128,128]{2,1,0:T(8,128)(2,1)S(1)} %get-tuple-element.53), channel_id=1, source_target_pairs={{0,160},{32,128},{64,224},{96,192},{128,32},{160,0},{192,96},{224,... | collective-permute-start | bytes 196616 | tf_op jit(solution)/shard_map/ppermute | solution.py:352
  82.2 7.5 %collective-permute-start.18 = (bf16[2,128,128]{2,1,0:T(8,128)(2,1)S(1)}, bf16[2,128,128]{2,1,0:T(8,128)(2,1)S(1)}, u32[]{:S(2)}, u32[]{:S(2)}) collective-permute-start(bf16[2,128,128]{2,1,0:T(8,128)(2,1)S(1)} %get-tuple-element.53), channel_id=1, source_target_pairs={{0,224},{32,192},{64,160},{96,128},{128,96},{160,64},{192,32},{224... | collective-permute-start | bytes 196616 | tf_op jit(solution)/shard_map/ppermute | solution.py:352
  84.8 7.8 %collective-permute-start.12 = (bf16[2,128,128]{2,1,0:T(8,128)(2,1)S(1)}, bf16[2,128,128]{2,1,0:T(8,128)(2,1)S(1)}, u32[]{:S(2)}, u32[]{:S(2)}) collective-permute-start(bf16[2,128,128]{2,1,0:T(8,128)(2,1)S(1)} %get-tuple-element.51), channel_id=1, source_target_pairs={{0,64},{32,96},{64,0},{96,32},{128,192},{160,224},{192,128},{224,1... | collective-permute-start | bytes 196616 | tf_op jit(solution)/shard_map/ppermute | solution.py:352
  87.4 6.3 %collective-permute-start.13 = (bf16[2,128,128]{2,1,0:T(8,128)(2,1)S(1)}, bf16[2,128,128]{2,1,0:T(8,128)(2,1)S(1)}, u32[]{:S(2)}, u32[]{:S(2)}) collective-permute-start(bf16[2,128,128]{2,1,0:T(8,128)(2,1)S(1)} %get-tuple-element.51), channel_id=1, source_target_pairs={{0,160},{32,128},{64,224},{96,192},{128,32},{160,0},{192,96},{224,... | collective-permute-start | bytes 196616 | tf_op jit(solution)/shard_map/ppermute | solution.py:352
  87.4 6.9 %collective-permute-start.14 = (bf16[2,128,128]{2,1,0:T(8,128)(2,1)S(1)}, bf16[2,128,128]{2,1,0:T(8,128)(2,1)S(1)}, u32[]{:S(2)}, u32[]{:S(2)}) collective-permute-start(bf16[2,128,128]{2,1,0:T(8,128)(2,1)S(1)} %get-tuple-element.51), channel_id=1, source_target_pairs={{0,224},{32,192},{64,160},{96,128},{128,96},{160,64},{192,32},{224... | collective-permute-start | bytes 196616 | tf_op jit(solution)/shard_map/ppermute | solution.py:352
  89.8 7.0 %collective-permute-start.19 = (bf16[2,128,128]{2,1,0:T(8,128)(2,1)S(1)}, bf16[2,128,128]{2,1,0:T(8,128)(2,1)S(1)}, u32[]{:S(2)}, u32[]{:S(2)}) collective-permute-start(bf16[2,128,128]{2,1,0:T(8,128)(2,1)S(1)} %four_sum.7.refs_1_), channel_id=1, source_target_pairs={{0,32},{32,0},{64,96},{96,64},{128,160},{160,128},{192,224},{224,1... | collective-permute-start | bytes 196616 | tf_op jit(solution)/shard_map/ppermute | solution.py:352
  94.3 4.2 %collective-permute-start.15 = (bf16[2,128,128]{2,1,0:T(8,128)(2,1)S(1)}, bf16[2,128,128]{2,1,0:T(8,128)(2,1)S(1)}, u32[]{:S(2)}, u32[]{:S(2)}) collective-permute-start(bf16[2,128,128]{2,1,0:T(8,128)(2,1)S(1)} %four_sum.6.refs_0_), channel_id=1, source_target_pairs={{0,32},{32,0},{64,96},{96,64},{128,160},{160,128},{192,224},{224,1... | collective-permute-start | bytes 196616 | tf_op jit(solution)/shard_map/ppermute | solution.py:352
  99.2 5.0 %collective-permute-start.20 = (bf16[16,128,128]{2,1,0:T(8,128)(2,1)S(1)}, bf16[16,128,128]{2,1,0:T(8,128)(2,1)S(1)}, u32[]{:S(2)}, u32[]{:S(2)}) collective-permute-start(bf16[16,128,128]{2,1,0:T(8,128)(2,1)S(1)} %odd_other.3), channel_id=1, source_target_pairs={{0,1},{1,0},{2,3},{3,2},{4,5},{5,4},{6,7},{7,6},{8,9},{9,8},{10,11... | collective-permute-start | bytes 1572872 | tf_op jit(solution)/shard_map/ppermute | solution.py:347
  130.9 4.2 %collective-permute-start.21 = (f32[40,128]{1,0:T(8,128)S(1)}, f32[40,128]{1,0:T(8,128)S(1)}, u32[]{:S(2)}, u32[]{:S(2)}) collective-permute-start(f32[40,128]{1,0:T(8,128)S(1)} %get-tuple-element.59), channel_id=1, source_target_pairs={{0,1},{1,0},{2,3},{3,2},{4,5},{5,4},{6,7},{7,6},{8,9},{9,8},{10,11... | collective-permute-start | bytes 61448 | tf_op jit(solution)/shard_map/ppermute | solution.py:347
  149.3 3.2 %collective-permute-start.22 = (f32[40,128]{1,0:T(8,128)S(1)}, f32[40,128]{1,0:T(8,128)S(1)}, u32[]{:S(2)}, u32[]{:S(2)}) collective-permute-start(f32[40,128]{1,0:T(8,128)S(1)} %gram_sum.2.mine_ref), channel_id=1, source_target_pairs={{0,1},{1,0},{2,3},{3,2},{4,5},{5,4},{6,7},{7,6},{8,9},{9,8},{10,11... | collective-permute-start | bytes 61448 | tf_op jit(solution)/shard_map/ppermute | solution.py:347
  157.5 1.3 collective-permute-start.23
  170.4 2.5 %collective-permute-start.24 = (f32[40,128]{1,0:T(8,128)S(1)}, f32[40,128]{1,0:T(8,128)S(1)}, u32[]{:S(2)}, u32[]{:S(2)}) collective-permute-start(f32[40,128]{1,0:T(8,128)S(1)} %gram_sum.3.mine_ref), channel_id=1, source_target_pairs={{0,1},{1,0},{2,3},{3,2},{4,5},{5,4},{6,7},{7,6},{8,9},{9,8},{10,11... | collective-permute-start | bytes 61448 | tf_op jit(solution)/shard_map/ppermute | solution.py:347
